TPU v7x, 128 devices: a whole 4x4x4 slice. The times are simulated.
128 devices in a mesh: img: 2 (over y_hi), row: 16 (over x, z), col: 4 (over y_lo, core).
Axes of the slice: x: 4, y: 4 (y_hi: 2, y_lo: 2; y = y_hi * 2 + y_lo), z: 4, core: 2. Of those that a mesh axis runs over, the one named last changes fastest.
Arguments:
- image: bfloat16 [512, 256, 1024], P('img', 'row', 'col'), parts along dimension 0, may hold values from -6 to 6
- from_local: bfloat16 [9, 256, 64], replicated, may hold values from -0.25 to 0.25
- from_global: bfloat16 [9, 64, 192], replicated, may hold values from -0.15625 to 0.15625
- section_weight: bfloat16 [96, 192], replicated, may hold values from -0.4375 to 0.4375
- section_scale: float32 [96], replicated, may hold values from 0.5 to 2
- section_shift: float32 [96], replicated, may hold values from -2 to 2
- fourier_weight: bfloat16 [192, 192], replicated, may hold values from -0.4375 to 0.4375
- fourier_scale: float32 [192], replicated, may hold values from 0.5 to 2
- fourier_shift: float32 [192], replicated, may hold values from -2 to 2
- mix_weight: bfloat16 [192, 96], replicated, may hold values from -0.625 to 0.625
- out_scale: float32 [256], replicated, may hold values from 0.5 to 2
- out_shift: float32 [256], replicated, may hold values from -2 to 2
Outputs:
- result: bfloat16 [512, 256, 1024], P('img', 'row', 'col'), parts along dimension 0
There are 2 independent parts, one for each index of `img`. A program takes and returns all parts, laid end to end along the dimension named above; an argument that names none is the same for every part. Nothing has to cross between parts.
All inputs are finite; a program needn't handle non-finite values.
Results may differ from a plain program's by a relative error of at most 0.013.
Values may be sent and summed in bfloat16 or wider, within the bound.
No kernel may reach another device: no remote copies, remote signals or barrier semaphores. Data moves between devices by JAX's collectives and lax.ppermute only.
A program may use at most 128 MiB of HBM per device.

v0:
```python
import functools
import math

import jax
import jax.numpy as jnp
import numpy as np
from jax import lax
from jax.experimental import pallas as pl
from jax.experimental.pallas import tpu as pltpu
from jax.sharding import PartitionSpec as P

F32 = jnp.float32
BF16 = jnp.bfloat16
VMEM_LIMIT = 48 * 1024 * 1024

H, W = 256, 1024
ROWS, COLS = 16, 4
PEERS = ROWS * COLS
NF = W // 2 // PEERS
CF = 96
HS = H // PEERS
LANES = HS * CF
MID = H // HS


def bf(table):
    return np.asarray(table, np.float32).astype(jnp.bfloat16)


@functools.lru_cache(None)
def width_tables():
    k = np.arange(W // 2)
    w = np.arange(W)
    angle = 2 * math.pi / W * ((w[:, None] * k[None, :]) % W)
    alternate = np.where(w % 2 == 0, 1.0, -1.0)
    cos, sin = np.cos(angle), np.sin(angle)
    fwd = np.stack([cos, np.where(k[None, :] == 0, alternate[:, None], -sin)], 0)
    inv = np.stack([np.where(k[None, :] == 0, 1.0, 2.0) * cos, np.where(k[None, :] == 0, alternate[:, None], -2.0 * sin)], 0)
    order = lambda t: t.reshape(2, W, PEERS, NF).transpose(2, 0, 3, 1).reshape(W, W)
    norm = 1.0 / math.sqrt(W)
    return bf(order(fwd) * norm), bf(order(inv).T * norm)


@functools.lru_cache(None)
def height_tables():
    m = np.arange(MID)
    angle = 2 * math.pi / MID * ((m[:, None] * m[None, :]) % MID)
    cos, sin = np.cos(angle), np.sin(angle)
    norm = 1.0 / math.sqrt(H)
    fwd = np.zeros((2, NF + 1, 2, MID, MID, 2, NF))
    inv = np.zeros((2, MID, 2, NF, NF + 1, 2, MID))
    for z in range(2):
        for f in range(NF + 1):
            src = f % NF
            use_re = f < NF and True
            if f < NF and not (z and f == 0):
                fwd[z, f, 0, :, :, 0, f] = cos
                fwd[z, f, 0, :, :, 1, f] = sin
                fwd[z, f, 1, :, :, 0, f] = -sin
                fwd[z, f, 1, :, :, 1, f] = cos
                inv[z, :, 0, f, f, 0, :] = cos
                inv[z, :, 0, f, f, 1, :] = -sin
                inv[z, :, 1, f, f, 0, :] = sin
                inv[z, :, 1, f, f, 1, :] = cos
            elif z:
                part = 0 if f == 0 else 1
                fwd[z, f, 0, :, :, part, 0] = cos
                fwd[z, f, 1, :, :, part, 0] = -sin
                inv[z, :, part, 0, f, 0, :] = cos
                inv[z, :, part, 0, f, 1, :] = -sin
    size = 2 * NF * MID
    wide = 2 * (NF + 1) * MID
    return bf(fwd.reshape(2, wide, size) * norm), bf(inv.reshape(2, size, 3, wide // 3).transpose(0, 2, 1, 3) * norm)


@functools.lru_cache(None)
def twiddles():
    m = np.arange(MID)[:, None]
    r = np.repeat(np.arange(HS), CF)[None, :]
    angle = 2 * math.pi / H * (m * r)
    return np.stack([np.cos(angle), -np.sin(angle)], 0).astype(np.float32)


def quarter_turn(t):
    return np.round(np.cos(math.pi / 2 * t)), np.round(np.sin(math.pi / 2 * t))


@functools.lru_cache(None)
def mix_signs():
    j = np.arange(HS)[:, None]
    r = np.arange(HS)[None, :]
    c, s = quarter_turn(j * r)
    s = -s
    real = np.stack([c, -s], 1)
    imag = np.stack([s, c], 1)
    return real.astype(np.float32), imag.astype(np.float32)


@functools.lru_cache(None)
def unmix_table():
    table = np.zeros((HS, 2, CF, 2, HS, CF))
    eye = np.eye(CF)
    for j in range(HS):
        for r in range(HS):
            c, s = quarter_turn(np.asarray(j * r))
            table[j, 0, :, 0, r, :] = c * eye
            table[j, 1, :, 0, r, :] = -s * eye
            table[j, 0, :, 1, r, :] = s * eye
            table[j, 1, :, 1, r, :] = c * eye
    return bf(table.reshape(HS, 2 * CF, 2 * LANES))


def dot(a, b):
    return jnp.dot(a, b, preferred_element_type=F32)


def dot_nt(a, b):
    return lax.dot_general(a, b, (((1,), (1,)), ((), ())), preferred_element_type=F32)


def call(body, out_shape, flops, nbytes, **kw):
    return pl.pallas_call(
        body,
        out_shape=out_shape,
        compiler_params=pltpu.CompilerParams(vmem_limit_bytes=VMEM_LIMIT),
        cost_estimate=pl.CostEstimate(flops=flops, bytes_accessed=nbytes, transcendentals=0),
        **kw,
    )


def section_body(x_ref, w_ref, scale_ref, shift_ref, o_ref):
    skip = x_ref.shape[1] - w_ref.shape[1]
    for h in range(x_ref.shape[0]):
        lin = dot(w_ref[...], x_ref[h, skip:, :])
        o_ref[h] = jnp.maximum(scale_ref[...] * lin + shift_ref[...], 0.0).astype(BF16)


def width_body(t_ref, d_ref, o_ref):
    wide = d_ref.shape[2]
    total = dot_nt(t_ref[:, :wide], d_ref[0])
    for p in range(1, d_ref.shape[0]):
        total = total + dot_nt(t_ref[:, p * wide : (p + 1) * wide], d_ref[p])
    o_ref[...] = total.astype(BF16)


def middle_body(z_ref, fwd_ref, inv_ref, d_ref, tw_ref, g_ref, q_ref, scale_ref, shift_ref, o_ref, total):
    step = pl.program_id(0)
    count = fwd_ref.shape[1] // (2 * MID)
    u = dot(fwd_ref[0], d_ref[...])
    twr, twi = tw_ref[0], tw_ref[1]
    rows = []
    for f in range(count):
        ur = u[2 * f * MID : (2 * f + 1) * MID]
        ui = u[(2 * f + 1) * MID : (2 * f + 2) * MID]
        rows.append(jnp.concatenate([ur * twr - ui * twi, ur * twi + ui * twr], 1).astype(BF16))
    v = jnp.concatenate(rows, 0)
    back = None
    for j in range(HS):
        mixed = dot(v, g_ref[j])
        active = jnp.maximum(scale_ref[...] * mixed + shift_ref[...], 0.0).astype(BF16)
        term = dot(active, q_ref[j])
        back = term if back is None else back + term
    rows = []
    for f in range(count):
        br = back[f * MID : (f + 1) * MID, :LANES]
        bi = back[f * MID : (f + 1) * MID, LANES:]
        rows.append((br * twr + bi * twi).astype(BF16))
        rows.append((bi * twr - br * twi).astype(BF16))
    part = dot(inv_ref[0, 0], jnp.concatenate(rows, 0))

    @pl.when(step == 0)
    def _():
        total[...] = part

    @pl.when(step > 0)
    def _():
        total[...] += part

    @pl.when(step == pl.num_programs(0) - 1)
    def _():
        o_ref[...] = total[...].astype(BF16)


def inverse_body(t_ref, d_ref, o_ref):
    o_ref[...] = dot(t_ref[...], d_ref[...]).astype(BF16)


def conv_body(x_ref, wl_ref, wg_ref, wm_ref, sec_ref, o_ref):
    h = pl.program_id(0)
    cl = wl_ref.shape[1] // 3
    cg = wg_ref.shape[1] // 3
    channels = cl + cg
    width = o_ref.shape[2]
    ext = x_ref.shape[2]
    rows = [x_ref[h + dy] for dy in range(3)]
    local = jnp.concatenate([row[:cl] for row in rows], 0)
    other = jnp.concatenate([row[cl:] for row in rows], 0)
    parts = []
    for dx in range(3):
        yl = dot(wl_ref[dx * channels : (dx + 1) * channels], local)
        yg = dot(wg_ref[dx * cl : (dx + 1) * cl], other)
        parts.append(jnp.concatenate([yl[:cl] + yg, yl[cl:]], 0))
    acc = parts[1] + pltpu.roll(parts[0], 1, 1) + pltpu.roll(parts[2], ext - 1, 1)
    mix = dot(wm_ref[...], sec_ref[0])
    o_ref[0, :cl] = acc[:cl, :width].astype(BF16)
    o_ref[0, cl:] = (acc[cl:, :width] + mix).astype(BF16)


def final_body(x_ref, pre_ref, f_ref, w_ref, scale_ref, shift_ref, o_ref):
    outs = w_ref.shape[0] // HS
    low = x_ref.shape[1] - outs
    res = dot_nt(w_ref[...], f_ref[0])
    for r in range(HS):
        pre = pre_ref[r].astype(F32)
        pre = jnp.concatenate([pre[:low], pre[low:] + res[r * outs : (r + 1) * outs]], 0)
        act = jnp.maximum(scale_ref[...] * pre + shift_ref[...], 0.0)
        o_ref[r] = (x_ref[r].astype(F32) + act).astype(BF16)


def shift_along(block, axis, step):
    count = lax.axis_size(axis)
    pairs = [(i, i + step) for i in range(count) if 0 <= i + step < count]
    return lax.ppermute(block, axis, pairs)


def full(shape):
    return pl.BlockSpec(shape, lambda *_: (0,) * len(shape))


def per_device(
    image,
    from_local,
    from_global,
    section_weight,
    section_scale,
    section_shift,
    fourier_weight,
    fourier_scale,
    fourier_shift,
    mix_weight,
    out_scale,
    out_shift,
):
    channels, rows, width = image.shape
    cl = from_local.shape[2]
    cg = channels - cl
    holds_zero = jnp.logical_and(lax.axis_index("row") == 0, lax.axis_index("col") == 0)
    z = holds_zero.astype(jnp.int32).reshape(1)

    x = jnp.transpose(image, (1, 0, 2))
    section = call(
        section_body,
        jax.ShapeDtypeStruct((rows, CF, width), BF16),
        2 * rows * CF * cg * width,
        4 * 2**20,
    )(x, section_weight, section_scale[:, None], section_shift[:, None])

    sent = lax.all_to_all(section.reshape(COLS, HS * CF, width), "col", split_axis=0, concat_axis=0, tiled=True)

    fwd_w, inv_w = width_tables()
    spectra = call(
        width_body,
        jax.ShapeDtypeStruct((W, LANES), BF16),
        2 * W * W * LANES,
        4 * 2**20,
        grid=(4,),
        in_specs=[pl.BlockSpec((W // 4, W), lambda i: (i, 0)), full((COLS, LANES, width))],
        out_specs=pl.BlockSpec((W // 4, LANES), lambda i: (i, 0)),
    )(jnp.asarray(fwd_w), sent)

    spectra = lax.all_to_all(
        spectra.reshape(PEERS, 2 * NF, LANES), ("row", "col"), split_axis=0, concat_axis=0, tiled=True
    ).reshape(W, LANES)

    fwd_h, inv_h = height_tables()
    sign_re, sign_im = mix_signs()
    fw_re = fourier_weight[:, :CF].T[None, None, None]
    fw_im = fourier_weight[:, CF:].T[None, None, None]
    mixer = (
        jnp.asarray(sign_re, BF16)[..., None, None] * fw_re + jnp.asarray(sign_im, BF16)[..., None, None] * fw_im
    ).reshape(HS, 2 * LANES, 2 * CF)
    wide = 2 * (NF + 1) * MID // 3
    returned = pl.pallas_call(
        middle_body,
        out_shape=jax.ShapeDtypeStruct((W, LANES), BF16),
        grid_spec=pltpu.PrefetchScalarGridSpec(
            num_scalar_prefetch=1,
            grid=(3,),
            in_specs=[
                pl.BlockSpec((1, wide, W), lambda i, s: (s[0], i, 0)),
                pl.BlockSpec((1, 1, W, wide), lambda i, s: (s[0], i, 0, 0)),
                full((W, LANES)),
                full((2, MID, LANES)),
                full((HS, 2 * LANES, 2 * CF)),
                full((HS, 2 * CF, 2 * LANES)),
                full((1, 2 * CF)),
                full((1, 2 * CF)),
            ],
            out_specs=full((W, LANES)),
            scratch_shapes=[pltpu.VMEM((W, LANES), F32)],
        ),
        compiler_params=pltpu.CompilerParams(vmem_limit_bytes=VMEM_LIMIT),
        cost_estimate=pl.CostEstimate(flops=3 * 10**9, bytes_accessed=10 * 2**20, transcendentals=0),
    )(
        z,
        jnp.asarray(fwd_h),
        jnp.asarray(inv_h),
        spectra,
        jnp.asarray(twiddles()),
        mixer,
        jnp.asarray(unmix_table()),
        fourier_scale[None],
        fourier_shift[None],
    )

    returned = lax.all_to_all(
        returned.reshape(PEERS, 2 * NF, LANES), ("row", "col"), split_axis=0, concat_axis=0, tiled=True
    ).reshape(W, LANES)

    fourier = call(
        inverse_body,
        jax.ShapeDtypeStruct((W, LANES), BF16),
        2 * W * W * LANES,
        4 * 2**20,
        grid=(4,),
        in_specs=[pl.BlockSpec((W // 4, W), lambda i: (i, 0)), full((W, LANES))],
        out_specs=pl.BlockSpec((W // 4, LANES), lambda i: (i, 0)),
    )(jnp.asarray(inv_w), returned)
    fourier = lax.all_to_all(
        fourier.reshape(COLS, width, LANES), "col", split_axis=0, concat_axis=0, tiled=True
    )

    above = shift_along(x[rows - 1], "row", 1)
    below = shift_along(x[0], "row", -1)
    tall = jnp.concatenate([above[None], x, below[None]], 0)
    left = shift_along(tall[:, :, width - 1], "col", 1)
    right = shift_along(tall[:, :, 0], "col", -1)
    ext = width + 128
    padded = jnp.concatenate(
        [tall, right[:, :, None], jnp.zeros((rows + 2, channels, 126), BF16), left[:, :, None]], 2
    )
    wl = from_local.reshape(3, 3, channels, cl).transpose(1, 2, 0, 3).reshape(3 * channels, 3 * cl)
    wg = from_global.reshape(3, 3, cl, cg).transpose(1, 2, 0, 3).reshape(3 * cl, 3 * cg)
    pre = call(
        conv_body,
        jax.ShapeDtypeStruct((rows, channels, width), BF16),
        3 * 10**9,
        6 * 2**20,
        grid=(rows,),
        in_specs=[
            full((rows + 2, channels, ext)),
            full((3 * channels, 3 * cl)),
            full((3 * cl, 3 * cg)),
            full((cg, CF)),
            pl.BlockSpec((1, CF, width), lambda i: (i, 0, 0)),
        ],
        out_specs=pl.BlockSpec((1, channels, width), lambda i: (i, 0, 0)),
    )(padded, wl, wg, mix_weight, section)

    eye = jnp.asarray(np.eye(HS, dtype=np.float32), BF16)
    mix4 = (eye[:, None, :, None] * mix_weight[None, :, None, :]).reshape(HS * cg, LANES)
    result = call(
        final_body,
        jax.ShapeDtypeStruct((rows, channels, width), BF16),
        10**9,
        7 * 2**20,
        grid=(COLS,),
        in_specs=[
            pl.BlockSpec((HS, channels, width), lambda i: (i, 0, 0)),
            pl.BlockSpec((HS, channels, width), lambda i: (i, 0, 0)),
            pl.BlockSpec((1, width, LANES), lambda i: (i, 0, 0)),
            full((HS * cg, LANES)),
            full((channels, 1)),
            full((channels, 1)),
        ],
        out_specs=pl.BlockSpec((HS, channels, width), lambda i: (i, 0, 0)),
    )(x, pre, fourier, mix4, out_scale[:, None], out_shift[:, None])
    return jnp.transpose(result, (1, 0, 2))


def solution(mesh):
    return jax.shard_map(
        per_device,
        mesh=mesh,
        in_specs=(P("img", "row", "col"), P(), P(), P(), P(), P(), P(), P(), P(), P(), P(), P()),
        out_specs=P("img", "row", "col"),
        check_vma=False,
    )
```

profile of v0, /device:TPU:1, one launch (start us, length us, event | category | flops | bytes accessed | tf_op | source)
XLA Modules:
  0.0 131.8 jit_solution(8605254982591225452)
XLA Ops:
  0.0 2.3 %copy.61 = bf16[256,16,256]{2,0,1:T(8,128)(2,1)S(1)} copy(bf16[256,16,256]{2,1,0:T(8,128)(2,1)} %param.21) | data formatting | bytes 4194304 | tf_op args[0]
  3.1 14.9 %all_to_all.20.d_ref = bf16[4,384,256]{2,1,0:T(8,128)(2,1)S(1)} all-to-all(bf16[4,384,256]{2,1,0:T(8,128)(2,1)S(1)} %bitcast.52), channel_id=1, replica_groups=mesh['img'=2,'row'=16,'col'=4] {'col'}, dimensions={0} | all-to-all | bytes 1572864 | tf_op jit(solution)/shard_map/all_to_all | solution.py:258
  18.9 1.8 %shard_map.201 = bf16[1024,384]{1,0:T(8,128)(2,1)S(1)} custom-call(bf16[1024,1024]{1,0:T(8,128)(2,1)S(1)} %copy-done.6, bf16[4,384,256]{2,1,0:T(8,128)(2,1)S(1)} %all_to_all.20.d_ref), custom_call_target="tpu_custom_call" | custom-call | flops 805306368 | bytes 4194304 | tf_op jit(solution)/shard_map/pallas_call | solution.py:261
  21.7 9.5 %all-to-all-start.1 = ((bf16[64,16,384]{2,1,0:T(8,128)(2,1)}), bf16[64,16,384]{2,1,0:T(8,128)(2,1)S(1)}, u32[]{:S(2)}, u32[]{:S(2)}) async-start(bf16[64,16,384]{2,1,0:T(8,128)(2,1)} %bitcast.50), calls=%async_computation.1 | async-start | bytes 1572864 | tf_op jit(solution)/shard_map/all_to_all | solution.py:271
  31.9 1.9 %multiply_add_fusion.g_ref = bf16[4,768,192]{2,1,0:T(8,128)(2,1)} fusion(bf16[768,192]{1,0:T(8,128)(2,1)S(1)} %bitcast.56, bf16[4,768]{1,0:T(4,128)(2,1)S(1)} %mul.69, bf16[768,192]{1,0:T(8,128)(2,1)S(1)} %bitcast.55, bf16[4,768]{1,0:T(4,128)(2,1)S(1)} %mul.62), kind=kLoop, calls=%fused_computation.3 | loop fusion | flops 1769472 | bytes 1781760 | tf_op jit(solution)/shard_map/add | solution.py:280
  33.8 12.6 %all-to-all-done.1 = bf16[64,16,384]{2,1,0:T(8,128)(2,1)S(1)} async-done(((bf16[64,16,384]{2,1,0:T(8,128)(2,1)}), bf16[64,16,384]{2,1,0:T(8,128)(2,1)S(1)}, u32[]{:S(2)}, u32[]{:S(2)}) %all-to-all-start.1) | async-done | bytes 786464 | tf_op jit(solution)/shard_map/all_to_all | solution.py:271
  46.4 1.4 %copy-done = bf16[4,768,192]{2,1,0:T(8,128)(2,1)S(1)} copy-done((bf16[4,768,192]{2,1,0:T(8,128)(2,1)S(1)}, bf16[4,768,192]{2,1,0:T(8,128)(2,1)}, u32[]{:S(2)}) %copy-start) | copy-done | bytes 1179672
  49.1 9.9 %shard_map.202 = bf16[1024,384]{1,0:T(8,128)(2,1)} custom-call(s32[1]{0:T(128)} %bitcast.13.z_ref, bf16[2,1152,1024]{2,1,0:T(8,128)(2,1)} %constant.34.clone.fwd_ref, bf16[2,3,1024,384]{3,2,1,0:T(8,128)(2,1)} %constant.35.clone.inv_ref, bf16[1024,384]{1,0:T(8,128)(2,1)S(1)} %bitcast.49, f32[2,64,384]{2,1,0:T(8,128)S(1)} %copy-done.13, ...), custom_call_target="tpu_custom_call" | custom-call | flops 3000000000 | bytes 10485760 | tf_op jit(solution)/shard_map/pallas_call | solution.py:283
  59.0 4.6 %all-to-all-start.2 = ((bf16[64,16,384]{2,1,0:T(8,128)(2,1)}), bf16[64,16,384]{2,1,0:T(8,128)(2,1)S(1)}, u32[]{:S(2)}, u32[]{:S(2)}) async-start(bf16[64,16,384]{2,1,0:T(8,128)(2,1)} %bitcast.23), calls=%async_computation.2 | async-start | bytes 1572864 | tf_op jit(solution)/shard_map/all_to_all | solution.py:316
  63.6 3.3 %collective-permute-start = (bf16[256,256]{1,0:T(8,128)(2,1)S(1)}, bf16[256,256]{1,0:T(8,128)(2,1)S(1)}, u32[]{:S(2)}, u32[]{:S(2)}) collective-permute-start(bf16[256,256]{1,0:T(8,128)(2,1)S(1)} %get-tuple-element.7), channel_id=1, source_target_pairs={{0,4},{4,8},{8,12},{12,16},{16,20},{20,24},{24,28},{28,32},{32,36}... | collective-permute-start | bytes 393224 | tf_op jit(solution)/shard_map/ppermute | solution.py:223
  68.2 8.4 %collective-permute-done = bf16[256,256]{1,0:T(8,128)(2,1)S(1)} collective-permute-done((bf16[256,256]{1,0:T(8,128)(2,1)S(1)}, bf16[256,256]{1,0:T(8,128)(2,1)S(1)}, u32[]{:S(2)}, u32[]{:S(2)}) %collective-permute-start) | collective-permute-done | bytes 131104 | tf_op jit(solution)/shard_map/ppermute | solution.py:223
  76.6 2.1 %collective-permute-done.1 = bf16[256,256]{1,0:T(8,128)(2,1)S(1)} collective-permute-done((bf16[256,256]{1,0:T(8,128)(2,1)S(1)}, bf16[256,256]{1,0:T(8,128)(2,1)S(1)}, u32[]{:S(2)}, u32[]{:S(2)}) %collective-permute-start.1) | collective-permute-done | bytes 131104 | tf_op jit(solution)/shard_map/ppermute | solution.py:223
  80.5 2.5 %collective-permute-start.2 = (bf16[18,256]{1,0:T(8,128)(2,1)S(1)}, bf16[18,256]{1,0:T(8,128)(2,1)}, u32[]{:S(2)}, u32[]{:S(2)}) collective-permute-start(bf16[18,256]{1,0:T(8,128)(2,1)S(1)} %get-tuple-element.5), channel_id=1, source_target_pairs={{1,0},{2,1},{3,2},{5,4},{6,5},{7,6},{9,8},{10,9},{11,10},{13,12},{... | collective-permute-start | bytes 27656 | tf_op jit(solution)/shard_map/ppermute | solution.py:223
  83.0 3.0 %collective-permute-start.3 = (bf16[18,256]{1,0:T(8,128)(2,1)S(1)}, bf16[18,256]{1,0:T(8,128)(2,1)}, u32[]{:S(2)}, u32[]{:S(2)}) collective-permute-start(bf16[18,256]{1,0:T(8,128)(2,1)S(1)} %get-tuple-element.6), channel_id=1, source_target_pairs={{0,1},{1,2},{2,3},{4,5},{5,6},{6,7},{8,9},{9,10},{10,11},{12,13},{... | collective-permute-start | bytes 27656 | tf_op jit(solution)/shard_map/ppermute | solution.py:223
  90.8 1.8 %mul.78.w_ref = bf16[768,384]{1,0:T(8,128)(2,1)S(1)} reshape(bf16[4,192,4,96]{3,2,1,0:T(4,128)(2,1)} %broadcast_multiply_fusion) | data formatting | bytes 1179648 | tf_op jit(solution)/shard_map/mul | solution.py:361
  94.3 2.2 %copy.46 = bf16[18,256,1]{2,1,0:T(8,128)(2,1)} copy(bf16[18,256,1]{1,0,2:T(8,128)(2,1)} %bitcast.5) | data formatting | bytes 18432 | tf_op jit(solution)/shard_map/broadcast_in_dim | solution.py:340
  96.5 2.2 %copy.47 = bf16[18,256,1]{2,1,0:T(8,128)(2,1)} copy(bf16[18,256,1]{1,0,2:T(8,128)(2,1)} %bitcast.6) | data formatting | bytes 18432 | tf_op jit(solution)/shard_map/broadcast_in_dim | solution.py:340
  98.7 1.6 %copy-done.5 = bf16[1024,1024]{1,0:T(8,128)(2,1)S(1)} copy-done((bf16[1024,1024]{1,0:T(8,128)(2,1)S(1)}, bf16[1024,1024]{1,0:T(8,128)(2,1)}, u32[]{:S(2)}) %copy-start.5) | copy-done | bytes 2097176
  100.2 1.8 %shard_map.203 = bf16[1024,384]{1,0:T(8,128)(2,1)S(1)} custom-call(bf16[1024,1024]{1,0:T(8,128)(2,1)S(1)} %copy-done.5, bf16[1024,384]{1,0:T(8,128)(2,1)S(1)} %bitcast.48), custom_call_target="tpu_custom_call" | custom-call | flops 805306368 | bytes 4194304 | tf_op jit(solution)/shard_map/pallas_call | solution.py:320
  102.9 3.7 %all-to-all-start.3 = ((bf16[4,256,384]{2,1,0:T(8,128)(2,1)}), bf16[4,256,384]{2,1,0:T(8,128)(2,1)S(1)}, u32[]{:S(2)}, u32[]{:S(2)}) async-start(bf16[4,256,384]{2,1,0:T(8,128)(2,1)} %bitcast.51), calls=%async_computation.3 | async-start | bytes 1572864 | tf_op jit(solution)/shard_map/all_to_all | solution.py:329
  106.6 4.3 %pad_maximum_fusion.x_ref = bf16[18,256,384]{2,1,0:T(8,128)(2,1)} fusion(bf16[18,256,1]{2,1,0:T(8,128)(2,1)} %copy.47, bf16[18,256,1]{2,1,0:T(8,128)(2,1)} %copy.46, bf16[1,256,256]{2,1,0:T(8,128)(2,1)} %bitcast.63, bf16[16,256,256]{2,1,0:T(8,128)(2,1)S(1)} %bitcast.45, bf16[1,256,256]{2,1,0:T(8,128)(2,1)} %bitcast.61, bf16[384]{0:T(512)(128)(2,1)S(1)} %pad.4.clone), kind=kLoop, calls=%fused_computation | loop fusion | flops 21233664 | bytes 5917440 | tf_op jit(solution)/shard_map/concatenate | solution.py:339
  111.0 11.7 %shard_map.200.pre_ref = bf16[16,256,256]{2,1,0:T(8,128)(2,1)S(1)} custom-call(bf16[18,256,384]{2,1,0:T(8,128)(2,1)} %pad_maximum_fusion.x_ref, bf16[768,192]{1,0:T(8,128)(2,1)S(1)} %copy-done.11, bf16[192,576]{1,0:T(8,128)(2,1)S(1)} %copy-done.12, bf16[192,96]{1,0:T(8,128)(2,1)S(1)} %copy-done.14, bf16[16,96,256]{2,1,0:T(8,128)(2,1)S(1)} %copy-done.4), custom_call_target="tpu_custom_call" | custom-call | flops 3000000000 | bytes 6291456 | tf_op jit(solution)/shard_map/pallas_call | solution.py:344
  125.8 3.5 %shard_map.204 = bf16[16,256,256]{2,1,0:T(8,128)(2,1)S(1)} custom-call(bf16[16,256,256]{2,1,0:T(8,128)(2,1)S(1)} %bitcast.46, bf16[16,256,256]{2,1,0:T(8,128)(2,1)} %copy-done.7, bf16[4,256,384]{2,1,0:T(8,128)(2,1)S(1)} %all-to-all-done.3.f_ref, bf16[768,384]{1,0:T(8,128)(2,1)S(1)} %mul.78.w_ref, f32[256,1]{1,0:T(8,128)S(1)} %copy-done.9, ...), custom_call_target="tpu_custom_call" | custom-call | flops 1000000000 | bytes 7340032 | tf_op jit(solution)/shard_map/pallas_call | solution.py:362
  129.3 2.5 %copy.57 = bf16[256,16,256]{2,1,0:T(8,128)(2,1)} copy(bf16[256,16,256]{2,0,1:T(8,128)(2,1)S(1)} %bitcast.47) | data formatting | bytes 4194304 | tf_op jit(solution)/shard_map/transpose | solution.py:378
  (86 shorter events, 18.0 us)
Async XLA Ops:
  0.0 2.5 %copy-start.28 = (f32[96]{0:T(128)S(1)}, f32[96]{0:T(128)}, u32[]{:S(2)}) copy-start(f32[96]{0:T(128)} %param.26) | copy-start | bytes 1156
  0.0 2.6 %copy-start.15 = (bf16[96,192]{1,0:T(8,128)(2,1)S(1)}, bf16[96,192]{1,0:T(8,128)(2,1)}, u32[]{:S(2)}) copy-start(bf16[96,192]{1,0:T(8,128)(2,1)} %w_ref.1) | copy-start | bytes 110596
  2.6 16.4 %copy-start.6 = (bf16[1024,1024]{1,0:T(8,128)(2,1)S(1)}, bf16[1024,1024]{1,0:T(8,128)(2,1)}, u32[]{:S(2)}) copy-start(bf16[1024,1024]{1,0:T(8,128)(2,1)} %constant.31.clone.t_ref) | copy-start | bytes 6291460
  18.9 12.3 %copy-start.21 = (bf16[192,192]{1,0:T(8,128)(2,1)S(1)}, bf16[192,192]{1,0:T(8,128)(2,1)}, u32[]{:S(2)}) copy-start(bf16[192,192]{1,0:T(8,128)(2,1)} %param.27) | copy-start | bytes 221188
  18.9 12.6 %copy-start.23 = (bf16[4,2,4]{2,1,0:T(2,128)(2,1)S(1)}, bf16[4,2,4]{2,1,0:T(2,128)(2,1)}, u32[]{:S(2)}) copy-start(bf16[4,2,4]{2,1,0:T(2,128)(2,1)} %constant.32.clone) | copy-start | bytes 196
  18.9 12.8 %copy-start.22 = (bf16[4,2,4]{2,1,0:T(2,128)(2,1)S(1)}, bf16[4,2,4]{2,1,0:T(2,128)(2,1)}, u32[]{:S(2)}) copy-start(bf16[4,2,4]{2,1,0:T(2,128)(2,1)} %constant.33.clone) | copy-start | bytes 196
  21.7 24.7 %copy-start.13 = (f32[2,64,384]{2,1,0:T(8,128)S(1)}, f32[2,64,384]{2,1,0:T(8,128)}, u32[]{:S(2)}) copy-start(f32[2,64,384]{2,1,0:T(8,128)} %constant.36.clone.tw_ref) | copy-start | bytes 589828
  21.7 24.7 %copy-start.16 = (f32[192]{0:T(256)S(1)}, f32[192]{0:T(256)}, u32[]{:S(2)}) copy-start(f32[192]{0:T(256)} %param.28) | copy-start | bytes 2308
  21.7 24.7 %copy-start.17 = (f32[192]{0:T(256)S(1)}, f32[192]{0:T(256)}, u32[]{:S(2)}) copy-start(f32[192]{0:T(256)} %param.29) | copy-start | bytes 2308
  21.7 24.7 %all-to-all-start.1 = ((bf16[64,16,384]{2,1,0:T(8,128)(2,1)}), bf16[64,16,384]{2,1,0:T(8,128)(2,1)S(1)}, u32[]{:S(2)}, u32[]{:S(2)}) async-start(bf16[64,16,384]{2,1,0:T(8,128)(2,1)} %bitcast.50), calls=%async_computation.1 | async-start | bytes 1572864 | tf_op jit(solution)/shard_map/all_to_all | solution.py:271
  59.0 39.6 %all-to-all-start.2 = ((bf16[64,16,384]{2,1,0:T(8,128)(2,1)}), bf16[64,16,384]{2,1,0:T(8,128)(2,1)S(1)}, u32[]{:S(2)}, u32[]{:S(2)}) async-start(bf16[64,16,384]{2,1,0:T(8,128)(2,1)} %bitcast.23), calls=%async_computation.2 | async-start | bytes 1572864 | tf_op jit(solution)/shard_map/all_to_all | solution.py:316
  63.6 13.0 %collective-permute-start = (bf16[256,256]{1,0:T(8,128)(2,1)S(1)}, bf16[256,256]{1,0:T(8,128)(2,1)S(1)}, u32[]{:S(2)}, u32[]{:S(2)}) collective-permute-start(bf16[256,256]{1,0:T(8,128)(2,1)S(1)} %get-tuple-element.7), channel_id=1, source_target_pairs={{0,4},{4,8},{8,12},{12,16},{16,20},{20,24},{24,28},{28,32},{32,36}... | collective-permute-start | bytes 393224 | tf_op jit(solution)/shard_map/ppermute | solution.py:223
  66.9 11.8 %collective-permute-start.1 = (bf16[256,256]{1,0:T(8,128)(2,1)S(1)}, bf16[256,256]{1,0:T(8,128)(2,1)S(1)}, u32[]{:S(2)}, u32[]{:S(2)}) collective-permute-start(bf16[256,256]{1,0:T(8,128)(2,1)S(1)} %get-tuple-element.8), channel_id=1, source_target_pairs={{4,0},{8,4},{12,8},{16,12},{20,16},{24,20},{28,24},{32,28},{36,32}... | collective-permute-start | bytes 393224 | tf_op jit(solution)/shard_map/ppermute | solution.py:223
  79.4 6.7 %copy-start.14 = (bf16[192,96]{1,0:T(8,128)(2,1)S(1)}, bf16[192,96]{1,0:T(8,128)(2,1)}, u32[]{:S(2)}) copy-start(bf16[192,96]{1,0:T(8,128)(2,1)} %wm_ref.1) | copy-start | bytes 110596
  79.4 6.7 %copy-start.26 = (bf16[4,4]{1,0:T(4,128)(2,1)S(1)}, bf16[4,4]{1,0:T(4,128)(2,1)}, u32[]{:S(2)}) copy-start(bf16[4,4]{1,0:T(4,128)(2,1)} %constant.39.clone) | copy-start | bytes 100
  79.4 7.9 %copy-start.20 = (bf16[9,256,64]{1,2,0:T(8,128)(2,1)S(1)}, bf16[9,256,64]{1,2,0:T(8,128)(2,1)}, u32[]{:S(2)}) copy-start(bf16[9,256,64]{1,2,0:T(8,128)(2,1)} %param.22) | copy-start | bytes 884740
  80.5 13.8 %collective-permute-start.2 = (bf16[18,256]{1,0:T(8,128)(2,1)S(1)}, bf16[18,256]{1,0:T(8,128)(2,1)}, u32[]{:S(2)}, u32[]{:S(2)}) collective-permute-start(bf16[18,256]{1,0:T(8,128)(2,1)S(1)} %get-tuple-element.5), channel_id=1, source_target_pairs={{1,0},{2,1},{3,2},{5,4},{6,5},{7,6},{9,8},{10,9},{11,10},{13,12},{... | collective-permute-start | bytes 27656 | tf_op jit(solution)/shard_map/ppermute | solution.py:223
  83.0 13.4 %collective-permute-start.3 = (bf16[18,256]{1,0:T(8,128)(2,1)S(1)}, bf16[18,256]{1,0:T(8,128)(2,1)}, u32[]{:S(2)}, u32[]{:S(2)}) collective-permute-start(bf16[18,256]{1,0:T(8,128)(2,1)S(1)} %get-tuple-element.6), channel_id=1, source_target_pairs={{0,1},{1,2},{2,3},{4,5},{5,6},{6,7},{8,9},{9,10},{10,11},{12,13},{... | collective-permute-start | bytes 27656 | tf_op jit(solution)/shard_map/ppermute | solution.py:223
  87.3 5.3 %copy-start.24 = (f32[256]{0:T(256)S(1)}, f32[256]{0:T(256)}, u32[]{:S(2)}) copy-start(f32[256]{0:T(256)} %param.31) | copy-start | bytes 3076
  87.3 6.1 %copy-start.25 = (f32[256]{0:T(256)S(1)}, f32[256]{0:T(256)}, u32[]{:S(2)}) copy-start(f32[256]{0:T(256)} %param.32) | copy-start | bytes 3076
  102.9 21.0 %all-to-all-start.3 = ((bf16[4,256,384]{2,1,0:T(8,128)(2,1)}), bf16[4,256,384]{2,1,0:T(8,128)(2,1)S(1)}, u32[]{:S(2)}, u32[]{:S(2)}) async-start(bf16[4,256,384]{2,1,0:T(8,128)(2,1)} %bitcast.51), calls=%async_computation.3 | async-start | bytes 1572864 | tf_op jit(solution)/shard_map/all_to_all | solution.py:329
  106.6 4.3 %copy-start.4 = (bf16[16,96,256]{2,1,0:T(8,128)(2,1)S(1)}, bf16[16,96,256]{2,1,0:T(8,128)(2,1)}, u32[]{:S(2)}) copy-start(bf16[16,96,256]{2,1,0:T(8,128)(2,1)} %copy-done.3) | copy-start | bytes 2359300
  106.6 4.3 %copy-start.11 = (bf16[768,192]{1,0:T(8,128)(2,1)S(1)}, bf16[768,192]{1,0:T(8,128)(2,1)}, u32[]{:S(2)}) copy-start(bf16[768,192]{1,0:T(8,128)(2,1)} %copy.52.wl_ref) | copy-start | bytes 884740
  106.6 4.3 %copy-start.12 = (bf16[192,576]{1,0:T(8,128)(2,1)S(1)}, bf16[192,576]{1,0:T(8,128)(2,1)}, u32[]{:S(2)}) copy-start(bf16[192,576]{1,0:T(8,128)(2,1)} %reshape.53.wg_ref) | copy-start | bytes 663556
  (12 other events, 15.5 us)
where the time goes:
time: 133 us; the launch traced here: 132 us
  Pallas kernels  29.2 us (22%)
  local copies, waits for them, and re-layouts  28.6 us (22%)
  starting transfers between devices  27.9 us (21%)
  waiting for transfers between devices  23.1 us (17%)
  blocking collectives  14.9 us (11%)
  other arithmetic  7.74 us (6%)
    all_to_all x1, blocking collectives, per_device(): lax.all_to_all(section.reshape(COLS, HS * CF, width), 'col', split_axis=0...  14.9 us
    unnamed x60, local copies, waits for them, and re-layouts  12.9 us
    all_to_all x1, waiting for transfers between devices, per_device(): lax.all_to_all(spectra.reshape(PEERS, 2 * NF, LANES), ('row', 'col'), spl...  12.6 us
    pallas_call x1, Pallas kernels, per_device(): call(conv_body, jax.ShapeDtypeStruct((rows, channels, width), BF16), 3 *...  11.7 us
    ppermute x4, waiting for transfers between devices, shift_along(): return lax.ppermute(block, axis, pairs)  10.5 us
    ppermute x4, starting transfers between devices, shift_along(): return lax.ppermute(block, axis, pairs)  10.2 us
    pallas_call x1, Pallas kernels, per_device(): pl.pallas_call(middle_body, out_shape=jax.ShapeDtypeStruct((W, LANES), BF...  9.94 us
    all_to_all x1, starting transfers between devices, per_device(): lax.all_to_all(spectra.reshape(PEERS, 2 * NF, LANES), ('row', 'col'), spl...  9.51 us
  transfers between devices with their start and end apart: 7, of which 3 were waited for; matrix products, arithmetic and copies ran while one was open for 16% of the time, Pallas kernels for 9%

commit v1 on v0

v1 whole, which is shorter than its diff:
```python
import functools
import math

import jax
import jax.numpy as jnp
import numpy as np
from jax import lax
from jax.experimental import pallas as pl
from jax.experimental.pallas import tpu as pltpu
from jax.sharding import PartitionSpec as P

F32 = jnp.float32
BF16 = jnp.bfloat16
MIB = 1024 * 1024

H, W = 256, 1024
ROWS, COLS = 16, 4
PEERS = ROWS * COLS
NF = W // 2 // PEERS
CF = 96
HS = H // PEERS
LANES = HS * CF
LANE = 128
WIDE = HS * LANE
MID = H // HS
ORDER = (2, 3, 1, 0)


def bf(table):
    return np.asarray(table, np.float32).astype(jnp.bfloat16)


@functools.lru_cache(None)
def width_tables():
    k = np.arange(W // 2)
    w = np.arange(W)
    angle = 2 * math.pi / W * ((w[:, None] * k[None, :]) % W)
    alternate = np.where(w % 2 == 0, 1.0, -1.0)
    cos, sin = np.cos(angle), np.sin(angle)
    fwd = np.stack([cos, np.where(k[None, :] == 0, alternate[:, None], -sin)], 0)
    inv = np.stack([np.where(k[None, :] == 0, 1.0, 2.0) * cos, np.where(k[None, :] == 0, alternate[:, None], -2.0 * sin)], 0)
    order = lambda t: t.reshape(2, W, PEERS, NF).transpose(2, 0, 3, 1).reshape(W, W)
    norm = 1.0 / math.sqrt(W)
    fwd = (order(fwd) * norm).reshape(W, COLS, W // COLS).transpose(1, 0, 2)
    inv = (order(inv).T * norm).reshape(COLS, W // COLS, W)
    return bf(fwd), bf(inv)


@functools.lru_cache(None)
def height_tables():
    m = np.arange(MID)
    angle = 2 * math.pi / MID * ((m[:, None] * m[None, :]) % MID)
    cos, sin = np.cos(angle), np.sin(angle)
    norm = 1.0 / math.sqrt(H)
    fwd = np.zeros((2, NF + 1, 2, MID, MID, 2, NF))
    inv = np.zeros((2, MID, 2, NF, NF + 1, 2, MID))
    for z in range(2):
        for f in range(NF + 1):
            if f < NF and not (z and f == 0):
                fwd[z, f, 0, :, :, 0, f] = cos
                fwd[z, f, 0, :, :, 1, f] = sin
                fwd[z, f, 1, :, :, 0, f] = -sin
                fwd[z, f, 1, :, :, 1, f] = cos
                inv[z, :, 0, f, f, 0, :] = cos
                inv[z, :, 0, f, f, 1, :] = -sin
                inv[z, :, 1, f, f, 0, :] = sin
                inv[z, :, 1, f, f, 1, :] = cos
            elif z:
                part = 0 if f == 0 else 1
                fwd[z, f, 0, :, :, part, 0] = cos
                fwd[z, f, 1, :, :, part, 0] = -sin
                inv[z, :, part, 0, f, 0, :] = cos
                inv[z, :, part, 0, f, 1, :] = -sin
    size = 2 * NF * MID
    wide = 2 * (NF + 1) * MID
    return bf(fwd.reshape(2, wide, size) * norm), bf(inv.reshape(2, size, wide) * norm)


@functools.lru_cache(None)
def twiddles():
    m = np.arange(MID)[:, None]
    r = np.repeat(np.arange(HS), LANE)[None, :]
    angle = 2 * math.pi / H * (m * r)
    return np.stack([np.cos(angle), -np.sin(angle)], 0).astype(np.float32)


def dot(a, b):
    return jnp.dot(a, b, preferred_element_type=F32)


def dot_nt(a, b):
    return lax.dot_general(a, b, (((1,), (1,)), ((), ())), preferred_element_type=F32)


def call(body, out_shape, operands, smem=(), hbm=(), hbm_out=False, limit=16, flops=10**9, **kw):
    place = lambda i: pltpu.SMEM if i in smem else pltpu.HBM if i in hbm else pltpu.VMEM
    out_place = pltpu.HBM if hbm_out else pltpu.VMEM
    operands = [v if i in smem else pltpu.with_memory_space_constraint(v, place(i)) for i, v in enumerate(operands)]
    return pl.pallas_call(
        body,
        out_shape=jax.tree.map(lambda s: out_place(s.shape, s.dtype), out_shape),
        in_specs=[pl.BlockSpec(memory_space=place(i)) for i in range(len(operands))],
        out_specs=jax.tree.map(lambda _: pl.BlockSpec(memory_space=out_place), out_shape),
        compiler_params=pltpu.CompilerParams(vmem_limit_bytes=limit * MIB),
        cost_estimate=pl.CostEstimate(flops=flops, bytes_accessed=4 * MIB, transcendentals=0),
        **kw,
    )(*operands)


def prepare_body(fl_ref, fg_ref, mix_ref, fw_ref, scale_ref, shift_ref, wl_ref, wg_ref, mix4_ref, mixer_ref, affine_ref):
    cl, channels = fl_ref.shape[1], fl_ref.shape[2]
    for dx in range(3):
        taps = jnp.concatenate([fl_ref[3 * dy + dx] for dy in range(3)], 0)
        wl_ref[dx * channels : (dx + 1) * channels] = taps.T
        wg_ref[dx * cl : (dx + 1) * cl] = jnp.concatenate([fg_ref[3 * dy + dx] for dy in range(3)], 1)
    mix = mix_ref[...]
    count = mix.shape[0]
    for r in range(HS):
        sides = [jnp.zeros((count, CF * r), BF16), mix, jnp.zeros((count, LANES - CF * (r + 1)), BF16)]
        mix4_ref[r * count : (r + 1) * count] = jnp.concatenate([s for s in sides if s.shape[1]], 1)
    spread = lambda t: jnp.concatenate([t[:, :CF], gap(t), t[:, CF:], gap(t)], 1)
    gap = lambda t: jnp.zeros((t.shape[0], LANE - CF), t.dtype)
    wide = spread(fw_ref[...].T)
    low = jnp.zeros((LANE - CF, 2 * LANE), BF16)
    mixer_ref[...] = jnp.concatenate([wide[:CF], low, wide[CF:], low], 0)
    affine_ref[...] = jnp.concatenate([spread(scale_ref[...]), spread(shift_ref[...])], 0)


def section_body(me_ref, x_ref, w_ref, affine_ref, o_ref, *sent):
    rows, channels, width = x_ref.shape
    skip = channels - w_ref.shape[1]
    for s in ORDER:
        first = HS * lax.bitwise_xor(me_ref[0], s)
        for r in range(HS):
            lin = dot(w_ref[...], x_ref[first + r, skip:, :])
            value = jnp.maximum(affine_ref[:, 0:1] * lin + affine_ref[:, 1:2], 0.0).astype(BF16)
            o_ref[first + r] = value
            sent[s][r * CF : (r + 1) * CF] = value
    place = lax.broadcasted_iota(jnp.int32, (2 * rows, width), 0)
    lane = lax.broadcasted_iota(jnp.int32, (2 * rows, width), 1)
    ends = jnp.zeros((2 * rows, channels), F32)
    for h in range(rows):
        pick = ((place == h) & (lane == 0)) | ((place == rows + h) & (lane == width - 1))
        ends = ends + dot_nt(pick.astype(F32).astype(BF16), x_ref[h])
    ends = ends.astype(BF16)
    sent[1][LANES:] = ends
    sent[3][LANES:] = ends


def halo_body(me_ref, x_ref, next_ref, last_ref, down_ref, up_ref, side_ref):
    rows, channels, _ = x_ref.shape
    me = me_ref[0]
    odd = lax.rem(me, 2).astype(F32)
    near = next_ref[LANES:].astype(F32)
    far = last_ref[LANES:].astype(F32)
    even = 1.0 - odd
    left = (odd * near[rows:] + even * far[rows:]) * jnp.where(me > 0, 1.0, 0.0)
    right = (odd * far[:rows] + even * near[:rows]) * jnp.where(me < COLS - 1, 1.0, 0.0)
    sides = jnp.concatenate([left, right], 0).astype(BF16)
    side_ref[...] = sides
    down_ref[:channels] = x_ref[rows - 1]
    down_ref[channels:] = sides
    up_ref[:channels] = x_ref[0]
    up_ref[channels:] = sides


def width_near_body(me_ref, t_ref, near_ref, next_ref, o_ref):
    me = me_ref[0]
    o_ref[...] = dot_nt(t_ref[me], near_ref[...]) + dot_nt(t_ref[lax.bitwise_xor(me, 1)], next_ref[:LANES])


def width_far_body(me_ref, t_ref, part_ref, far_ref, last_ref, o_ref, held, sem):
    me = me_ref[0]
    size = o_ref.shape[0] // 4
    copies = []
    for i in range(4):
        span = pl.ds(i * size, size)
        total = part_ref[span] + dot_nt(t_ref[lax.bitwise_xor(me, 2), span], far_ref[...])
        held[span] = (total + dot_nt(t_ref[lax.bitwise_xor(me, 3), span], last_ref[:LANES])).astype(BF16)
        copies.append(pltpu.make_async_copy(held.at[span], o_ref.at[span], sem.at[i]))
        copies[-1].start()
    for copy in copies:
        copy.wait()


def widen(d):
    gap = jnp.zeros((d.shape[0], LANE - CF), d.dtype)
    return jnp.concatenate(sum([[d[:, CF * r : CF * r + CF], gap] for r in range(HS)], []), 1)


def narrow(d):
    return jnp.concatenate([d[:, LANE * r : LANE * r + CF] for r in range(HS)], 1)


def turns(real, imag):
    s02r, d02r, s13r, d13r = real[0] + real[2], real[0] - real[2], real[1] + real[3], real[1] - real[3]
    s02i, d02i, s13i, d13i = imag[0] + imag[2], imag[0] - imag[2], imag[1] + imag[3], imag[1] - imag[3]
    return (
        (s02r + s13r, s02i + s13i),
        (d02r + d13i, d02i - d13r),
        (s02r - s13r, s02i - s13i),
        (d02r - d13i, d02i + d13r),
    )


def middle_body(z_ref, fwd_ref, inv_ref, d_ref, tw_ref, w_ref, affine_ref, o_ref, fwd, inv, held, sem):
    z = z_ref[0]
    step = fwd.shape[0] // 3
    loads = []
    for i in range(3):
        span = pl.ds(i * step, step)
        loads.append(pltpu.make_async_copy(fwd_ref.at[z, span], fwd.at[span], sem.at[i]))
    quarter = inv.shape[0] // 4
    for i in range(4):
        span = pl.ds(i * quarter, quarter)
        loads.append(pltpu.make_async_copy(inv_ref.at[z, span], inv.at[span], sem.at[3 + i]))
    for load in loads:
        load.start()
    d = widen(d_ref[...])
    parts = []
    for i in range(3):
        loads[i].wait()
        parts.append(dot(fwd[pl.ds(i * step, step)], d))
    u = jnp.concatenate(parts, 0)
    twr, twi = tw_ref[0], tw_ref[1]
    rows = []
    for f in range(NF + 1):
        ur = u[2 * f * MID : (2 * f + 1) * MID]
        ui = u[(2 * f + 1) * MID : (2 * f + 2) * MID]
        vr = ur * twr - ui * twi
        vi = ur * twi + ui * twr
        groups = [slice(LANE * r, LANE * r + LANE) for r in range(HS)]
        for real, imag in turns([vr[:, g] for g in groups], [vi[:, g] for g in groups]):
            rows.append(jnp.concatenate([real, imag], 1).astype(BF16))
    mixed = dot(jnp.concatenate(rows, 0), w_ref[...])
    active = jnp.maximum(affine_ref[0:1] * mixed + affine_ref[1:2], 0.0)
    rows = []
    for f in range(NF + 1):
        own = [active[(HS * f + j) * MID : (HS * f + j + 1) * MID] for j in range(HS)]
        own = [own[j] for j in (0, 3, 2, 1)]
        turned = turns([v[:, :LANE] for v in own], [v[:, LANE:] for v in own])
        br = jnp.concatenate([v[0] for v in turned], 1)
        bi = jnp.concatenate([v[1] for v in turned], 1)
        rows.append((br * twr + bi * twi).astype(BF16))
        rows.append((bi * twr - br * twi).astype(BF16))
    back = jnp.concatenate(rows, 0)
    stores = []
    for i in range(4):
        span = pl.ds(i * quarter, quarter)
        loads[3 + i].wait()
        held[span] = narrow(dot(inv[span], back).astype(BF16))
        stores.append(pltpu.make_async_copy(held.at[span], o_ref.at[span], sem.at[7 + i]))
        stores[-1].start()
    for store in stores:
        store.wait()


def inverse_body(pair, me_ref, t_ref, d_ref, a_ref, b_ref):
    for s, o_ref in zip(pair, (a_ref, b_ref)):
        o_ref[...] = dot(t_ref[lax.bitwise_xor(me_ref[0], s)], d_ref[...]).astype(BF16)


def conv_body(x_ref, above_ref, below_ref, side_ref, wl_ref, wg_ref, wm_ref, sec_ref, o_ref, cols, edge):
    cl = wl_ref.shape[1] // 3
    cg = wg_ref.shape[1] // 3
    rows, channels, width = x_ref.shape
    cols[...] = jnp.zeros_like(cols)
    for side in range(2):
        own = pl.ds(side * rows, rows)
        held = pl.ds(channels + side * rows, rows)
        cols[side, 0:rows] = above_ref[held]
        cols[side, rows : 2 * rows] = side_ref[own]
        cols[side, 2 * rows : 3 * rows] = below_ref[held]
        dx = 2 * side
        total = None
        for dy in range(3):
            taps = wl_ref[dx * channels : (dx + 1) * channels, dy * cl : (dy + 1) * cl]
            term = dot_nt(taps, cols[side, :, :cl])
            taps = wg_ref[dx * cl : (dx + 1) * cl, dy * cg : (dy + 1) * cg]
            extra = dot_nt(taps, cols[side, :, cl:])
            term = jnp.concatenate([term[:cl] + extra, term[cl:]], 0)
            term = pltpu.roll(term, LANE - (rows - 1 + dy), 1)
            total = term if total is None else total + term
        edge[side] = total
    lane = lax.broadcasted_iota(jnp.int32, (channels, LANE), 1)

    def emit(h, three):
        local = jnp.concatenate([row[:cl] for row in three], 0)
        other = jnp.concatenate([row[cl:] for row in three], 0)
        parts = []
        for dx in range(3):
            yl = dot(wl_ref[dx * channels : (dx + 1) * channels], local)
            yg = dot(wg_ref[dx * cl : (dx + 1) * cl], other)
            parts.append(jnp.concatenate([yl[:cl] + yg, yl[cl:]], 0))
        before = pltpu.roll(parts[0], 1, 1)
        behind = pltpu.roll(parts[2], width - 1, 1)
        first = pltpu.roll(edge[0], lax.rem(LANE - h, LANE), 1)
        final = pltpu.roll(edge[1], LANE - 1 - h, 1)
        before = jnp.concatenate([jnp.where(lane == 0, first, before[:, :LANE]), before[:, LANE:]], 1)
        behind = jnp.concatenate([behind[:, : width - LANE], jnp.where(lane == LANE - 1, final, behind[:, width - LANE :])], 1)
        acc = parts[1] + before + behind
        mix = dot(wm_ref[...], sec_ref[h])
        o_ref[h, :cl] = acc[:cl].astype(BF16)
        o_ref[h, cl:] = (acc[cl:] + mix).astype(BF16)

    emit(0, [above_ref[:channels], x_ref[0], x_ref[1]])

    def step(h, carry):
        emit(h, [x_ref[h - 1], x_ref[h], x_ref[h + 1]])
        return carry

    lax.fori_loop(1, rows - 1, step, 0)
    emit(rows - 1, [x_ref[rows - 2], x_ref[rows - 1], below_ref[:channels]])


def final_body(pair, me_ref, x_ref, pre_ref, a_ref, b_ref, w_ref, affine_ref, *outs):
    o_ref = outs[-1]
    count = w_ref.shape[0] // HS
    low = x_ref.shape[1] - count
    for s, f_ref in zip(pair, (a_ref, b_ref)):
        first = HS * lax.bitwise_xor(me_ref[0], s)
        res = dot_nt(w_ref[...], f_ref[...])
        for r in range(HS):
            pre = pre_ref[first + r].astype(F32)
            pre = jnp.concatenate([pre[:low], pre[low:] + res[r * count : (r + 1) * count]], 0)
            act = jnp.maximum(affine_ref[:, 0:1] * pre + affine_ref[:, 1:2], 0.0)
            o_ref[first + r] = (x_ref[first + r].astype(F32) + act).astype(BF16)


def shift_along(block, axis, step):
    count = lax.axis_size(axis)
    pairs = [(i, i + step) for i in range(count) if 0 <= i + step < count]
    return lax.ppermute(block, axis, pairs)


def swap(block, s):
    return lax.ppermute(block, "col", [(i, i ^ s) for i in range(COLS)])


def after(value, *others):
    return lax.optimization_barrier((value,) + others)


def per_device(
    image,
    from_local,
    from_global,
    section_weight,
    section_scale,
    section_shift,
    fourier_weight,
    fourier_scale,
    fourier_shift,
    mix_weight,
    out_scale,
    out_shift,
):
    channels, rows, width = image.shape
    cl = from_local.shape[2]
    cg = channels - cl
    me = lax.axis_index("col").astype(jnp.int32).reshape(1)
    z = jnp.logical_and(lax.axis_index("row") == 0, lax.axis_index("col") == 0).astype(jnp.int32).reshape(1)
    shape = jax.ShapeDtypeStruct

    x = jnp.transpose(image, (1, 0, 2))
    block, block_ends = shape((LANES, width), BF16), shape((LANES + 2 * rows, width), BF16)
    section, near, other, far, last = call(
        section_body,
        (shape((rows, CF, width), BF16), block, block_ends, block, block_ends),
        (me, x, section_weight, jnp.stack([section_scale, section_shift], 1)),
        smem=(0,),
    )
    far, last, other = swap(far, 2), swap(last, 3), swap(other, 1)

    wl, wg, mix4, mixer, affine = call(
        prepare_body,
        (
            shape((3 * channels, 3 * cl), BF16),
            shape((3 * cl, 3 * cg), BF16),
            shape((HS * cg, LANES), BF16),
            shape((2 * LANE, 2 * LANE), BF16),
            shape((2, 2 * LANE), F32),
        ),
        (
            jnp.transpose(from_local, (0, 2, 1)),
            from_global,
            mix_weight,
            fourier_weight,
            fourier_scale[None],
            fourier_shift[None],
        ),
    )

    fwd_w, inv_w = (jnp.asarray(t) for t in width_tables())
    part = call(width_near_body, shape((W, LANES), F32), (me, fwd_w, near, other), smem=(0,))
    spectra = call(
        width_far_body,
        shape((W, LANES), BF16),
        (me, fwd_w, part, far, last),
        smem=(0,),
        hbm_out=True,
        scratch_shapes=[pltpu.VMEM((W, LANES), BF16), pltpu.SemaphoreType.DMA((4,))],
    )
    down, up, sides = call(
        halo_body,
        (shape((channels + 2 * rows, width), BF16),) * 2 + (shape((2 * rows, channels), BF16),),
        (me, x, other, last),
        smem=(0,),
        flops=10**6,
    )
    spectra, down, up = after(spectra, down, up)
    spectra = lax.all_to_all(
        spectra.reshape(PEERS, 2 * NF, LANES), ("row", "col"), split_axis=0, concat_axis=0, tiled=True
    ).reshape(W, LANES)
    above, below = shift_along(down, "row", 1), shift_along(up, "row", -1)
    spectra, above, below = after(spectra, above, below)

    fwd_h, inv_h = (jnp.asarray(t) for t in height_tables())
    size, wide = 2 * NF * MID, 2 * (NF + 1) * MID
    returned = call(
        middle_body,
        shape((W, LANES), BF16),
        (z, fwd_h, inv_h, spectra, jnp.asarray(twiddles()), mixer, affine),
        smem=(0,),
        hbm=(1, 2),
        hbm_out=True,
        limit=32,
        scratch_shapes=[
            pltpu.VMEM((wide, size), BF16),
            pltpu.VMEM((size, wide), BF16),
            pltpu.VMEM((W, LANES), BF16),
            pltpu.SemaphoreType.DMA((11,)),
        ],
    )
    returned, above, below = after(returned, above, below)
    returned = lax.all_to_all(
        returned.reshape(PEERS, 2 * NF, LANES), ("row", "col"), split_axis=0, concat_axis=0, tiled=True
    ).reshape(W, LANES)
    pre = call(
        conv_body,
        shape((rows, channels, width), BF16),
        (x, above, below, sides, wl, wg, mix_weight, section),
        flops=3 * 10**9,
        scratch_shapes=[pltpu.VMEM((2, LANE, channels), BF16), pltpu.VMEM((2, channels, LANE), F32)],
    )
    returned, pre = after(returned, pre)

    piece = shape((width, LANES), BF16)
    out_affine = jnp.stack([out_scale, out_shift], 1)
    far, last = call(functools.partial(inverse_body, (2, 3)), (piece, piece), (me, inv_w, returned), smem=(0,))
    far, last = swap(far, 2), swap(last, 3)
    other, near = call(functools.partial(inverse_body, (1, 0)), (piece, piece), (me, inv_w, returned), smem=(0,))
    other = swap(other, 1)
    whole = shape((rows, channels, width), BF16)
    half = call(
        functools.partial(final_body, (0, 1)), whole, (me, x, pre, near, other, mix4, out_affine), smem=(0,)
    )
    result = call(
        functools.partial(final_body, (2, 3)),
        whole,
        (me, x, pre, far, last, mix4, out_affine, half),
        smem=(0,),
        input_output_aliases={7: 0},
    )
    return jnp.transpose(result, (1, 0, 2))


def solution(mesh):
    return jax.shard_map(
        per_device,
        mesh=mesh,
        in_specs=(P("img", "row", "col"), P(), P(), P(), P(), P(), P(), P(), P(), P(), P(), P()),
        out_specs=P("img", "row", "col"),
        check_vma=False,
    )
```

time: 133 us -> 95.8 us (0.72)
  blocking collectives: 14.9 us -> 0 us
  local copies, waits for them, and re-layouts: 28.6 us -> 21.2 us
  other arithmetic: 7.74 us -> 0.69 us
  Pallas kernels: 29.2 us -> 25.8 us
  waiting for transfers between devices: 23.1 us -> 19.9 us
    all_to_all x1 -> x0, blocking collectives: 14.9 us -> none  [per_device(): lax.all_to_all(section.reshape(COLS, HS * CF, width), 'col', split_axis=0...]
    ppermute x0 -> x6, waiting for transfers between devices: none -> 12.7 us  [swap(): return lax.ppermute(block, 'col', [(i, i ^ s) for i in range(COLS)])]
    all_to_all x1, waiting for transfers between devices: 12.6 us -> 0.01 us  [per_device(): lax.all_to_all(spectra.reshape(PEERS, 2 * NF, LANES), ('row', 'col'), spl...]
    broadcast_in_dim x7 -> x0, local copies, waits for them, and re-layouts: 6.15 us -> none  [the longest x1 2.18 us: per_device(): right[:, :, None]]
    unnamed x60 -> x49, local copies, waits for them, and re-layouts: 12.9 us -> 18.5 us
    ppermute x4 -> x2, waiting for transfers between devices: 10.5 us -> 5.41 us  [shift_along(): return lax.ppermute(block, axis, pairs)]
    ppermute x0 -> x6, starting transfers between devices: none -> 4.97 us  [swap(): return lax.ppermute(block, 'col', [(i, i ^ s) for i in range(COLS)])]
    ppermute x4 -> x2, starting transfers between devices: 10.2 us -> 5.25 us  [shift_along(): return lax.ppermute(block, axis, pairs)]
  transfers between devices with their start and end apart: 7 -> 10, of which waited for: 3 -> 7; matrix products, arithmetic and copies ran while one was open for 16% -> 0% of each run, Pallas kernels for 9% -> 15%
where the time goes in v1:
time: 95.8 us; the launch traced here: 95 us
  starting transfers between devices  27.2 us (28%)
  Pallas kernels  25.8 us (27%)
  local copies, waits for them, and re-layouts  21.2 us (22%)
  waiting for transfers between devices  19.9 us (21%)
    pallas_call x11, Pallas kernels, call(): pl.pallas_call(body, out_shape=jax.tree.map(lambda s: out_place(s.shape,...  25.8 us
    unnamed x49, local copies, waits for them, and re-layouts  18.5 us
    ppermute x6, waiting for transfers between devices, swap(): return lax.ppermute(block, 'col', [(i, i ^ s) for i in range(COLS)])  12.7 us
    all_to_all x1, starting transfers between devices, per_device(): lax.all_to_all(spectra.reshape(PEERS, 2 * NF, LANES), ('row', 'col'), spl...  10.4 us
    all_to_all x1, starting transfers between devices, per_device(): lax.all_to_all(returned.reshape(PEERS, 2 * NF, LANES), ('row', 'col'), sp...  6.52 us
    ppermute x2, waiting for transfers between devices, shift_along(): return lax.ppermute(block, axis, pairs)  5.41 us
    ppermute x2, starting transfers between devices, shift_along(): return lax.ppermute(block, axis, pairs)  5.25 us
    ppermute x6, starting transfers between devices, swap(): return lax.ppermute(block, 'col', [(i, i ^ s) for i in range(COLS)])  4.97 us
  transfers between devices with their start and end apart: 10, of which 7 were waited for; matrix products, arithmetic and copies ran while one was open for 0% of the time, Pallas kernels for 15%

profile of v1, /device:TPU:1, one launch (start us, length us, event | category | flops | bytes accessed | tf_op | source)
XLA Modules:
  0.0 95.0 jit_solution(8005493477881223999)
XLA Ops:
  0.8 2.3 %copy.35 = bf16[256,16,256]{2,0,1:T(8,128)(2,1)S(1)} copy(bf16[256,16,256]{2,1,0:T(8,128)(2,1)} %param.17) | data formatting | bytes 4194304 | tf_op args[0]
  5.0 1.4 %collective-permute-start = (bf16[416,256]{1,0:T(8,128)(2,1)S(1)}, bf16[416,256]{1,0:T(8,128)(2,1)S(1)}, u32[]{:S(2)}, u32[]{:S(2)}) collective-permute-start(bf16[416,256]{1,0:T(8,128)(2,1)S(1)} %get-tuple-element.34), channel_id=1, source_target_pairs={{0,1},{1,0},{2,3},{3,2},{4,5},{5,4},{6,7},{7,6},{8,9},{9,8},{10,11... | collective-permute-start | bytes 638984 | tf_op jit(solution)/shard_map/ppermute | solution.py:337
  6.4 1.3 %collective-permute-start.2 = (bf16[416,256]{1,0:T(8,128)(2,1)S(1)}, bf16[416,256]{1,0:T(8,128)(2,1)S(1)}, u32[]{:S(2)}, u32[]{:S(2)}) collective-permute-start(bf16[416,256]{1,0:T(8,128)(2,1)S(1)} %get-tuple-element.36), channel_id=1, source_target_pairs={{0,3},{1,2},{2,1},{3,0},{4,7},{5,6},{6,5},{7,4},{8,11},{9,10},{10,... | collective-permute-start | bytes 638984 | tf_op jit(solution)/shard_map/ppermute | solution.py:337
  7.8 6.1 %collective-permute-done.2.last_ref = bf16[416,256]{1,0:T(8,128)(2,1)S(1)} collective-permute-done((bf16[416,256]{1,0:T(8,128)(2,1)S(1)}, bf16[416,256]{1,0:T(8,128)(2,1)S(1)}, u32[]{:S(2)}, u32[]{:S(2)}) %collective-permute-start.2) | collective-permute-done | bytes 213024 | tf_op jit(solution)/shard_map/ppermute | solution.py:337
  15.4 1.8 %collective-permute-done.1.far_ref = bf16[384,256]{1,0:T(8,128)(2,1)S(1)} collective-permute-done((bf16[384,256]{1,0:T(8,128)(2,1)S(1)}, bf16[384,256]{1,0:T(8,128)(2,1)S(1)}, u32[]{:S(2)}, u32[]{:S(2)}) %collective-permute-start.1) | collective-permute-done | bytes 196640 | tf_op jit(solution)/shard_map/ppermute | solution.py:337
  17.2 1.4 %shard_map.165 = bf16[1024,384]{1,0:T(8,128)(2,1)} custom-call(s32[1]{0:T(128)} %bitcast.me_ref, bf16[4,1024,256]{2,1,0:T(8,128)(2,1)S(1)} %copy-done, f32[1024,384]{1,0:T(8,128)S(1)} %shard_map.164.part_ref, bf16[384,256]{1,0:T(8,128)(2,1)S(1)} %collective-permute-done.1.far_ref, bf16[416,256]{1,0:T(8,128)(2,1)S(1)} %collective-permute-done.2.last_ref), custom_call_target="tpu_custom_call" | custom-call | flops 1000000000 | bytes 4194304 | tf_op jit(solution)/shard_map/pallas_call | solution.py:99
  18.6 10.4 %all-to-all-start = ((bf16[64,16,384]{2,1,0:T(8,128)(2,1)}), bf16[64,16,384]{2,1,0:T(8,128)(2,1)S(1)}, u32[]{:S(2)}, u32[]{:S(2)}) async-start(bf16[64,16,384]{2,1,0:T(8,128)(2,1)} %bitcast.29), calls=%async_computation | async-start | bytes 1572864 | tf_op jit(solution)/shard_map/all_to_all | solution.py:412
  29.1 4.0 %collective-permute-start.3 = (bf16[288,256]{1,0:T(8,128)(2,1)}, bf16[288,256]{1,0:T(8,128)(2,1)}, u32[]{:S(2)}, u32[]{:S(2)}) collective-permute-start(bf16[288,256]{1,0:T(8,128)(2,1)} %get-tuple-element.40), channel_id=1, source_target_pairs={{0,4},{4,8},{8,12},{12,16},{16,20},{20,24},{24,28},{28,32},{32,36}... | collective-permute-start | bytes 442376 | tf_op jit(solution)/shard_map/ppermute | solution.py:333
  33.0 1.3 %collective-permute-start.4 = (bf16[288,256]{1,0:T(8,128)(2,1)}, bf16[288,256]{1,0:T(8,128)(2,1)}, u32[]{:S(2)}, u32[]{:S(2)}) collective-permute-start(bf16[288,256]{1,0:T(8,128)(2,1)} %get-tuple-element.41), channel_id=1, source_target_pairs={{4,0},{8,4},{12,8},{16,12},{20,16},{24,20},{28,24},{32,28},{36,32}... | collective-permute-start | bytes 442376 | tf_op jit(solution)/shard_map/ppermute | solution.py:333
  39.6 3.0 %collective-permute-done.3.above_ref = bf16[288,256]{1,0:T(8,128)(2,1)} collective-permute-done((bf16[288,256]{1,0:T(8,128)(2,1)}, bf16[288,256]{1,0:T(8,128)(2,1)}, u32[]{:S(2)}, u32[]{:S(2)}) %collective-permute-start.3) | collective-permute-done | bytes 147488 | tf_op jit(solution)/shard_map/ppermute | solution.py:333
  42.6 2.4 %collective-permute-done.4.below_ref = bf16[288,256]{1,0:T(8,128)(2,1)} collective-permute-done((bf16[288,256]{1,0:T(8,128)(2,1)}, bf16[288,256]{1,0:T(8,128)(2,1)}, u32[]{:S(2)}, u32[]{:S(2)}) %collective-permute-start.4) | collective-permute-done | bytes 147488 | tf_op jit(solution)/shard_map/ppermute | solution.py:333
  46.9 7.4 %shard_map.168 = bf16[1024,384]{1,0:T(8,128)(2,1)} custom-call(s32[1]{0:T(128)} %bitcast.2.z_ref, bf16[2,1152,1024]{2,1,0:T(8,128)(2,1)} %constant.23.clone.fwd_ref, bf16[2,1024,1152]{2,1,0:T(8,128)(2,1)} %constant.24.clone.inv_ref, bf16[1024,384]{1,0:T(8,128)(2,1)S(1)} %bitcast.23, f32[2,64,512]{2,1,0:T(8,128)S(1)} %copy-done.3, ...), custom_call_target="tpu_custom_call" | custom-call | flops 1000000000 | bytes 4194304 | tf_op jit(solution)/shard_map/pallas_call | solution.py:99
  54.3 6.5 %all-to-all-start.1 = ((bf16[64,16,384]{2,1,0:T(8,128)(2,1)}), bf16[64,16,384]{2,1,0:T(8,128)(2,1)S(1)}, u32[]{:S(2)}, u32[]{:S(2)}) async-start(bf16[64,16,384]{2,1,0:T(8,128)(2,1)} %bitcast.30), calls=%async_computation.1 | async-start | bytes 1572864 | tf_op jit(solution)/shard_map/all_to_all | solution.py:436
  60.9 1.1 %copy-done.17 = bf16[16,96,256]{2,1,0:T(8,128)(2,1)S(1)} copy-done((bf16[16,96,256]{2,1,0:T(8,128)(2,1)S(1)}, bf16[16,96,256]{2,1,0:T(8,128)(2,1)}, u32[]{:S(2)}) %copy-start.17) | copy-done | bytes 786456
  63.9 9.0 %shard_map.169.pre_ref = bf16[16,256,256]{2,1,0:T(8,128)(2,1)S(1)} custom-call(bf16[16,256,256]{2,1,0:T(8,128)(2,1)S(1)} %bitcast.19, bf16[288,256]{1,0:T(8,128)(2,1)} %collective-permute-done.3.above_ref, bf16[288,256]{1,0:T(8,128)(2,1)} %collective-permute-done.4.below_ref, bf16[32,256]{1,0:T(8,128)(2,1)S(1)} %get-tuple-element.50.side_ref, ...), custom_call_target="tpu_custom_call" | custom-call | flops 3000000000 | bytes 4194304 | tf_op jit(solution)/shard_map/pallas_call | solution.py:99
  72.9 1.3 %copy-done.1 = bf16[16,256,256]{2,1,0:T(8,128)(2,1)} copy-done((bf16[16,256,256]{2,1,0:T(8,128)(2,1)}, bf16[16,256,256]{2,1,0:T(8,128)(2,1)S(1)}, u32[]{:S(2)}) %copy-start.1) | copy-done | bytes 2097176
  74.2 1.8 %all-to-all-done.1 = bf16[64,16,384]{2,1,0:T(8,128)(2,1)S(1)} async-done(((bf16[64,16,384]{2,1,0:T(8,128)(2,1)}), bf16[64,16,384]{2,1,0:T(8,128)(2,1)S(1)}, u32[]{:S(2)}, u32[]{:S(2)}) %all-to-all-start.1) | async-done | bytes 786464 | tf_op jit(solution)/shard_map/all_to_all | solution.py:436
  76.0 1.6 %copy-done.15 = bf16[4,256,1024]{2,1,0:T(8,128)(2,1)S(1)} copy-done((bf16[4,256,1024]{2,1,0:T(8,128)(2,1)S(1)}, bf16[4,256,1024]{2,1,0:T(8,128)(2,1)}, u32[]{:S(2)}) %copy-start.15) | copy-done | bytes 2097176
  79.1 1.4 %shard_map.170 = (bf16[256,384]{1,0:T(8,128)(2,1)}, bf16[256,384]{1,0:T(8,128)(2,1)}) custom-call(s32[1]{0:T(128)} %bitcast.me_ref, bf16[4,256,1024]{2,1,0:T(8,128)(2,1)S(1)} %copy-done.15, bf16[1024,384]{1,0:T(8,128)(2,1)S(1)} %bitcast.25), custom_call_target="tpu_custom_call" | custom-call | flops 1000000000 | bytes 4194304 | tf_op jit(solution)/shard_map/pallas_call | solution.py:99
  80.5 1.7 %collective-permute-start.6 = (bf16[256,384]{1,0:T(8,128)(2,1)}, bf16[256,384]{1,0:T(8,128)(2,1)S(1)}, u32[]{:S(2)}, u32[]{:S(2)}) collective-permute-start(bf16[256,384]{1,0:T(8,128)(2,1)} %get-tuple-element.57), channel_id=1, source_target_pairs={{0,3},{1,2},{2,1},{3,0},{4,7},{5,6},{6,5},{7,4},{8,11},{9,10},{10,... | collective-permute-start | bytes 589832 | tf_op jit(solution)/shard_map/ppermute | solution.py:337
  82.5 1.6 %copy-done.2 = bf16[16,256,256]{2,1,0:T(8,128)(2,1)S(1)} copy-done((bf16[16,256,256]{2,1,0:T(8,128)(2,1)S(1)}, bf16[16,256,256]{2,1,0:T(8,128)(2,1)}, u32[]{:S(2)}) %copy-start.2) | copy-done | bytes 2097176
  85.0 1.8 %shard_map.172.outs_0_ = bf16[16,256,256]{2,1,0:T(8,128)(2,1)S(1)} custom-call(s32[1]{0:T(128)} %bitcast.me_ref, bf16[16,256,256]{2,1,0:T(8,128)(2,1)S(1)} %bitcast.20, bf16[16,256,256]{2,1,0:T(8,128)(2,1)S(1)} %copy-done.2, bf16[256,384]{1,0:T(8,128)(2,1)S(1)} %copy-done.5, bf16[256,384]{1,0:T(8,128)(2,1)} %collective-permute-done.7.b_ref, ...), custom_call_target="tpu_custom_call" | custom-call | flops 1000000000 | bytes 4194304 | tf_op jit(solution)/shard_map/pallas_call | solution.py:99
  87.2 4.4 %collective-permute-done.6.b_ref = bf16[256,384]{1,0:T(8,128)(2,1)S(1)} collective-permute-done((bf16[256,384]{1,0:T(8,128)(2,1)}, bf16[256,384]{1,0:T(8,128)(2,1)S(1)}, u32[]{:S(2)}, u32[]{:S(2)}) %collective-permute-start.6) | collective-permute-done | bytes 196640 | tf_op jit(solution)/shard_map/ppermute | solution.py:337
  92.5 2.5 %copy.33 = bf16[256,16,256]{2,1,0:T(8,128)(2,1)} copy(bf16[256,16,256]{2,0,1:T(8,128)(2,1)S(1)} %bitcast.22) | data formatting | bytes 4194304 | tf_op jit(solution)/shard_map/transpose | solution.py:465
  (61 shorter events, 17.2 us)
Async XLA Ops:
  0.8 2.3 %copy-start.11 = (bf16[96,192]{1,0:T(8,128)(2,1)S(1)}, bf16[96,192]{1,0:T(8,128)(2,1)}, u32[]{:S(2)}) copy-start(bf16[96,192]{1,0:T(8,128)(2,1)} %w_ref.1) | copy-start | bytes 110596
  5.0 9.7 %copy-start = (bf16[4,1024,256]{2,1,0:T(8,128)(2,1)S(1)}, bf16[4,1024,256]{2,1,0:T(8,128)(2,1)}, u32[]{:S(2)}) copy-start(bf16[4,1024,256]{2,1,0:T(8,128)(2,1)} %constant.21.clone.t_ref) | copy-start | bytes 6291460
  5.0 2.8 %collective-permute-start = (bf16[416,256]{1,0:T(8,128)(2,1)S(1)}, bf16[416,256]{1,0:T(8,128)(2,1)S(1)}, u32[]{:S(2)}, u32[]{:S(2)}) collective-permute-start(bf16[416,256]{1,0:T(8,128)(2,1)S(1)} %get-tuple-element.34), channel_id=1, source_target_pairs={{0,1},{1,0},{2,3},{3,2},{4,5},{5,4},{6,7},{7,6},{8,9},{9,8},{10,11... | collective-permute-start | bytes 638984 | tf_op jit(solution)/shard_map/ppermute | solution.py:337
  6.4 7.5 %collective-permute-start.2 = (bf16[416,256]{1,0:T(8,128)(2,1)S(1)}, bf16[416,256]{1,0:T(8,128)(2,1)S(1)}, u32[]{:S(2)}, u32[]{:S(2)}) collective-permute-start(bf16[416,256]{1,0:T(8,128)(2,1)S(1)} %get-tuple-element.36), channel_id=1, source_target_pairs={{0,3},{1,2},{2,1},{3,0},{4,7},{5,6},{6,5},{7,4},{8,11},{9,10},{10,... | collective-permute-start | bytes 638984 | tf_op jit(solution)/shard_map/ppermute | solution.py:337
  7.7 9.5 %collective-permute-start.1 = (bf16[384,256]{1,0:T(8,128)(2,1)S(1)}, bf16[384,256]{1,0:T(8,128)(2,1)S(1)}, u32[]{:S(2)}, u32[]{:S(2)}) collective-permute-start(bf16[384,256]{1,0:T(8,128)(2,1)S(1)} %get-tuple-element.35), channel_id=1, source_target_pairs={{0,2},{1,3},{2,0},{3,1},{4,6},{5,7},{6,4},{7,5},{8,10},{9,11},{10,... | collective-permute-start | bytes 589832 | tf_op jit(solution)/shard_map/ppermute | solution.py:337
  15.4 19.0 %copy-start.12 = (bf16[192,96]{1,0:T(8,128)(2,1)S(1)}, bf16[192,96]{1,0:T(8,128)(2,1)}, u32[]{:S(2)}) copy-start(bf16[192,96]{1,0:T(8,128)(2,1)} %wm_ref.1) | copy-start | bytes 110596
  15.4 19.0 %copy-start.13 = (f32[192]{0:T(256)S(1)}, f32[192]{0:T(256)}, u32[]{:S(2)}) copy-start(f32[192]{0:T(256)} %param.24) | copy-start | bytes 2308
  15.4 19.0 %copy-start.14 = (f32[192]{0:T(256)S(1)}, f32[192]{0:T(256)}, u32[]{:S(2)}) copy-start(f32[192]{0:T(256)} %param.25) | copy-start | bytes 2308
  18.6 26.4 %all-to-all-start = ((bf16[64,16,384]{2,1,0:T(8,128)(2,1)}), bf16[64,16,384]{2,1,0:T(8,128)(2,1)S(1)}, u32[]{:S(2)}, u32[]{:S(2)}) async-start(bf16[64,16,384]{2,1,0:T(8,128)(2,1)} %bitcast.29), calls=%async_computation | async-start | bytes 1572864 | tf_op jit(solution)/shard_map/all_to_all | solution.py:412
  29.1 13.5 %collective-permute-start.3 = (bf16[288,256]{1,0:T(8,128)(2,1)}, bf16[288,256]{1,0:T(8,128)(2,1)}, u32[]{:S(2)}, u32[]{:S(2)}) collective-permute-start(bf16[288,256]{1,0:T(8,128)(2,1)} %get-tuple-element.40), channel_id=1, source_target_pairs={{0,4},{4,8},{8,12},{12,16},{16,20},{20,24},{24,28},{28,32},{32,36}... | collective-permute-start | bytes 442376 | tf_op jit(solution)/shard_map/ppermute | solution.py:333
  33.0 12.0 %collective-permute-start.4 = (bf16[288,256]{1,0:T(8,128)(2,1)}, bf16[288,256]{1,0:T(8,128)(2,1)}, u32[]{:S(2)}, u32[]{:S(2)}) collective-permute-start(bf16[288,256]{1,0:T(8,128)(2,1)} %get-tuple-element.41), channel_id=1, source_target_pairs={{4,0},{8,4},{12,8},{16,12},{20,16},{24,20},{28,24},{32,28},{36,32}... | collective-permute-start | bytes 442376 | tf_op jit(solution)/shard_map/ppermute | solution.py:333
  34.4 1.0 %copy-start.8 = (bf16[9,256,64]{1,2,0:T(8,128)(2,1)S(1)}, bf16[9,256,64]{1,2,0:T(8,128)(2,1)}, u32[]{:S(2)}) copy-start(bf16[9,256,64]{1,2,0:T(8,128)(2,1)} %param.18) | copy-start | bytes 884740
  54.3 21.7 %all-to-all-start.1 = ((bf16[64,16,384]{2,1,0:T(8,128)(2,1)}), bf16[64,16,384]{2,1,0:T(8,128)(2,1)S(1)}, u32[]{:S(2)}, u32[]{:S(2)}) async-start(bf16[64,16,384]{2,1,0:T(8,128)(2,1)} %bitcast.30), calls=%async_computation.1 | async-start | bytes 1572864 | tf_op jit(solution)/shard_map/all_to_all | solution.py:436
  60.9 1.1 %copy-start.17 = (bf16[16,96,256]{2,1,0:T(8,128)(2,1)S(1)}, bf16[16,96,256]{2,1,0:T(8,128)(2,1)}, u32[]{:S(2)}) copy-start(bf16[16,96,256]{2,1,0:T(8,128)(2,1)} %copy-done.16) | copy-start | bytes 2359300
  62.0 1.0 %copy-start.19 = (bf16[768,192]{1,0:T(8,128)(2,1)S(1)}, bf16[768,192]{1,0:T(8,128)(2,1)}, u32[]{:S(2)}) copy-start(bf16[768,192]{1,0:T(8,128)(2,1)} %copy-done.18) | copy-start | bytes 884740
  72.9 1.3 %copy-start.1 = (bf16[16,256,256]{2,1,0:T(8,128)(2,1)}, bf16[16,256,256]{2,1,0:T(8,128)(2,1)S(1)}, u32[]{:S(2)}) copy-start(bf16[16,256,256]{2,1,0:T(8,128)(2,1)S(1)} %shard_map.169.pre_ref) | copy-start | bytes 6291460
  76.0 1.6 %copy-start.15 = (bf16[4,256,1024]{2,1,0:T(8,128)(2,1)S(1)}, bf16[4,256,1024]{2,1,0:T(8,128)(2,1)}, u32[]{:S(2)}) copy-start(bf16[4,256,1024]{2,1,0:T(8,128)(2,1)} %constant.22.clone.t_ref) | copy-start | bytes 6291460
  78.7 3.5 %copy-start.4 = (bf16[256,384]{1,0:T(8,128)(2,1)}, bf16[256,384]{1,0:T(8,128)(2,1)S(1)}, u32[]{:S(2)}) copy-start(bf16[256,384]{1,0:T(8,128)(2,1)S(1)} %get-tuple-element.59.a_ref) | copy-start | bytes 589828
  78.7 3.5 %copy-start.22 = (f32[256]{0:T(256)S(1)}, f32[256]{0:T(256)}, u32[]{:S(2)}) copy-start(f32[256]{0:T(256)} %param.28) | copy-start | bytes 3076
  78.7 3.5 %copy-start.23 = (f32[256]{0:T(256)S(1)}, f32[256]{0:T(256)}, u32[]{:S(2)}) copy-start(f32[256]{0:T(256)} %param.27) | copy-start | bytes 3076
  78.7 3.7 %collective-permute-start.7 = (bf16[256,384]{1,0:T(8,128)(2,1)}, bf16[256,384]{1,0:T(8,128)(2,1)}, u32[]{:S(2)}, u32[]{:S(2)}) collective-permute-start(bf16[256,384]{1,0:T(8,128)(2,1)} %get-tuple-element.60), channel_id=1, source_target_pairs={{0,1},{1,0},{2,3},{3,2},{4,5},{5,4},{6,7},{7,6},{8,9},{9,8},{10,11... | collective-permute-start | bytes 589832 | tf_op jit(solution)/shard_map/ppermute | solution.py:337
  80.5 6.7 %collective-permute-start.5 = (bf16[256,384]{1,0:T(8,128)(2,1)}, bf16[256,384]{1,0:T(8,128)(2,1)S(1)}, u32[]{:S(2)}, u32[]{:S(2)}) collective-permute-start(bf16[256,384]{1,0:T(8,128)(2,1)} %get-tuple-element.56), channel_id=1, source_target_pairs={{0,2},{1,3},{2,0},{3,1},{4,6},{5,7},{6,4},{7,5},{8,10},{9,11},{10,... | collective-permute-start | bytes 589832 | tf_op jit(solution)/shard_map/ppermute | solution.py:337
  80.5 11.1 %collective-permute-start.6 = (bf16[256,384]{1,0:T(8,128)(2,1)}, bf16[256,384]{1,0:T(8,128)(2,1)S(1)}, u32[]{:S(2)}, u32[]{:S(2)}) collective-permute-start(bf16[256,384]{1,0:T(8,128)(2,1)} %get-tuple-element.57), channel_id=1, source_target_pairs={{0,3},{1,2},{2,1},{3,0},{4,7},{5,6},{6,5},{7,4},{8,11},{9,10},{10,... | collective-permute-start | bytes 589832 | tf_op jit(solution)/shard_map/ppermute | solution.py:337
  82.4 1.6 %copy-start.2 = (bf16[16,256,256]{2,1,0:T(8,128)(2,1)S(1)}, bf16[16,256,256]{2,1,0:T(8,128)(2,1)}, u32[]{:S(2)}) copy-start(bf16[16,256,256]{2,1,0:T(8,128)(2,1)} %copy-done.1) | copy-start | bytes 6291460
  (10 other events, 8.6 us)

commit v2 on v1

v2 whole, which is shorter than its diff:
```python
import functools
import math

import jax
import jax.numpy as jnp
import numpy as np
from jax import lax
from jax.experimental import pallas as pl
from jax.experimental.pallas import tpu as pltpu
from jax.sharding import PartitionSpec as P

F32 = jnp.float32
BF16 = jnp.bfloat16
MIB = 1024 * 1024

H, W = 256, 1024
ROWS, COLS = 16, 4
PEERS = ROWS * COLS
NF = W // 2 // PEERS
CF = 96
HS = H // PEERS
LANES = HS * CF
LANE = 128
WIDE = HS * LANE
MID = H // HS
PARTS = 8
SPLIT = 9


def bf(table):
    return np.asarray(table, np.float32).astype(jnp.bfloat16)


@functools.lru_cache(None)
def width_tables():
    k = np.arange(W // 2)
    w = np.arange(W)
    angle = 2 * math.pi / W * ((w[:, None] * k[None, :]) % W)
    alternate = np.where(w % 2 == 0, 1.0, -1.0)
    cos, sin = np.cos(angle), np.sin(angle)
    fwd = np.stack([cos, np.where(k[None, :] == 0, alternate[:, None], -sin)], 0)
    inv = np.stack([np.where(k[None, :] == 0, 1.0, 2.0) * cos, np.where(k[None, :] == 0, alternate[:, None], -2.0 * sin)], 0)
    order = lambda t: t.reshape(2, W, PEERS, NF).transpose(2, 0, 3, 1).reshape(W, W)
    norm = 1.0 / math.sqrt(W)
    fwd = (order(fwd) * norm).reshape(W, COLS, W // COLS).transpose(1, 0, 2)
    inv = (order(inv) * norm).reshape(W, COLS, W // COLS).transpose(1, 0, 2)
    return bf(fwd), bf(inv)


@functools.lru_cache(None)
def height_tables():
    m = np.arange(MID)
    angle = 2 * math.pi / MID * ((m[:, None] * m[None, :]) % MID)
    cos, sin, zero = np.cos(angle), np.sin(angle), np.zeros((MID, MID))
    norm = 1.0 / math.sqrt(H)
    fwd = np.block([[cos, sin], [-sin, cos]])
    inv = np.block([[cos, -sin], [sin, cos]])
    none = np.zeros_like(fwd)
    pair = lambda t: np.block([[t, none], [none, t]])
    fwd_edge = np.stack(
        [np.block([[fwd], [none]]), np.block([[cos, zero], [-sin, zero], [zero, cos], [zero, -sin]])], 0
    )
    inv_edge = np.stack(
        [np.block([[inv, none]]), np.block([[cos, -sin, zero, zero], [zero, zero, cos, -sin]])], 0
    )
    return tuple(bf(t * norm) for t in (pair(fwd), pair(inv), fwd_edge, inv_edge))


@functools.lru_cache(None)
def twiddles():
    m = np.arange(MID)[:, None]
    r = np.repeat(np.arange(HS), LANE)[None, :]
    angle = 2 * math.pi / H * (m * r)
    return np.stack([np.cos(angle), -np.sin(angle)], 0).astype(np.float32)


def dot(a, b):
    return jnp.dot(a, b, preferred_element_type=F32)


def dot_nt(a, b):
    return lax.dot_general(a, b, (((1,), (1,)), ((), ())), preferred_element_type=F32)


def staged(body, staged_at, total, outs, refs):
    ins, rest = list(refs[:total]), refs[total:]
    count = len(staged_at)
    targets, sem, rest = rest[outs : outs + count], rest[outs + count], rest[:outs] + rest[outs + count + 1 :]
    loads = [pltpu.make_async_copy(ins[i], t, sem.at[n]) for n, (i, t) in enumerate(zip(staged_at, targets))]
    for load in loads:
        load.start()
    for i, t in zip(staged_at, targets):
        ins[i] = t
    for load in loads:
        load.wait()
    body(*ins, *rest)


def call(body, out_shape, operands, smem=(), hbm=(), stage=(), hbm_out=(), limit=16, flops=10**6, scratch=(), **kw):
    place = lambda i: pltpu.SMEM if i in smem else pltpu.HBM if i in hbm or i in stage else pltpu.VMEM
    single = not isinstance(out_shape, tuple)
    outs = [out_shape] if single else list(out_shape)
    spaces = [pltpu.HBM if i in hbm_out else pltpu.VMEM for i in range(len(outs))]
    shapes = [space(s.shape, s.dtype) for space, s in zip(spaces, outs)]
    specs = [pl.BlockSpec(memory_space=space) for space in spaces]
    operands = [v if i in smem else pltpu.with_memory_space_constraint(v, place(i)) for i, v in enumerate(operands)]
    if stage:
        inner, total = body, len(operands)
        body = lambda *refs: staged(inner, stage, total, len(outs), refs)
        held = [pltpu.VMEM(operands[i].shape, operands[i].dtype) for i in stage]
        scratch = held + [pltpu.SemaphoreType.DMA((len(stage),))] + list(scratch)
    return pl.pallas_call(
        body,
        out_shape=shapes[0] if single else tuple(shapes),
        in_specs=[pl.BlockSpec(memory_space=place(i)) for i in range(len(operands))],
        out_specs=specs[0] if single else tuple(specs),
        scratch_shapes=scratch,
        compiler_params=pltpu.CompilerParams(vmem_limit_bytes=limit * MIB),
        cost_estimate=pl.CostEstimate(flops=flops, bytes_accessed=flops // 1000, transcendentals=0),
        **kw,
    )(*operands)


def column(row):
    count = row.shape[1]
    diagonal = lax.broadcasted_iota(jnp.int32, (count, count), 0) == lax.broadcasted_iota(jnp.int32, (count, count), 1)
    return jnp.sum(jnp.where(diagonal, jnp.broadcast_to(row, (count, count)), 0.0), 1, keepdims=True)


def section_rows(weight, scale, shift, x):
    return jnp.maximum(scale * dot(weight, x) + shift, 0.0).astype(BF16)


def first_body(
    me_ref, image_ref, w_ref, scale_ref, shift_ref, x_ref, far_ref, affine_ref, held, weight, scale_row, shift_row, sem
):
    channels = image_ref.shape[0]
    size = channels // PARTS
    small = [(w_ref, weight), (scale_ref, scale_row), (shift_ref, shift_row)]
    others = [pltpu.make_async_copy(a, b, sem.at[PARTS + i]) for i, (a, b) in enumerate(small)]
    loads = []
    for i in range(PARTS):
        span = pl.ds(i * size, size)
        loads.append(pltpu.make_async_copy(image_ref.at[span], held.at[span], sem.at[i]))
    for load in others + loads[::-1]:
        load.start()
    for load in others:
        load.wait()
    scale, shift = column(scale_row[...]), column(shift_row[...])
    affine_ref[:, 0:1] = scale
    affine_ref[:, 1:2] = shift
    for i in range(PARTS - 1, -1, -1):
        span = slice(i * size, (i + 1) * size)
        loads[i].wait()
        x_ref[:, span, :] = jnp.swapaxes(held[span], 0, 1)
    first = HS * lax.bitwise_xor(me_ref[0], 2)
    skip = channels - w_ref.shape[1]
    for r in range(HS):
        far_ref[r * CF : (r + 1) * CF] = section_rows(weight[...], scale, shift, x_ref[first + r, skip:, :])


def rest_body(me_ref, x_ref, w_ref, affine_ref, near_ref, next_ref, last_ref):
    rows, channels, width = x_ref.shape
    skip = channels - w_ref.shape[1]
    scale, shift = affine_ref[:, 0:1], affine_ref[:, 1:2]
    for s, o_ref in ((3, last_ref), (1, next_ref), (0, near_ref)):
        first = HS * lax.bitwise_xor(me_ref[0], s)
        for r in range(HS):
            o_ref[r * CF : (r + 1) * CF] = section_rows(w_ref[...], scale, shift, x_ref[first + r, skip:, :])
    place = lax.broadcasted_iota(jnp.int32, (2 * rows, width), 0)
    lane = lax.broadcasted_iota(jnp.int32, (2 * rows, width), 1)
    ends = jnp.zeros((2 * rows, channels), F32)
    for h in range(rows):
        pick = ((place == h) & (lane == 0)) | ((place == rows + h) & (lane == width - 1))
        ends = ends + dot_nt(pick.astype(F32).astype(BF16), x_ref[h])
    ends = ends.astype(BF16)
    last_ref[LANES:] = ends
    next_ref[LANES:] = ends


def halo_body(me_ref, x_ref, next_ref, last_ref, down_ref, up_ref, side_ref):
    rows, channels, _ = x_ref.shape
    me = me_ref[0]
    odd = lax.rem(me, 2).astype(F32)
    near = next_ref[LANES:].astype(F32)
    far = last_ref[LANES:].astype(F32)
    even = 1.0 - odd
    left = (odd * near[rows:] + even * far[rows:]) * jnp.where(me > 0, 1.0, 0.0)
    right = (odd * far[:rows] + even * near[:rows]) * jnp.where(me < COLS - 1, 1.0, 0.0)
    sides = jnp.concatenate([left, right], 0).astype(BF16)
    side_ref[...] = sides
    down_ref[:channels] = x_ref[rows - 1]
    down_ref[channels:] = sides
    up_ref[:channels] = x_ref[0]
    up_ref[channels:] = sides


def width_near_body(me_ref, t_ref, near_ref, next_ref, o_ref):
    me = me_ref[0]
    o_ref[...] = dot_nt(t_ref[me], near_ref[...]) + dot_nt(t_ref[lax.bitwise_xor(me, 1)], next_ref[:LANES])


def width_far_body(me_ref, t_ref, part_ref, far_ref, last_ref, o_ref, held, sem):
    me = me_ref[0]
    size = o_ref.shape[0] // 4
    copies = []
    for i in range(4):
        span = pl.ds(i * size, size)
        total = part_ref[span] + dot_nt(t_ref[lax.bitwise_xor(me, 2), span], far_ref[...])
        held[span] = (total + dot_nt(t_ref[lax.bitwise_xor(me, 3), span], last_ref[:LANES])).astype(BF16)
        copies.append(pltpu.make_async_copy(held.at[span], o_ref.at[span], sem.at[i]))
        copies[-1].start()
    for copy in copies:
        copy.wait()


def widen(d):
    gap = jnp.zeros((d.shape[0], LANE - CF), d.dtype)
    return jnp.concatenate(sum([[d[:, CF * r : CF * r + CF], gap] for r in range(HS)], []), 1)


def narrow(d):
    return jnp.concatenate([d[:, LANE * r : LANE * r + CF] for r in range(HS)], 1)


def turns(real, imag):
    s02r, d02r, s13r, d13r = real[0] + real[2], real[0] - real[2], real[1] + real[3], real[1] - real[3]
    s02i, d02i, s13i, d13i = imag[0] + imag[2], imag[0] - imag[2], imag[1] + imag[3], imag[1] - imag[3]
    return (
        (s02r + s13r, s02i + s13i),
        (d02r + d13i, d02i - d13r),
        (s02r - s13r, s02i - s13i),
        (d02r - d13i, d02i + d13r),
    )


def spread(t):
    gap = jnp.zeros((t.shape[0], LANE - CF), t.dtype)
    return jnp.concatenate([t[:, :CF], gap, t[:, CF:], gap], 1)


def middle_body(
    z_ref, d_ref, *refs
):
    o_ref = refs[8]
    wide, back_ref = refs[17], refs[18]
    held, sem = refs[19], refs[20]
    z = z_ref[0]
    tables = refs[9:17]
    loads = []
    for i, (source, target) in enumerate(zip(refs[:8], tables)):
        source = source.at[z] if i in (2, 3) else source
        loads.append(pltpu.make_async_copy(source, target, sem.at[i]))
        loads[-1].start()
    fwd, inv, fwd_edge, inv_edge, tw, fw, scale_row, shift_row = tables
    wide[...] = widen(jnp.swapaxes(d_ref[...], 0, 1).reshape(W, LANES))
    for load in loads:
        load.wait()
    twr, twi = tw[0], tw[1]
    mixer = spread(fw[...].T)
    low = jnp.zeros((LANE - CF, 2 * LANE), BF16)
    mixer = jnp.concatenate([mixer[:CF], low, mixer[CF:], low], 0)
    scale, shift = spread(scale_row[...]), spread(shift_row[...])
    groups = [slice(LANE * r, LANE * r + LANE) for r in range(HS)]
    for own in ((0,), (1, 2), (3, 4), (5, 6), (7,)):
        data = jnp.concatenate(
            [wide[(p * NF + f) * MID : (p * NF + f + 1) * MID] for f in own for p in range(2)], 0
        )
        count = 2 if own == (0,) else len(own)
        half = 2 * MID * len(own)
        ahead = fwd_edge[...] if own == (0,) else fwd[:half, :half]
        u = dot(ahead, data)
        rows = []
        for f in range(count):
            ur = u[2 * f * MID : (2 * f + 1) * MID]
            ui = u[(2 * f + 1) * MID : (2 * f + 2) * MID]
            vr = ur * twr - ui * twi
            vi = ur * twi + ui * twr
            for real, imag in turns([vr[:, g] for g in groups], [vi[:, g] for g in groups]):
                rows.append(jnp.concatenate([real, imag], 1).astype(BF16))
        mixed = dot(jnp.concatenate(rows, 0), mixer)
        active = jnp.maximum(scale * mixed + shift, 0.0)
        rows = []
        for f in range(count):
            part = [active[(HS * f + j) * MID : (HS * f + j + 1) * MID] for j in (0, 3, 2, 1)]
            turned = turns([v[:, :LANE] for v in part], [v[:, LANE:] for v in part])
            br = jnp.concatenate([v[0] for v in turned], 1)
            bi = jnp.concatenate([v[1] for v in turned], 1)
            rows.append((br * twr + bi * twi).astype(BF16))
            rows.append((bi * twr - br * twi).astype(BF16))
        behind = inv_edge[...] if own == (0,) else inv[:half, :half]
        done = narrow(dot(behind, jnp.concatenate(rows, 0)).astype(BF16))
        for i, f in enumerate(own):
            for p in range(2):
                back_ref[p * NF + f] = done[(2 * i + p) * MID : (2 * i + p + 1) * MID]
    stores = []
    size = MID // 4
    for i in range(4):
        span = pl.ds(i * size, size)
        held[span] = jnp.swapaxes(back_ref[:, i * size : (i + 1) * size, :], 0, 1)
        stores.append(pltpu.make_async_copy(held.at[span], o_ref.at[span], sem.at[8 + i]))
        stores[-1].start()
    for store in stores:
        store.wait()


def inverse_body(pieces, me_ref, t_ref, d_ref, *refs):
    count = len(pieces)
    table, sem = refs[count:]
    loads = []
    for i, s in enumerate(pieces):
        loads.append(pltpu.make_async_copy(t_ref.at[lax.bitwise_xor(me_ref[0], s)], table.at[i], sem.at[i]))
        loads[-1].start()
    data = d_ref[...].T
    for i in range(count):
        loads[i].wait()
        refs[i][...] = dot(data, table[i]).astype(BF16)


def conv_setup(fl_ref, fg_ref, wl_ref, wg_ref):
    cl, channels = fl_ref.shape[1], fl_ref.shape[2]
    for dx in range(3):
        wl_ref[dx * channels : (dx + 1) * channels] = jnp.concatenate([fl_ref[3 * dy + dx] for dy in range(3)], 0).T
        wg_ref[dx * cl : (dx + 1) * cl] = jnp.concatenate([fg_ref[3 * dy + dx] for dy in range(3)], 1)


def conv_edges(side_ref, around, wl_ref, wg_ref, cols, edge):
    rows, channels = side_ref.shape[0] // 2, side_ref.shape[1]
    cl, cg = wl_ref.shape[1] // 3, wg_ref.shape[1] // 3
    cols[...] = jnp.zeros_like(cols)
    for side in range(2):
        own = pl.ds(side * rows, rows)
        cols[side, rows : 2 * rows] = side_ref[own]
        for i, other in enumerate(around):
            cols[side, 2 * i * rows : (2 * i + 1) * rows] = other[pl.ds(channels + side * rows, rows)]
        dx = 2 * side
        total = None
        for dy in range(3):
            taps = wl_ref[dx * channels : (dx + 1) * channels, dy * cl : (dy + 1) * cl]
            term = dot_nt(taps, cols[side, :, :cl])
            taps = wg_ref[dx * cl : (dx + 1) * cl, dy * cg : (dy + 1) * cg]
            extra = dot_nt(taps, cols[side, :, cl:])
            term = jnp.concatenate([term[:cl] + extra, term[cl:]], 0)
            term = pltpu.roll(term, LANE - (rows - 1 + dy), 1)
            total = term if total is None else total + term
        edge[side] = total


def edge_lanes(h, edge, before, behind):
    lane = lax.broadcasted_iota(jnp.int32, edge.shape[1:], 1)
    width = before.shape[1]
    first = pltpu.roll(edge[0], lax.rem(LANE - h, LANE), 1)
    final = pltpu.roll(edge[1], LANE - 1 - h, 1)
    before = jnp.concatenate([jnp.where(lane == 0, first, before[:, :LANE]), before[:, LANE:]], 1)
    last = jnp.where(lane == LANE - 1, final, behind[:, width - LANE :])
    return before, jnp.concatenate([behind[:, : width - LANE], last], 1)


def conv_row(h, three, wl_ref, wg_ref, wm_ref, ws_ref, affine_ref, edge, o_ref, out_ref, sem):
    channels, width = three[1].shape
    cl = wl_ref.shape[1] // 3
    local = jnp.concatenate([row[:cl] for row in three], 0)
    other = jnp.concatenate([row[cl:] for row in three], 0)
    parts = []
    for dx in range(3):
        yl = dot(wl_ref[dx * channels : (dx + 1) * channels], local)
        yg = dot(wg_ref[dx * cl : (dx + 1) * cl], other)
        parts.append(jnp.concatenate([yl[:cl] + yg, yl[cl:]], 0))
    before = pltpu.roll(parts[0], 1, 1)
    behind = pltpu.roll(parts[2], width - 1, 1)
    before, behind = edge_lanes(h, edge, before, behind)
    acc = parts[1] + before + behind
    mix = dot(wm_ref[...], section_rows(ws_ref[...], affine_ref[:, 0:1], affine_ref[:, 1:2], three[1][cl:]))
    o_ref[h, :cl] = acc[:cl].astype(BF16)
    o_ref[h, cl:] = (acc[cl:] + mix).astype(BF16)
    pltpu.make_async_copy(o_ref.at[h], out_ref.at[h], sem.at[0]).start()


def conv_inner_body(
    x_ref, fl_ref, fg_ref, wm_ref, ws_ref, affine_ref, out_ref, o_ref, edge, wl_ref, wg_ref, sem
):
    conv_setup(fl_ref, fg_ref, wl_ref, wg_ref)
    edge[...] = jnp.zeros_like(edge)

    def step(h, carry):
        three = [x_ref[h - 1], x_ref[h], x_ref[h + 1]]
        conv_row(h, three, wl_ref, wg_ref, wm_ref, ws_ref, affine_ref, edge, o_ref, out_ref, sem)
        return carry

    lax.fori_loop(1, SPLIT, step, 0)
    done = pl.ds(1, SPLIT - 1)
    pltpu.make_async_copy(o_ref.at[done], out_ref.at[done], sem.at[0]).wait()


def conv_outer_body(
    x_ref,
    side_ref,
    fl_ref,
    fg_ref,
    wm_ref,
    ws_ref,
    affine_ref,
    above_ref,
    below_ref,
    given_ref,
    out_ref,
    o_ref,
    cols,
    edge,
    wl_ref,
    wg_ref,
    sem,
):
    rows, channels, width = x_ref.shape
    inner = pl.ds(1, SPLIT - 1)
    load = pltpu.make_async_copy(given_ref.at[inner], o_ref.at[inner], sem.at[1])
    load.start()
    conv_setup(fl_ref, fg_ref, wl_ref, wg_ref)
    conv_edges(side_ref, (above_ref, below_ref), wl_ref, wg_ref, cols, edge)
    rest = (wl_ref, wg_ref, wm_ref, ws_ref, affine_ref, edge, o_ref, out_ref, sem)

    def step(h, carry):
        conv_row(h, [x_ref[h - 1], x_ref[h], x_ref[h + 1]], *rest)
        return carry

    lax.fori_loop(SPLIT, rows - 1, step, 0)
    conv_row(0, [above_ref[:channels], x_ref[0], x_ref[1]], *rest)
    conv_row(rows - 1, [x_ref[rows - 2], x_ref[rows - 1], below_ref[:channels]], *rest)
    load.wait()

    def fix(h, carry):
        none = jnp.zeros((channels, width), F32)
        before, behind = edge_lanes(h, edge, none, none)
        o_ref[h] = (o_ref[h].astype(F32) + before + behind).astype(BF16)
        return carry

    lax.fori_loop(1, SPLIT, fix, 0)
    store = pltpu.make_async_copy(o_ref.at[inner], out_ref.at[inner], sem.at[1])
    store.start()
    for done in (pl.ds(SPLIT, rows - SPLIT), pl.ds(0, 1)):
        pltpu.make_async_copy(o_ref.at[done], out_ref.at[done], sem.at[0]).wait()
    store.wait()


def final_rows(pieces, me_ref, x_ref, pre_ref, w_ref, affine_ref, o_ref, finish=None):
    channels = x_ref.shape[1]
    count = w_ref.shape[0]
    size = channels - count
    mixed = {}
    for s, piece in pieces:
        for r in range(HS):
            mixed[s, r] = dot(w_ref[...], piece[r * CF : (r + 1) * CF])
    for k in range(channels // size):
        span = slice(k * size, (k + 1) * size)
        scale, shift = affine_ref[span, 0:1], affine_ref[span, 1:2]
        for s, _ in pieces:
            first = HS * lax.bitwise_xor(me_ref[0], s)
            for r in range(HS):
                pre = pre_ref[first + r, span].astype(F32)
                if k:
                    pre = pre + mixed[s, r][(k - 1) * size : k * size]
                act = jnp.maximum(scale * pre + shift, 0.0)
                o_ref[first + r, span] = (x_ref[first + r, span].astype(F32) + act).astype(BF16)
        if finish is not None:
            finish(k, span)


def final_near_body(me_ref, x_ref, pre_ref, w_ref, affine_ref, t_ref, d_ref, next_ref, o_ref, table, sem):
    load = pltpu.make_async_copy(t_ref.at[me_ref[0]], table, sem.at[0])
    load.start()
    data = d_ref[...].T
    load.wait()
    near = dot(data, table[...]).astype(BF16)
    final_rows(((0, near), (1, next_ref)), me_ref, x_ref, pre_ref, w_ref, affine_ref, o_ref)


def final_far_body(me_ref, x_ref, pre_ref, w_ref, affine_ref, far_ref, given_ref, o_ref):
    final_rows(((2, far_ref),), me_ref, x_ref, pre_ref, w_ref, affine_ref, o_ref)


def final_last_body(me_ref, x_ref, pre_ref, w_ref, affine_ref, last_ref, given_ref, o_ref, out_ref, held, sem):
    copies = []

    def finish(k, span):
        held[span] = jnp.swapaxes(o_ref[:, span, :], 0, 1)
        copies.append(pltpu.make_async_copy(held.at[span], out_ref.at[span], sem.at[k]))
        copies[-1].start()

    final_rows(((3, last_ref),), me_ref, x_ref, pre_ref, w_ref, affine_ref, o_ref, finish)
    for copy in copies:
        copy.wait()


def shift_along(block, axis, step):
    count = lax.axis_size(axis)
    pairs = [(i, i + step) for i in range(count) if 0 <= i + step < count]
    return lax.ppermute(block, axis, pairs)


def swap(block, s):
    return lax.ppermute(block, "col", [(i, i ^ s) for i in range(COLS)])


def after(value, *others):
    return lax.optimization_barrier((value,) + others)


def per_device(
    image,
    from_local,
    from_global,
    section_weight,
    section_scale,
    section_shift,
    fourier_weight,
    fourier_scale,
    fourier_shift,
    mix_weight,
    out_scale,
    out_shift,
):
    channels, rows, width = image.shape
    cl = from_local.shape[2]
    cg = channels - cl
    me = lax.axis_index("col").astype(jnp.int32).reshape(1)
    z = jnp.logical_and(lax.axis_index("row") == 0, lax.axis_index("col") == 0).astype(jnp.int32).reshape(1)
    shape = jax.ShapeDtypeStruct
    dma = pltpu.SemaphoreType.DMA

    whole = shape((rows, channels, width), BF16)
    block, block_ends = shape((LANES, width), BF16), shape((LANES + 2 * rows, width), BF16)
    x, far, section_affine = call(
        first_body,
        (whole, block, shape((CF, 2), F32)),
        (me, image, section_weight, section_scale[None], section_shift[None]),
        smem=(0,),
        hbm=(1, 2, 3, 4),
        scratch=[
            pltpu.VMEM((channels, rows, width), BF16),
            pltpu.VMEM((CF, cg), BF16),
            pltpu.VMEM((1, CF), F32),
            pltpu.VMEM((1, CF), F32),
            dma((PARTS + 3,)),
        ],
    )
    far = swap(far, 2)
    near, other, last = call(
        rest_body, (block, block_ends, block_ends), (me, x, section_weight, section_affine), smem=(0,)
    )
    last, other = swap(last, 3), swap(other, 1)

    weights = (jnp.transpose(from_local, (0, 2, 1)), from_global, mix_weight, section_weight, section_affine)
    scratch = [
        pltpu.VMEM((rows, channels, width), BF16),
        pltpu.VMEM((2, LANE, channels), BF16),
        pltpu.VMEM((2, channels, LANE), F32),
        pltpu.VMEM((3 * channels, 3 * cl), BF16),
        pltpu.VMEM((3 * cl, 3 * cg), BF16),
        dma((2,)),
    ]
    pre = call(
        conv_inner_body,
        whole,
        (x,) + weights,
        hbm_out=(0,),
        stage=tuple(range(1, 6)),
        flops=10**9,
        scratch=scratch[:1] + scratch[2:],
    )
    fwd_w, inv_w = (jnp.asarray(t) for t in width_tables())
    part = call(width_near_body, shape((W, LANES), F32), (me, fwd_w, near, other), smem=(0,))
    part, pre = after(part, pre)
    spectra = call(
        width_far_body,
        shape((W, LANES), BF16),
        (me, fwd_w, part, far, last),
        smem=(0,),
        hbm_out=(0,),
        scratch=[pltpu.VMEM((W, LANES), BF16), dma((4,))],
    )
    spectra, other, last = after(spectra, other, last)
    spectra = lax.all_to_all(
        spectra.reshape(PEERS, 2 * NF, LANES), ("row", "col"), split_axis=0, concat_axis=0, tiled=True
    )
    ends = shape((channels + 2 * rows, width), BF16)
    down, up, sides = call(
        halo_body, (ends, ends, shape((2 * rows, channels), BF16)), (me, x, other, last), smem=(0,)
    )
    above, below = shift_along(down, "row", 1), shift_along(up, "row", -1)

    tables = [jnp.asarray(t) for t in height_tables() + (twiddles(),)]
    tables += [fourier_weight, fourier_scale[None], fourier_shift[None]]
    sizes = [t.shape[1:] if i in (2, 3) else t.shape for i, t in enumerate(tables)]
    returned = call(
        middle_body,
        shape((PEERS, 2 * NF, LANES), BF16),
        (z, spectra, *tables),
        smem=(0,),
        hbm=range(2, 10),
        hbm_out=(0,),
        limit=24,
        scratch=[pltpu.VMEM(s, t.dtype) for s, t in zip(sizes, tables)]
        + [
            pltpu.VMEM((W, WIDE), BF16),
            pltpu.VMEM((2 * NF, MID, LANES), BF16),
            pltpu.VMEM((PEERS, 2 * NF, LANES), BF16),
            dma((12,)),
        ],
    )
    returned, above, below = after(returned, above, below)
    returned = lax.all_to_all(returned, ("row", "col"), split_axis=0, concat_axis=0, tiled=True).reshape(W, LANES)
    pre = call(
        conv_outer_body,
        whole,
        (x, sides) + weights + (above, below, pre),
        hbm=(9,),
        hbm_out=(0,),
        stage=tuple(range(1, 9)),
        flops=10**9,
        input_output_aliases={9: 0},
        scratch=scratch,
    )
    returned, pre = after(returned, pre)

    piece = shape((LANES, width), BF16)
    affine = jnp.stack([out_scale, out_shift], 1)
    far, last, other = call(
        functools.partial(inverse_body, (2, 3, 1)),
        (piece,) * 3,
        (me, inv_w, returned),
        smem=(0,),
        hbm=(1,),
        scratch=[pltpu.VMEM((3, W, width), BF16), dma((3,))],
    )
    far, last, other = swap(far, 2), swap(last, 3), swap(other, 1)
    common = (me, x, pre, mix_weight, affine)
    half = call(
        final_near_body,
        whole,
        common + (inv_w, returned, other),
        smem=(0,),
        hbm=(5,),
        stage=(2, 3, 4),
        scratch=[pltpu.VMEM((W, width), BF16), dma((1,))],
    )
    half = call(
        final_far_body, whole, common + (far, half), smem=(0,), stage=(2, 3, 4), input_output_aliases={6: 0}
    )
    _, result = call(
        final_last_body,
        (whole, shape(image.shape, BF16)),
        common + (last, half),
        smem=(0,),
        hbm_out=(1,),
        input_output_aliases={6: 0},
        scratch=[pltpu.VMEM(image.shape, BF16), dma((8,))],
    )
    return result


def solution(mesh):
    return jax.shard_map(
        per_device,
        mesh=mesh,
        in_specs=(P("img", "row", "col"), P(), P(), P(), P(), P(), P(), P(), P(), P(), P(), P()),
        out_specs=P("img", "row", "col"),
        check_vma=False,
    )
```

time: 95.8 us -> 84.9 us (0.89)
  local copies, waits for them, and re-layouts: 21.2 us -> 1.44 us
  Pallas kernels: 25.8 us -> 36.7 us
  starting transfers between devices: 27.2 us -> 24.5 us
  waiting for transfers between devices: 19.9 us -> 21.2 us
    unnamed x49 -> x22, local copies, waits for them, and re-layouts: 18.5 us -> 0.64 us
    pallas_call x11 -> x12, Pallas kernels: 25.8 us -> 36.7 us  [call(): pl.pallas_call(body, out_shape=shapes[0] if single else tuple(shapes), in...]
    all_to_all x1, waiting for transfers between devices: 0.01 us -> 9.64 us  [per_device(): lax.all_to_all(spectra.reshape(PEERS, 2 * NF, LANES), ('row', 'col'), spl...]
    ppermute x6, waiting for transfers between devices: 12.7 us -> 4.81 us  [swap(): return lax.ppermute(block, 'col', [(i, i ^ s) for i in range(COLS)])]
    ppermute x2, waiting for transfers between devices: 5.41 us -> 0.01 us  [shift_along(): return lax.ppermute(block, axis, pairs)]
    all_to_all x1, waiting for transfers between devices: 1.82 us -> 6.78 us  [per_device(): lax.all_to_all(returned, ('row', 'col'), split_axis=0, concat_axis=0, til...]
    transpose x1 -> x0, local copies, waits for them, and re-layouts: 2.51 us -> none  [per_device(): return jnp.transpose(result, (1, 0, 2))]
    all_to_all x1, starting transfers between devices: 6.52 us -> 4.4 us  [per_device(): lax.all_to_all(returned, ('row', 'col'), split_axis=0, concat_axis=0, til...]
  transfers between devices with their start and end apart: 10 -> 10, of which waited for: 7 -> 5; matrix products, arithmetic and copies ran while one was open for 0% -> 1% of each run, Pallas kernels for 15% -> 32%
where the time goes in v2:
time: 84.9 us; the launch traced here: 84.3 us
  Pallas kernels  36.7 us (43%)
  starting transfers between devices  24.5 us (29%)
  waiting for transfers between devices  21.2 us (25%)
  local copies, waits for them, and re-layouts  1.44 us (2%)
    pallas_call x12, Pallas kernels, call(): pl.pallas_call(body, out_shape=shapes[0] if single else tuple(shapes), in...  36.7 us
    all_to_all x1, starting transfers between devices, per_device(): lax.all_to_all(spectra.reshape(PEERS, 2 * NF, LANES), ('row', 'col'), spl...  10.4 us
    all_to_all x1, waiting for transfers between devices, per_device(): lax.all_to_all(spectra.reshape(PEERS, 2 * NF, LANES), ('row', 'col'), spl...  9.64 us
    all_to_all x1, waiting for transfers between devices, per_device(): lax.all_to_all(returned, ('row', 'col'), split_axis=0, concat_axis=0, til...  6.78 us
    ppermute x6, starting transfers between devices, swap(): return lax.ppermute(block, 'col', [(i, i ^ s) for i in range(COLS)])  5.11 us
    ppermute x6, waiting for transfers between devices, swap(): return lax.ppermute(block, 'col', [(i, i ^ s) for i in range(COLS)])  4.81 us
    ppermute x2, starting transfers between devices, shift_along(): return lax.ppermute(block, axis, pairs)  4.58 us
    all_to_all x1, starting transfers between devices, per_device(): lax.all_to_all(returned, ('row', 'col'), split_axis=0, concat_axis=0, til...  4.4 us
  transfers between devices with their start and end apart: 10, of which 5 were waited for; matrix products, arithmetic and copies ran while one was open for 1% of the time, Pallas kernels for 32%

profile of v2, /device:TPU:1, one launch (start us, length us, event | category | flops | bytes accessed | tf_op | source)
XLA Modules:
  0.0 84.3 jit_solution(8465355631945256387)
XLA Ops:
  0.0 1.9 %shard_map.181 = (bf16[16,256,256]{2,1,0:T(8,128)(2,1)S(1)}, bf16[384,256]{1,0:T(8,128)(2,1)S(1)}, f32[96,2]{1,0:T(8,128)S(1)}) custom-call(s32[1]{0:T(128)} %bitcast.me_ref.refs_0_, bf16[256,16,256]{2,1,0:T(8,128)(2,1)} %image_ref.1, bf16[96,192]{1,0:T(8,128)(2,1)} %refs_5_.4, f32[1,96]{1,0:T(1,128)} %bitcast.20, f32[1,96]{1,0:T(1,128)} %bitcast.21), custom_call_target="tpu_custom_call" | custom-call | flops 1000000 | bytes 1000 | tf_op jit(solution)/shard_map/pallas_call | solution.py:112
  2.0 0.9 %shard_map.182 = (bf16[384,256]{1,0:T(8,128)(2,1)S(1)}, bf16[416,256]{1,0:T(8,128)(2,1)S(1)}, bf16[416,256]{1,0:T(8,128)(2,1)S(1)}) custom-call(s32[1]{0:T(128)} %bitcast.me_ref.refs_0_, bf16[16,256,256]{2,1,0:T(8,128)(2,1)S(1)} %get-tuple-element.28.x_ref.refs_0_.refs_1_, bf16[96,192]{1,0:T(8,128)(2,1)S(1)} %copy-done.4, ...), custom_call_target="tpu_custom_call" | custom-call | flops 1000000 | bytes 1000 | tf_op jit(solution)/shard_map/pallas_call | solution.py:112
  2.9 1.4 %collective-permute-start = (bf16[416,256]{1,0:T(8,128)(2,1)S(1)}, bf16[416,256]{1,0:T(8,128)(2,1)S(1)}, u32[]{:S(2)}, u32[]{:S(2)}) collective-permute-start(bf16[416,256]{1,0:T(8,128)(2,1)S(1)} %get-tuple-element.31), channel_id=1, source_target_pairs={{0,1},{1,0},{2,3},{3,2},{4,5},{5,4},{6,7},{7,6},{8,9},{9,8},{10,11... | collective-permute-start | bytes 638984 | tf_op jit(solution)/shard_map/ppermute | solution.py:501
  4.3 1.4 %collective-permute-start.2 = (bf16[416,256]{1,0:T(8,128)(2,1)S(1)}, bf16[416,256]{1,0:T(8,128)(2,1)S(1)}, u32[]{:S(2)}, u32[]{:S(2)}) collective-permute-start(bf16[416,256]{1,0:T(8,128)(2,1)S(1)} %get-tuple-element.34), channel_id=1, source_target_pairs={{0,3},{1,2},{2,1},{3,0},{4,7},{5,6},{6,5},{7,4},{8,11},{9,10},{10,... | collective-permute-start | bytes 638984 | tf_op jit(solution)/shard_map/ppermute | solution.py:501
  5.8 6.5 %shard_map.184.refs_9_ = bf16[16,256,256]{2,1,0:T(8,128)(2,1)} custom-call(bf16[16,256,256]{2,1,0:T(8,128)(2,1)S(1)} %get-tuple-element.28.x_ref.refs_0_.refs_1_, bf16[9,64,256]{2,1,0:T(8,128)(2,1)} %bitcast.14, bf16[9,64,192]{2,1,0:T(8,128)(2,1)} %refs_3_.6, bf16[192,96]{1,0:T(8,128)(2,1)} %w_ref.5, bf16[96,192]{1,0:T(8,128)(2,1)} %refs_5_.4, f32[96,2]{1,0:T(8,128)} %copy-done.5), custom_call_target="tpu_custom_call" | custom-call | flops 1000000000 | bytes 1000000 | tf_op jit(solution)/shard_map/pallas_call | solution.py:112
  12.2 0.7 shard_map.183.part_ref
  13.0 2.2 %collective-permute-done.1.far_ref = bf16[384,256]{1,0:T(8,128)(2,1)S(1)} collective-permute-done((bf16[384,256]{1,0:T(8,128)(2,1)S(1)}, bf16[384,256]{1,0:T(8,128)(2,1)S(1)}, u32[]{:S(2)}, u32[]{:S(2)}) %collective-permute-start.1) | collective-permute-done | bytes 196640 | tf_op jit(solution)/shard_map/ppermute | solution.py:501
  15.2 1.4 %shard_map.185 = bf16[1024,384]{1,0:T(8,128)(2,1)} custom-call(s32[1]{0:T(128)} %bitcast.me_ref.refs_0_, bf16[4,1024,256]{2,1,0:T(8,128)(2,1)S(1)} %copy-done.1, f32[1024,384]{1,0:T(8,128)S(1)} %shard_map.183.part_ref, bf16[384,256]{1,0:T(8,128)(2,1)S(1)} %collective-permute-done.1.far_ref, bf16[416,256]{1,0:T(8,128)(2,1)S(1)} %collective-permute-done.2.last_ref), custom_call_target="tpu_custom_call" | custom-call | flops 1000000 | bytes 1000 | tf_op jit(solution)/shard_map/pallas_call | solution.py:112
  16.6 10.4 %all-to-all-start = ((bf16[64,16,384]{2,1,0:T(8,128)(2,1)}), bf16[64,16,384]{2,1,0:T(8,128)(2,1)S(1)}, u32[]{:S(2)}, u32[]{:S(2)}) async-start(bf16[64,16,384]{2,1,0:T(8,128)(2,1)} %bitcast.13), calls=%async_computation | async-start | bytes 1572864 | tf_op jit(solution)/shard_map/all_to_all | solution.py:582
  27.0 0.7 shard_map.187
  28.3 3.3 %collective-permute-start.3 = (bf16[288,256]{1,0:T(8,128)(2,1)}, bf16[288,256]{1,0:T(8,128)(2,1)S(1)}, u32[]{:S(2)}, u32[]{:S(2)}) collective-permute-start(bf16[288,256]{1,0:T(8,128)(2,1)} %get-tuple-element.38), channel_id=1, source_target_pairs={{0,4},{4,8},{8,12},{12,16},{16,20},{20,24},{24,28},{28,32},{32,36}... | collective-permute-start | bytes 442376 | tf_op jit(solution)/shard_map/ppermute | solution.py:497
  31.6 1.3 %collective-permute-start.4 = (bf16[288,256]{1,0:T(8,128)(2,1)S(1)}, bf16[288,256]{1,0:T(8,128)(2,1)S(1)}, u32[]{:S(2)}, u32[]{:S(2)}) collective-permute-start(bf16[288,256]{1,0:T(8,128)(2,1)S(1)} %get-tuple-element.39), channel_id=1, source_target_pairs={{4,0},{8,4},{12,8},{16,12},{20,16},{24,20},{28,24},{32,28},{36,32}... | collective-permute-start | bytes 442376 | tf_op jit(solution)/shard_map/ppermute | solution.py:497
  32.9 9.6 %all-to-all-done.d_ref = bf16[64,16,384]{2,1,0:T(8,128)(2,1)S(1)} async-done(((bf16[64,16,384]{2,1,0:T(8,128)(2,1)}), bf16[64,16,384]{2,1,0:T(8,128)(2,1)S(1)}, u32[]{:S(2)}, u32[]{:S(2)}) %all-to-all-start) | async-done | bytes 786464 | tf_op jit(solution)/shard_map/all_to_all | solution.py:582
  42.6 5.2 %shard_map.186 = bf16[64,16,384]{2,1,0:T(8,128)(2,1)} custom-call(s32[1]{0:T(128)} %bitcast.3.z_ref, bf16[64,16,384]{2,1,0:T(8,128)(2,1)S(1)} %all-to-all-done.d_ref, bf16[256,256]{1,0:T(8,128)(2,1)} %constant.27.clone.refs_0_, bf16[256,256]{1,0:T(8,128)(2,1)} %constant.28.clone.refs_1_, bf16[2,256,128]{2,1,0:T(8,128)(2,1)} %constant.29.clone.refs_2_, ...), custom_call_target="tpu_custom_call" | custom-call | flops 1000000 | bytes 1000 | tf_op jit(solution)/shard_map/pallas_call | solution.py:112
  47.8 4.4 %all-to-all-start.1 = ((bf16[64,16,384]{2,1,0:T(8,128)(2,1)}), bf16[64,16,384]{2,1,0:T(8,128)(2,1)S(1)}, u32[]{:S(2)}, u32[]{:S(2)}) async-start(bf16[64,16,384]{2,1,0:T(8,128)(2,1)} %shard_map.186), calls=%async_computation.1 | async-start | bytes 1572864 | tf_op jit(solution)/shard_map/all_to_all | solution.py:611
  52.2 8.3 %shard_map.188.refs_2_.pre_ref = bf16[16,256,256]{2,1,0:T(8,128)(2,1)} custom-call(bf16[16,256,256]{2,1,0:T(8,128)(2,1)S(1)} %get-tuple-element.28.x_ref.refs_0_.refs_1_, bf16[32,256]{1,0:T(8,128)(2,1)} %copy-done.6, bf16[9,64,256]{2,1,0:T(8,128)(2,1)} %bitcast.15, bf16[9,64,192]{2,1,0:T(8,128)(2,1)} %refs_3_.6, ...), custom_call_target="tpu_custom_call", output_to_operand_aliasing={{}: (9, {})} | custom-call | flops 1000000000 | bytes 1000000 | tf_op jit(solution)/shard_map/pallas_call | solution.py:112
  60.6 6.8 %all-to-all-done.1 = bf16[64,16,384]{2,1,0:T(8,128)(2,1)S(1)} async-done(((bf16[64,16,384]{2,1,0:T(8,128)(2,1)}), bf16[64,16,384]{2,1,0:T(8,128)(2,1)S(1)}, u32[]{:S(2)}, u32[]{:S(2)}) %all-to-all-start.1) | async-done | bytes 786464 | tf_op jit(solution)/shard_map/all_to_all | solution.py:611
  67.3 3.3 %shard_map.189 = (bf16[384,256]{1,0:T(8,128)(2,1)}, bf16[384,256]{1,0:T(8,128)(2,1)}, bf16[384,256]{1,0:T(8,128)(2,1)}) custom-call(s32[1]{0:T(128)} %bitcast.me_ref.refs_0_, bf16[4,1024,256]{2,1,0:T(8,128)(2,1)} %constant.26.clone.t_ref.refs_5_, bf16[1024,384]{1,0:T(8,128)(2,1)S(1)} %bitcast.11), custom_call_target="tpu_custom_call" | custom-call | flops 1000000 | bytes 1000 | tf_op jit(solution)/shard_map/pallas_call | solution.py:112
  71.1 1.7 %collective-permute-start.5 = (bf16[384,256]{1,0:T(8,128)(2,1)}, bf16[384,256]{1,0:T(8,128)(2,1)S(1)}, u32[]{:S(2)}, u32[]{:S(2)}) collective-permute-start(bf16[384,256]{1,0:T(8,128)(2,1)} %get-tuple-element.47), channel_id=1, source_target_pairs={{0,3},{1,2},{2,1},{3,0},{4,7},{5,6},{6,5},{7,4},{8,11},{9,10},{10,... | collective-permute-start | bytes 589832 | tf_op jit(solution)/shard_map/ppermute | solution.py:501
  72.9 0.8 copy.27.refs_4_.affine_ref
  73.7 3.7 %shard_map.190.refs_6_ = bf16[16,256,256]{2,1,0:T(8,128)(2,1)S(1)} custom-call(s32[1]{0:T(128)} %bitcast.me_ref.refs_0_, bf16[16,256,256]{2,1,0:T(8,128)(2,1)S(1)} %get-tuple-element.28.x_ref.refs_0_.refs_1_, bf16[16,256,256]{2,1,0:T(8,128)(2,1)} %shard_map.188.refs_2_.pre_ref, bf16[192,96]{1,0:T(8,128)(2,1)} %w_ref.5, f32[256,2]{1,0:T(8,128)} %copy.27.refs_4_.affine_ref, ...), custom_call_target="tpu_custom_call" | custom-call | flops 1000000 | bytes 1000 | tf_op jit(solution)/shard_map/pallas_call | solution.py:112
  77.8 2.2 %shard_map.191.given_ref = bf16[16,256,256]{2,1,0:T(8,128)(2,1)S(1)} custom-call(s32[1]{0:T(128)} %bitcast.me_ref.refs_0_, bf16[16,256,256]{2,1,0:T(8,128)(2,1)S(1)} %get-tuple-element.28.x_ref.refs_0_.refs_1_, bf16[16,256,256]{2,1,0:T(8,128)(2,1)} %shard_map.188.refs_2_.pre_ref, bf16[192,96]{1,0:T(8,128)(2,1)} %w_ref.5, ...), custom_call_target="tpu_custom_call", output_to_operand_aliasing={{}: (6, {})} | custom-call | flops 1000000 | bytes 1000 | tf_op jit(solution)/shard_map/pallas_call | solution.py:112
  80.0 2.2 %collective-permute-done.5.last_ref = bf16[384,256]{1,0:T(8,128)(2,1)S(1)} collective-permute-done((bf16[384,256]{1,0:T(8,128)(2,1)}, bf16[384,256]{1,0:T(8,128)(2,1)S(1)}, u32[]{:S(2)}, u32[]{:S(2)}) %collective-permute-start.5) | collective-permute-done | bytes 196640 | tf_op jit(solution)/shard_map/ppermute | solution.py:501
  82.2 1.9 %shard_map.192 = (bf16[16,256,256]{2,1,0:T(8,128)(2,1)S(1)}, bf16[256,16,256]{2,1,0:T(8,128)(2,1)}) custom-call(s32[1]{0:T(128)} %bitcast.me_ref.refs_0_, bf16[16,256,256]{2,1,0:T(8,128)(2,1)S(1)} %get-tuple-element.28.x_ref.refs_0_.refs_1_, bf16[16,256,256]{2,1,0:T(8,128)(2,1)S(1)} %copy-done, ...), custom_call_target="tpu_custom_call", output_to_operand_aliasing={{0}: (6, {})} | custom-call | flops 1000000 | bytes 1000 | tf_op jit(solution)/shard_map/pallas_call | solution.py:112
  (32 shorter events, 1.6 us)
Async XLA Ops:
  0.0 2.0 %copy-start.4 = (bf16[96,192]{1,0:T(8,128)(2,1)S(1)}, bf16[96,192]{1,0:T(8,128)(2,1)}, u32[]{:S(2)}) copy-start(bf16[96,192]{1,0:T(8,128)(2,1)} %refs_5_.4) | copy-start | bytes 110596
  2.0 3.8 %copy-start.5 = (f32[96,2]{1,0:T(8,128)}, f32[96,2]{1,0:T(8,128)S(1)}, u32[]{:S(2)}) copy-start(f32[96,2]{1,0:T(8,128)S(1)} %get-tuple-element.29.affine_ref.refs_5_.refs_6_) | copy-start | bytes 2308
  2.9 9.4 %collective-permute-start = (bf16[416,256]{1,0:T(8,128)(2,1)S(1)}, bf16[416,256]{1,0:T(8,128)(2,1)S(1)}, u32[]{:S(2)}, u32[]{:S(2)}) collective-permute-start(bf16[416,256]{1,0:T(8,128)(2,1)S(1)} %get-tuple-element.31), channel_id=1, source_target_pairs={{0,1},{1,0},{2,3},{3,2},{4,5},{5,4},{6,7},{7,6},{8,9},{9,8},{10,11... | collective-permute-start | bytes 638984 | tf_op jit(solution)/shard_map/ppermute | solution.py:501
  4.3 10.9 %collective-permute-start.2 = (bf16[416,256]{1,0:T(8,128)(2,1)S(1)}, bf16[416,256]{1,0:T(8,128)(2,1)S(1)}, u32[]{:S(2)}, u32[]{:S(2)}) collective-permute-start(bf16[416,256]{1,0:T(8,128)(2,1)S(1)} %get-tuple-element.34), channel_id=1, source_target_pairs={{0,3},{1,2},{2,1},{3,0},{4,7},{5,6},{6,5},{7,4},{8,11},{9,10},{10,... | collective-permute-start | bytes 638984 | tf_op jit(solution)/shard_map/ppermute | solution.py:501
  5.7 9.5 %collective-permute-start.1 = (bf16[384,256]{1,0:T(8,128)(2,1)S(1)}, bf16[384,256]{1,0:T(8,128)(2,1)S(1)}, u32[]{:S(2)}, u32[]{:S(2)}) collective-permute-start(bf16[384,256]{1,0:T(8,128)(2,1)S(1)} %get-tuple-element.33), channel_id=1, source_target_pairs={{0,2},{1,3},{2,0},{3,1},{4,6},{5,7},{6,4},{7,5},{8,10},{9,11},{10,... | collective-permute-start | bytes 589832 | tf_op jit(solution)/shard_map/ppermute | solution.py:501
  5.8 6.5 %copy-start.1 = (bf16[4,1024,256]{2,1,0:T(8,128)(2,1)S(1)}, bf16[4,1024,256]{2,1,0:T(8,128)(2,1)}, u32[]{:S(2)}) copy-start(bf16[4,1024,256]{2,1,0:T(8,128)(2,1)} %constant.25.clone.t_ref) | copy-start | bytes 6291460
  16.6 25.9 %all-to-all-start = ((bf16[64,16,384]{2,1,0:T(8,128)(2,1)}), bf16[64,16,384]{2,1,0:T(8,128)(2,1)S(1)}, u32[]{:S(2)}, u32[]{:S(2)}) async-start(bf16[64,16,384]{2,1,0:T(8,128)(2,1)} %bitcast.13), calls=%async_computation | async-start | bytes 1572864 | tf_op jit(solution)/shard_map/all_to_all | solution.py:582
  27.7 0.6 copy-start.6
  28.3 19.5 %collective-permute-start.3 = (bf16[288,256]{1,0:T(8,128)(2,1)}, bf16[288,256]{1,0:T(8,128)(2,1)S(1)}, u32[]{:S(2)}, u32[]{:S(2)}) collective-permute-start(bf16[288,256]{1,0:T(8,128)(2,1)} %get-tuple-element.38), channel_id=1, source_target_pairs={{0,4},{4,8},{8,12},{12,16},{16,20},{20,24},{24,28},{28,32},{32,36}... | collective-permute-start | bytes 442376 | tf_op jit(solution)/shard_map/ppermute | solution.py:497
  31.6 16.2 %collective-permute-start.4 = (bf16[288,256]{1,0:T(8,128)(2,1)S(1)}, bf16[288,256]{1,0:T(8,128)(2,1)S(1)}, u32[]{:S(2)}, u32[]{:S(2)}) collective-permute-start(bf16[288,256]{1,0:T(8,128)(2,1)S(1)} %get-tuple-element.39), channel_id=1, source_target_pairs={{4,0},{8,4},{12,8},{16,12},{20,16},{24,20},{28,24},{32,28},{36,32}... | collective-permute-start | bytes 442376 | tf_op jit(solution)/shard_map/ppermute | solution.py:497
  47.8 4.4 %copy-start.7 = (bf16[288,256]{1,0:T(8,128)(2,1)}, bf16[288,256]{1,0:T(8,128)(2,1)S(1)}, u32[]{:S(2)}) copy-start(bf16[288,256]{1,0:T(8,128)(2,1)S(1)} %collective-permute-done.3.refs_7_) | copy-start | bytes 442372
  47.8 4.4 %copy-start.8 = (bf16[288,256]{1,0:T(8,128)(2,1)}, bf16[288,256]{1,0:T(8,128)(2,1)S(1)}, u32[]{:S(2)}) copy-start(bf16[288,256]{1,0:T(8,128)(2,1)S(1)} %collective-permute-done.4.refs_8_) | copy-start | bytes 442372
  47.8 19.5 %all-to-all-start.1 = ((bf16[64,16,384]{2,1,0:T(8,128)(2,1)}), bf16[64,16,384]{2,1,0:T(8,128)(2,1)S(1)}, u32[]{:S(2)}, u32[]{:S(2)}) async-start(bf16[64,16,384]{2,1,0:T(8,128)(2,1)} %shard_map.186), calls=%async_computation.1 | async-start | bytes 1572864 | tf_op jit(solution)/shard_map/all_to_all | solution.py:611
  60.5 12.3 %copy-start.9 = (f32[256]{0:T(256)S(1)}, f32[256]{0:T(256)}, u32[]{:S(2)}) copy-start(f32[256]{0:T(256)} %param.30) | copy-start | bytes 3076
  60.5 12.3 %copy-start.10 = (f32[256]{0:T(256)S(1)}, f32[256]{0:T(256)}, u32[]{:S(2)}) copy-start(f32[256]{0:T(256)} %param.29) | copy-start | bytes 3076
  70.7 3.0 %collective-permute-start.7 = (bf16[384,256]{1,0:T(8,128)(2,1)}, bf16[384,256]{1,0:T(8,128)(2,1)S(1)}, u32[]{:S(2)}, u32[]{:S(2)}) collective-permute-start(bf16[384,256]{1,0:T(8,128)(2,1)} %get-tuple-element.49), channel_id=1, source_target_pairs={{0,1},{1,0},{2,3},{3,2},{4,5},{5,4},{6,7},{7,6},{8,9},{9,8},{10,11... | collective-permute-start | bytes 589832 | tf_op jit(solution)/shard_map/ppermute | solution.py:501
  71.1 6.7 %collective-permute-start.6 = (bf16[384,256]{1,0:T(8,128)(2,1)}, bf16[384,256]{1,0:T(8,128)(2,1)S(1)}, u32[]{:S(2)}, u32[]{:S(2)}) collective-permute-start(bf16[384,256]{1,0:T(8,128)(2,1)} %get-tuple-element.48), channel_id=1, source_target_pairs={{0,2},{1,3},{2,0},{3,1},{4,6},{5,7},{6,4},{7,5},{8,10},{9,11},{10,... | collective-permute-start | bytes 589832 | tf_op jit(solution)/shard_map/ppermute | solution.py:501
  71.1 11.1 %collective-permute-start.5 = (bf16[384,256]{1,0:T(8,128)(2,1)}, bf16[384,256]{1,0:T(8,128)(2,1)S(1)}, u32[]{:S(2)}, u32[]{:S(2)}) collective-permute-start(bf16[384,256]{1,0:T(8,128)(2,1)} %get-tuple-element.47), channel_id=1, source_target_pairs={{0,3},{1,2},{2,1},{3,0},{4,7},{5,6},{6,5},{7,4},{8,11},{9,10},{10,... | collective-permute-start | bytes 589832 | tf_op jit(solution)/shard_map/ppermute | solution.py:501
  77.4 4.8 %copy-start = (bf16[16,256,256]{2,1,0:T(8,128)(2,1)S(1)}, bf16[16,256,256]{2,1,0:T(8,128)(2,1)}, u32[]{:S(2)}) copy-start(bf16[16,256,256]{2,1,0:T(8,128)(2,1)} %shard_map.188.refs_2_.pre_ref) | copy-start | bytes 6291460
  77.4 4.8 %copy-start.2 = (f32[256,2]{1,0:T(8,128)S(1)}, f32[256,2]{1,0:T(8,128)}, u32[]{:S(2)}) copy-start(f32[256,2]{1,0:T(8,128)} %copy.27.refs_4_.affine_ref) | copy-start | bytes 6148
  77.4 4.8 %copy-start.3 = (bf16[192,96]{1,0:T(8,128)(2,1)S(1)}, bf16[192,96]{1,0:T(8,128)(2,1)}, u32[]{:S(2)}) copy-start(bf16[192,96]{1,0:T(8,128)(2,1)} %w_ref.5) | copy-start | bytes 110596

commit v3 on v2

--- a/solution.py
+++ b/solution.py
@@ -63,7 +63,12 @@
     inv_edge = np.stack(
         [np.block([[inv, none]]), np.block([[cos, -sin, zero, zero], [zero, zero, cos, -sin]])], 0
     )
-    return tuple(bf(t * norm) for t in (pair(fwd), pair(inv), fwd_edge, inv_edge))
+    inv_edge = inv_edge.reshape(2, 2 * MID, 2, 2 * MID).transpose(0, 2, 1, 3).reshape(2, 4 * MID, 2 * MID)
+    tw = twiddles().reshape(2, MID, 2, 2 * LANE).transpose(0, 2, 1, 3).reshape(4 * MID, 2 * LANE)
+    high = bf(tw)
+    low = bf(tw - high.astype(np.float32))
+    pairs = np.stack([bf(pair(fwd) * norm), bf(pair(inv) * norm), high, low], 0)
+    return pairs, bf(fwd_edge * norm), bf(inv_edge * norm)
 
 
 @functools.lru_cache(None)
@@ -178,9 +183,33 @@
     next_ref[LANES:] = ends
 
 
-def halo_body(me_ref, x_ref, next_ref, last_ref, down_ref, up_ref, side_ref):
-    rows, channels, _ = x_ref.shape
-    me = me_ref[0]
+def halo_body(
+    me_ref,
+    z_ref,
+    x_ref,
+    next_ref,
+    last_ref,
+    fw_ref,
+    pair_ref,
+    fwd_edge_ref,
+    inv_edge_ref,
+    down_ref,
+    up_ref,
+    side_ref,
+    kept_ref,
+    sem,
+):
+    rows, channels = side_ref.shape[0] // 2, side_ref.shape[1]
+    me, z = me_ref[0], z_ref[0]
+    loads = [
+        pltpu.make_async_copy(pair_ref, kept_ref.at[pl.ds(0, 4)], sem.at[0]),
+        pltpu.make_async_copy(fwd_edge_ref.at[z], kept_ref.at[4, :, pl.ds(0, 2 * MID)], sem.at[1]),
+        pltpu.make_async_copy(inv_edge_ref.at[z], kept_ref.at[4, :, pl.ds(2 * MID, 2 * MID)], sem.at[2]),
+        pltpu.make_async_copy(x_ref.at[rows - 1], down_ref.at[pl.ds(0, channels)], sem.at[3]),
+        pltpu.make_async_copy(x_ref.at[0], up_ref.at[pl.ds(0, channels)], sem.at[4]),
+    ]
+    for load in loads:
+        load.start()
     odd = lax.rem(me, 2).astype(F32)
     near = next_ref[LANES:].astype(F32)
     far = last_ref[LANES:].astype(F32)
@@ -189,10 +218,13 @@
     right = (odd * far[:rows] + even * near[:rows]) * jnp.where(me < COLS - 1, 1.0, 0.0)
     sides = jnp.concatenate([left, right], 0).astype(BF16)
     side_ref[...] = sides
-    down_ref[:channels] = x_ref[rows - 1]
     down_ref[channels:] = sides
-    up_ref[:channels] = x_ref[0]
     up_ref[channels:] = sides
+    mixer = spread(fw_ref[...].T)
+    low = jnp.zeros((LANE - CF, 2 * LANE), BF16)
+    kept_ref[5] = jnp.concatenate([mixer[:CF], low, mixer[CF:], low], 0)
+    for load in loads:
+        load.wait()
 
 
 def width_near_body(me_ref, t_ref, near_ref, next_ref, o_ref):
@@ -239,27 +271,28 @@
     return jnp.concatenate([t[:, :CF], gap, t[:, CF:], gap], 1)
 
 
-def middle_body(
-    z_ref, d_ref, *refs
-):
-    o_ref = refs[8]
-    wide, back_ref = refs[17], refs[18]
-    held, sem = refs[19], refs[20]
-    z = z_ref[0]
-    tables = refs[9:17]
-    loads = []
-    for i, (source, target) in enumerate(zip(refs[:8], tables)):
-        source = source.at[z] if i in (2, 3) else source
-        loads.append(pltpu.make_async_copy(source, target, sem.at[i]))
-        loads[-1].start()
-    fwd, inv, fwd_edge, inv_edge, tw, fw, scale_row, shift_row = tables
+def middle_body(d_ref, x_ref, scale_ref, shift_ref, o_ref, scale_row, shift_row, tw_ref, edge_ref, wide, back_ref, held, sem):
+    loads = [
+        pltpu.make_async_copy(scale_ref, scale_row, sem.at[0]),
+        pltpu.make_async_copy(shift_ref, shift_row, sem.at[1]),
+    ]
+    for load in loads:
+        load.start()
+    first = 0
     wide[...] = widen(jnp.swapaxes(d_ref[...], 0, 1).reshape(W, LANES))
+    fwd, inv, edges = x_ref.at[first], x_ref.at[first + 1], x_ref.at[first + 4]
+    tw = x_ref[first + 2].astype(F32) + x_ref[first + 3].astype(F32)
+    for i in range(4):
+        half = slice((i % 2) * 2 * LANE, (i % 2 + 1) * 2 * LANE)
+        tw_ref[i // 2, :, half] = tw[i * MID : (i + 1) * MID]
+    twr, twi = tw_ref[0], tw_ref[1]
+    fwd_edge = edges.at[:, : 2 * MID][...]
+    edge_ref[:, : 2 * MID] = edges[: 2 * MID, 2 * MID :]
+    edge_ref[:, 2 * MID :] = edges[2 * MID :, 2 * MID :]
+    inv_edge = edge_ref[...]
+    mixer = x_ref[first + 5]
     for load in loads:
         load.wait()
-    twr, twi = tw[0], tw[1]
-    mixer = spread(fw[...].T)
-    low = jnp.zeros((LANE - CF, 2 * LANE), BF16)
-    mixer = jnp.concatenate([mixer[:CF], low, mixer[CF:], low], 0)
     scale, shift = spread(scale_row[...]), spread(shift_row[...])
     groups = [slice(LANE * r, LANE * r + LANE) for r in range(HS)]
     for own in ((0,), (1, 2), (3, 4), (5, 6), (7,)):
@@ -268,15 +301,17 @@
         )
         count = 2 if own == (0,) else len(own)
         half = 2 * MID * len(own)
-        ahead = fwd_edge[...] if own == (0,) else fwd[:half, :half]
+        ahead = fwd_edge if own == (0,) else fwd[:half, :half]
         u = dot(ahead, data)
         rows = []
         for f in range(count):
             ur = u[2 * f * MID : (2 * f + 1) * MID]
             ui = u[(2 * f + 1) * MID : (2 * f + 2) * MID]
-            vr = ur * twr - ui * twi
-            vi = ur * twi + ui * twr
-            for real, imag in turns([vr[:, g] for g in groups], [vi[:, g] for g in groups]):
+            vr, vi = [ur[:, groups[0]]], [ui[:, groups[0]]]
+            for g in groups[1:]:
+                vr.append(ur[:, g] * twr[:, g] - ui[:, g] * twi[:, g])
+                vi.append(ur[:, g] * twi[:, g] + ui[:, g] * twr[:, g])
+            for real, imag in turns(vr, vi):
                 rows.append(jnp.concatenate([real, imag], 1).astype(BF16))
         mixed = dot(jnp.concatenate(rows, 0), mixer)
         active = jnp.maximum(scale * mixed + shift, 0.0)
@@ -284,11 +319,13 @@
         for f in range(count):
             part = [active[(HS * f + j) * MID : (HS * f + j + 1) * MID] for j in (0, 3, 2, 1)]
             turned = turns([v[:, :LANE] for v in part], [v[:, LANE:] for v in part])
-            br = jnp.concatenate([v[0] for v in turned], 1)
-            bi = jnp.concatenate([v[1] for v in turned], 1)
-            rows.append((br * twr + bi * twi).astype(BF16))
-            rows.append((bi * twr - br * twi).astype(BF16))
-        behind = inv_edge[...] if own == (0,) else inv[:half, :half]
+            br, bi = [turned[0][0].astype(BF16)], [turned[0][1].astype(BF16)]
+            for g, (real, imag) in zip(groups[1:], turned[1:]):
+                br.append((real * twr[:, g] + imag * twi[:, g]).astype(BF16))
+                bi.append((imag * twr[:, g] - real * twi[:, g]).astype(BF16))
+            rows.append(jnp.concatenate(br, 1))
+            rows.append(jnp.concatenate(bi, 1))
+        behind = inv_edge if own == (0,) else inv[:half, :half]
         done = narrow(dot(behind, jnp.concatenate(rows, 0)).astype(BF16))
         for i, f in enumerate(own):
             for p in range(2):
@@ -304,17 +341,10 @@
         store.wait()
 
 
-def inverse_body(pieces, me_ref, t_ref, d_ref, *refs):
-    count = len(pieces)
-    table, sem = refs[count:]
-    loads = []
-    for i, s in enumerate(pieces):
-        loads.append(pltpu.make_async_copy(t_ref.at[lax.bitwise_xor(me_ref[0], s)], table.at[i], sem.at[i]))
-        loads[-1].start()
+def inverse_body(t_ref, d_ref, *outs):
     data = d_ref[...].T
-    for i in range(count):
-        loads[i].wait()
-        refs[i][...] = dot(data, table[i]).astype(BF16)
+    for i, o_ref in enumerate(outs):
+        o_ref[...] = dot(data, t_ref[i]).astype(BF16)
 
 
 def conv_setup(fl_ref, fg_ref, wl_ref, wg_ref):
@@ -377,8 +407,10 @@
 
 
 def conv_inner_body(
-    x_ref, fl_ref, fg_ref, wm_ref, ws_ref, affine_ref, out_ref, o_ref, edge, wl_ref, wg_ref, sem
+    x_ref, fl_ref, fg_ref, wm_ref, ws_ref, affine_ref, out_ref, kept_ref, o_ref, edge, wl_ref, wg_ref, sem
 ):
+    keep = pltpu.make_async_copy(x_ref, kept_ref, sem.at[1])
+    keep.start()
     conv_setup(fl_ref, fg_ref, wl_ref, wg_ref)
     edge[...] = jnp.zeros_like(edge)
 
@@ -390,6 +422,7 @@
     lax.fori_loop(1, SPLIT, step, 0)
     done = pl.ds(1, SPLIT - 1)
     pltpu.make_async_copy(o_ref.at[done], out_ref.at[done], sem.at[0]).wait()
+    keep.wait()
 
 
 def conv_outer_body(
@@ -403,7 +436,10 @@
     above_ref,
     below_ref,
     given_ref,
+    table_ref,
+    me_ref,
     out_ref,
+    kept_ref,
     o_ref,
     cols,
     edge,
@@ -415,6 +451,11 @@
     inner = pl.ds(1, SPLIT - 1)
     load = pltpu.make_async_copy(given_ref.at[inner], o_ref.at[inner], sem.at[1])
     load.start()
+    keeps = []
+    for i, s in enumerate((2, 3, 1)):
+        source = table_ref.at[lax.bitwise_xor(me_ref[0], s)]
+        keeps.append(pltpu.make_async_copy(source, kept_ref.at[i], sem.at[2 + i]))
+        keeps[-1].start()
     conv_setup(fl_ref, fg_ref, wl_ref, wg_ref)
     conv_edges(side_ref, (above_ref, below_ref), wl_ref, wg_ref, cols, edge)
     rest = (wl_ref, wg_ref, wm_ref, ws_ref, affine_ref, edge, o_ref, out_ref, sem)
@@ -440,6 +481,8 @@
     for done in (pl.ds(SPLIT, rows - SPLIT), pl.ds(0, 1)):
         pltpu.make_async_copy(o_ref.at[done], out_ref.at[done], sem.at[0]).wait()
     store.wait()
+    for keep in keeps:
+        keep.wait()
 
 
 def final_rows(pieces, me_ref, x_ref, pre_ref, w_ref, affine_ref, o_ref, finish=None):
@@ -465,17 +508,39 @@
             finish(k, span)
 
 
-def final_near_body(me_ref, x_ref, pre_ref, w_ref, affine_ref, t_ref, d_ref, next_ref, o_ref, table, sem):
-    load = pltpu.make_async_copy(t_ref.at[me_ref[0]], table, sem.at[0])
+def fetch_rows(x_ref, pre_ref, first, count, x, pre, sem):
+    span = pl.ds(first, count)
+    loads = [
+        pltpu.make_async_copy(x_ref.at[span], x.at[span], sem.at[0]),
+        pltpu.make_async_copy(pre_ref.at[span], pre.at[span], sem.at[1]),
+    ]
+    for load in loads:
+        load.start()
+    return loads
+
+
+def final_near_body(
+    me_ref, x_ref, pre_ref, w_ref, scale_ref, shift_ref, t_ref, d_ref, next_ref, o_ref, affine_ref, x, pre, table, sem
+):
+    me = me_ref[0]
+    load = pltpu.make_async_copy(t_ref.at[me], table, sem.at[2])
     load.start()
+    loads = fetch_rows(x_ref, pre_ref, 2 * HS * (me // 2), 2 * HS, x, pre, sem)
+    affine_ref[:, 0:1] = column(scale_ref[...])
+    affine_ref[:, 1:2] = column(shift_ref[...])
     data = d_ref[...].T
     load.wait()
     near = dot(data, table[...]).astype(BF16)
-    final_rows(((0, near), (1, next_ref)), me_ref, x_ref, pre_ref, w_ref, affine_ref, o_ref)
-
-
-def final_far_body(me_ref, x_ref, pre_ref, w_ref, affine_ref, far_ref, given_ref, o_ref):
-    final_rows(((2, far_ref),), me_ref, x_ref, pre_ref, w_ref, affine_ref, o_ref)
+    for load in loads:
+        load.wait()
+    final_rows(((0, near), (1, next_ref)), me_ref, x, pre, w_ref, affine_ref, o_ref)
+
+
+def final_far_body(me_ref, x_ref, pre_ref, w_ref, affine_ref, far_ref, given_ref, o_ref, x, pre, sem):
+    loads = fetch_rows(x_ref, pre_ref, HS * lax.bitwise_xor(me_ref[0], 2), HS, x, pre, sem)
+    for load in loads:
+        load.wait()
+    final_rows(((2, far_ref),), me_ref, x, pre, w_ref, affine_ref, o_ref)
 
 
 def final_last_body(me_ref, x_ref, pre_ref, w_ref, affine_ref, last_ref, given_ref, o_ref, out_ref, held, sem):
@@ -556,13 +621,13 @@
         pltpu.VMEM((2, channels, LANE), F32),
         pltpu.VMEM((3 * channels, 3 * cl), BF16),
         pltpu.VMEM((3 * cl, 3 * cg), BF16),
-        dma((2,)),
+        dma((5,)),
     ]
-    pre = call(
+    pre, x = call(
         conv_inner_body,
-        whole,
+        (whole, whole),
         (x,) + weights,
-        hbm_out=(0,),
+        hbm_out=(0, 1),
         stage=tuple(range(1, 6)),
         flops=10**9,
         scratch=scratch[:1] + scratch[2:],
@@ -583,24 +648,30 @@
         spectra.reshape(PEERS, 2 * NF, LANES), ("row", "col"), split_axis=0, concat_axis=0, tiled=True
     )
     ends = shape((channels + 2 * rows, width), BF16)
-    down, up, sides = call(
-        halo_body, (ends, ends, shape((2 * rows, channels), BF16)), (me, x, other, last), smem=(0,)
+    pairs, fwd_edge, inv_edge = (jnp.asarray(t) for t in height_tables())
+    down, up, sides, kept = call(
+        halo_body,
+        (ends, ends, shape((2 * rows, channels), BF16), shape((6, channels, width), BF16)),
+        (me, z, x, other, last, fourier_weight, pairs, fwd_edge, inv_edge),
+        smem=(0, 1),
+        hbm=(2, 6, 7, 8),
+        stage=(5,),
+        scratch=[dma((5,))],
     )
     above, below = shift_along(down, "row", 1), shift_along(up, "row", -1)
 
-    tables = [jnp.asarray(t) for t in height_tables() + (twiddles(),)]
-    tables += [fourier_weight, fourier_scale[None], fourier_shift[None]]
-    sizes = [t.shape[1:] if i in (2, 3) else t.shape for i, t in enumerate(tables)]
     returned = call(
         middle_body,
         shape((PEERS, 2 * NF, LANES), BF16),
-        (z, spectra, *tables),
-        smem=(0,),
-        hbm=range(2, 10),
+        (spectra, kept, fourier_scale[None], fourier_shift[None]),
+        hbm=(2, 3),
         hbm_out=(0,),
         limit=24,
-        scratch=[pltpu.VMEM(s, t.dtype) for s, t in zip(sizes, tables)]
-        + [
+        scratch=[
+            pltpu.VMEM((1, 2 * CF), F32),
+            pltpu.VMEM((1, 2 * CF), F32),
+            pltpu.VMEM((2, MID, WIDE), F32),
+            pltpu.VMEM((2 * MID, 4 * MID), BF16),
             pltpu.VMEM((W, WIDE), BF16),
             pltpu.VMEM((2 * NF, MID, LANES), BF16),
             pltpu.VMEM((PEERS, 2 * NF, LANES), BF16),
@@ -609,42 +680,41 @@
     )
     returned, above, below = after(returned, above, below)
     returned = lax.all_to_all(returned, ("row", "col"), split_axis=0, concat_axis=0, tiled=True).reshape(W, LANES)
-    pre = call(
+    pre, table = call(
         conv_outer_body,
-        whole,
-        (x, sides) + weights + (above, below, pre),
-        hbm=(9,),
+        (whole, shape((3, W, width), BF16)),
+        (x, sides) + weights + (above, below, pre, inv_w, me),
+        smem=(11,),
+        hbm=(9, 10),
         hbm_out=(0,),
-        stage=tuple(range(1, 9)),
+        stage=tuple(range(7)),
         flops=10**9,
         input_output_aliases={9: 0},
         scratch=scratch,
     )
-    returned, pre = after(returned, pre)
 
     piece = shape((LANES, width), BF16)
-    affine = jnp.stack([out_scale, out_shift], 1)
-    far, last, other = call(
-        functools.partial(inverse_body, (2, 3, 1)),
-        (piece,) * 3,
-        (me, inv_w, returned),
+    far, last, other = call(inverse_body, (piece,) * 3, (table, returned))
+    far, last, other = swap(far, 2), swap(last, 3), swap(other, 1)
+    rows_held = [pltpu.VMEM(whole.shape, BF16), pltpu.VMEM(whole.shape, BF16)]
+    half, affine = call(
+        final_near_body,
+        (whole, shape((channels, 2), F32)),
+        (me, x, pre, mix_weight, out_scale[None], out_shift[None], inv_w, returned, other),
         smem=(0,),
-        hbm=(1,),
-        scratch=[pltpu.VMEM((3, W, width), BF16), dma((3,))],
-    )
-    far, last, other = swap(far, 2), swap(last, 3), swap(other, 1)
+        hbm=(1, 2, 6),
+        stage=(3, 4, 5),
+        scratch=rows_held + [pltpu.VMEM((W, width), BF16), dma((3,))],
+    )
     common = (me, x, pre, mix_weight, affine)
     half = call(
-        final_near_body,
+        final_far_body,
         whole,
-        common + (inv_w, returned, other),
+        common + (far, half),
         smem=(0,),
-        hbm=(5,),
-        stage=(2, 3, 4),
-        scratch=[pltpu.VMEM((W, width), BF16), dma((1,))],
-    )
-    half = call(
-        final_far_body, whole, common + (far, half), smem=(0,), stage=(2, 3, 4), input_output_aliases={6: 0}
+        hbm=(1, 2),
+        input_output_aliases={6: 0},
+        scratch=rows_held + [dma((2,))],
     )
     _, result = call(
         final_last_body,

time: 84.9 us -> 81.6 us (0.961)
  Pallas kernels: 36.7 us -> 34.5 us
    pallas_call x12, Pallas kernels: 36.7 us -> 34.5 us  [call(): pl.pallas_call(body, out_shape=shapes[0] if single else tuple(shapes), in...]
    ppermute x6, waiting for transfers between devices: 4.81 us -> 6.3 us  [swap(): return lax.ppermute(block, 'col', [(i, i ^ s) for i in range(COLS)])]
    all_to_all x1, waiting for transfers between devices: 9.64 us -> 8.21 us  [per_device(): lax.all_to_all(spectra.reshape(PEERS, 2 * NF, LANES), ('row', 'col'), spl...]
  transfers between devices with their start and end apart: 10 -> 10, of which waited for: 5 -> 5; matrix products, arithmetic and copies ran while one was open for 1% -> 0% of each run, Pallas kernels for 32% -> 34%
where the time goes in v3:
time: 81.6 us; the launch traced here: 81 us
  Pallas kernels  34.5 us (42%)
  starting transfers between devices  24.5 us (30%)
  waiting for transfers between devices  21 us (26%)
    pallas_call x12, Pallas kernels, call(): pl.pallas_call(body, out_shape=shapes[0] if single else tuple(shapes), in...  34.5 us
    all_to_all x1, starting transfers between devices, per_device(): lax.all_to_all(spectra.reshape(PEERS, 2 * NF, LANES), ('row', 'col'), spl...  10.4 us
    all_to_all x1, waiting for transfers between devices, per_device(): lax.all_to_all(spectra.reshape(PEERS, 2 * NF, LANES), ('row', 'col'), spl...  8.21 us
    all_to_all x1, waiting for transfers between devices, per_device(): lax.all_to_all(returned, ('row', 'col'), split_axis=0, concat_axis=0, til...  6.45 us
    ppermute x6, waiting for transfers between devices, swap(): return lax.ppermute(block, 'col', [(i, i ^ s) for i in range(COLS)])  6.3 us
    ppermute x6, starting transfers between devices, swap(): return lax.ppermute(block, 'col', [(i, i ^ s) for i in range(COLS)])  5.32 us
    ppermute x2, starting transfers between devices, shift_along(): return lax.ppermute(block, axis, pairs)  4.58 us
    all_to_all x1, starting transfers between devices, per_device(): lax.all_to_all(returned, ('row', 'col'), split_axis=0, concat_axis=0, til...  4.25 us
  transfers between devices with their start and end apart: 10, of which 5 were waited for; matrix products, arithmetic and copies ran while one was open for 0% of the time, Pallas kernels for 34%

profile of v3, /device:TPU:1, one launch (start us, length us, event | category | flops | bytes accessed | tf_op | source)
XLA Modules:
  0.0 81.0 jit_solution(6808165823416812252)
XLA Ops:
  0.0 1.9 %shard_map.163 = (bf16[16,256,256]{2,1,0:T(8,128)(2,1)S(1)}, bf16[384,256]{1,0:T(8,128)(2,1)S(1)}, f32[96,2]{1,0:T(8,128)S(1)}) custom-call(s32[1]{0:T(128)} %bitcast.me_ref.refs_0_.refs_11_, bf16[256,16,256]{2,1,0:T(8,128)(2,1)} %image_ref.1, bf16[96,192]{1,0:T(8,128)(2,1)} %refs_5_.3, f32[1,96]{1,0:T(1,128)} %bitcast.20, f32[1,96]{1,0:T(1,128)} %bitcast.21), custom_call_target="tpu_custom_call" | custom-call | flops 1000000 | bytes 1000 | tf_op jit(solution)/shard_map/pallas_call | solution.py:117
  2.0 0.9 %shard_map.165 = (bf16[384,256]{1,0:T(8,128)(2,1)S(1)}, bf16[416,256]{1,0:T(8,128)(2,1)S(1)}, bf16[416,256]{1,0:T(8,128)(2,1)S(1)}) custom-call(s32[1]{0:T(128)} %bitcast.me_ref.refs_0_.refs_11_, bf16[16,256,256]{2,1,0:T(8,128)(2,1)S(1)} %get-tuple-element.33.refs_0_.x_ref, bf16[96,192]{1,0:T(8,128)(2,1)S(1)} %copy-done.4, ...), custom_call_target="tpu_custom_call" | custom-call | flops 1000000 | bytes 1000 | tf_op jit(solution)/shard_map/pallas_call | solution.py:117
  2.9 1.5 %collective-permute-start = (bf16[416,256]{1,0:T(8,128)(2,1)S(1)}, bf16[416,256]{1,0:T(8,128)(2,1)S(1)}, u32[]{:S(2)}, u32[]{:S(2)}) collective-permute-start(bf16[416,256]{1,0:T(8,128)(2,1)S(1)} %get-tuple-element.37), channel_id=1, source_target_pairs={{0,1},{1,0},{2,3},{3,2},{4,5},{5,4},{6,7},{7,6},{8,9},{9,8},{10,11... | collective-permute-start | bytes 638984 | tf_op jit(solution)/shard_map/ppermute | solution.py:566
  4.4 1.4 %collective-permute-start.2 = (bf16[416,256]{1,0:T(8,128)(2,1)S(1)}, bf16[416,256]{1,0:T(8,128)(2,1)S(1)}, u32[]{:S(2)}, u32[]{:S(2)}) collective-permute-start(bf16[416,256]{1,0:T(8,128)(2,1)S(1)} %get-tuple-element.41), channel_id=1, source_target_pairs={{0,3},{1,2},{2,1},{3,0},{4,7},{5,6},{6,5},{7,4},{8,11},{9,10},{10,... | collective-permute-start | bytes 638984 | tf_op jit(solution)/shard_map/ppermute | solution.py:566
  5.8 6.3 %shard_map.164 = (bf16[16,256,256]{2,1,0:T(8,128)(2,1)}, bf16[16,256,256]{2,1,0:T(8,128)(2,1)}) custom-call(bf16[16,256,256]{2,1,0:T(8,128)(2,1)S(1)} %get-tuple-element.33.refs_0_.x_ref, bf16[9,64,256]{2,1,0:T(8,128)(2,1)} %bitcast.14, bf16[9,64,192]{2,1,0:T(8,128)(2,1)} %refs_3_.4, bf16[192,96]{1,0:T(8,128)(2,1)} %w_ref.7, bf16[96,192]{1,0:T(8,128)(2,1)} %refs_5_.3, ...), custom_call_target="tpu_custom_call" | custom-call | flops 1000000000 | bytes 1000000 | tf_op jit(solution)/shard_map/pallas_call | solution.py:117
  12.2 0.7 shard_map.166.part_ref
  12.9 2.4 %collective-permute-done.1.far_ref = bf16[384,256]{1,0:T(8,128)(2,1)S(1)} collective-permute-done((bf16[384,256]{1,0:T(8,128)(2,1)S(1)}, bf16[384,256]{1,0:T(8,128)(2,1)S(1)}, u32[]{:S(2)}, u32[]{:S(2)}) %collective-permute-start.1) | collective-permute-done | bytes 196640 | tf_op jit(solution)/shard_map/ppermute | solution.py:566
  15.3 1.4 %shard_map.167 = bf16[1024,384]{1,0:T(8,128)(2,1)} custom-call(s32[1]{0:T(128)} %bitcast.me_ref.refs_0_.refs_11_, bf16[4,1024,256]{2,1,0:T(8,128)(2,1)S(1)} %copy-done.2, f32[1024,384]{1,0:T(8,128)S(1)} %shard_map.166.part_ref, bf16[384,256]{1,0:T(8,128)(2,1)S(1)} %collective-permute-done.1.far_ref, bf16[416,256]{1,0:T(8,128)(2,1)S(1)} %collective-permute-done.2.last_ref.refs_4_), custom_call_target="tpu_custom_call" | custom-call | flops 1000000 | bytes 1000 | tf_op jit(solution)/shard_map/pallas_call | solution.py:117
  16.7 10.4 %all-to-all-start = ((bf16[64,16,384]{2,1,0:T(8,128)(2,1)}), bf16[64,16,384]{2,1,0:T(8,128)(2,1)S(1)}, u32[]{:S(2)}, u32[]{:S(2)}) async-start(bf16[64,16,384]{2,1,0:T(8,128)(2,1)} %bitcast.13), calls=%async_computation | async-start | bytes 1572864 | tf_op jit(solution)/shard_map/all_to_all | solution.py:647
  27.2 2.1 %shard_map.168 = (bf16[288,256]{1,0:T(8,128)(2,1)S(1)}, bf16[288,256]{1,0:T(8,128)(2,1)S(1)}, bf16[32,256]{1,0:T(8,128)(2,1)S(1)}, bf16[6,256,256]{2,1,0:T(8,128)(2,1)S(1)}) custom-call(s32[1]{0:T(128)} %bitcast.me_ref.refs_0_.refs_11_, s32[1]{0:T(128)} %bitcast.4.refs_1_, bf16[16,256,256]{2,1,0:T(8,128)(2,1)} %get-tuple-element.35.refs_2_.refs_0_.refs_1_.x_ref, ...), custom_call_target="tpu_custom_call" | custom-call | flops 1000000 | bytes 1000 | tf_op jit(solution)/shard_map/pallas_call | solution.py:117
  29.9 3.3 %collective-permute-start.3 = (bf16[288,256]{1,0:T(8,128)(2,1)S(1)}, bf16[288,256]{1,0:T(8,128)(2,1)S(1)}, u32[]{:S(2)}, u32[]{:S(2)}) collective-permute-start(bf16[288,256]{1,0:T(8,128)(2,1)S(1)} %get-tuple-element.47), channel_id=1, source_target_pairs={{0,4},{4,8},{8,12},{12,16},{16,20},{20,24},{24,28},{28,32},{32,36}... | collective-permute-start | bytes 442376 | tf_op jit(solution)/shard_map/ppermute | solution.py:562
  33.1 1.3 %collective-permute-start.4 = (bf16[288,256]{1,0:T(8,128)(2,1)S(1)}, bf16[288,256]{1,0:T(8,128)(2,1)S(1)}, u32[]{:S(2)}, u32[]{:S(2)}) collective-permute-start(bf16[288,256]{1,0:T(8,128)(2,1)S(1)} %get-tuple-element.48), channel_id=1, source_target_pairs={{4,0},{8,4},{12,8},{16,12},{20,16},{24,20},{28,24},{32,28},{36,32}... | collective-permute-start | bytes 442376 | tf_op jit(solution)/shard_map/ppermute | solution.py:562
  34.4 8.2 %all-to-all-done.d_ref = bf16[64,16,384]{2,1,0:T(8,128)(2,1)S(1)} async-done(((bf16[64,16,384]{2,1,0:T(8,128)(2,1)}), bf16[64,16,384]{2,1,0:T(8,128)(2,1)S(1)}, u32[]{:S(2)}, u32[]{:S(2)}) %all-to-all-start) | async-done | bytes 786464 | tf_op jit(solution)/shard_map/all_to_all | solution.py:647
  42.7 4.6 %shard_map.169 = bf16[64,16,384]{2,1,0:T(8,128)(2,1)} custom-call(bf16[64,16,384]{2,1,0:T(8,128)(2,1)S(1)} %all-to-all-done.d_ref, bf16[6,256,256]{2,1,0:T(8,128)(2,1)S(1)} %get-tuple-element.46.x_ref, f32[1,192]{1,0:T(1,128)} %bitcast.16, f32[1,192]{1,0:T(1,128)} %bitcast.17), custom_call_target="tpu_custom_call" | custom-call | flops 1000000 | bytes 1000 | tf_op jit(solution)/shard_map/pallas_call | solution.py:117
  47.2 4.2 %all-to-all-start.1 = ((bf16[64,16,384]{2,1,0:T(8,128)(2,1)}), bf16[64,16,384]{2,1,0:T(8,128)(2,1)S(1)}, u32[]{:S(2)}, u32[]{:S(2)}) async-start(bf16[64,16,384]{2,1,0:T(8,128)(2,1)} %shard_map.169), calls=%async_computation.1 | async-start | bytes 1572864 | tf_op jit(solution)/shard_map/all_to_all | solution.py:682
  51.5 8.8 %shard_map.170 = (bf16[16,256,256]{2,1,0:T(8,128)(2,1)}, bf16[3,1024,256]{2,1,0:T(8,128)(2,1)S(1)}) custom-call(bf16[16,256,256]{2,1,0:T(8,128)(2,1)} %get-tuple-element.35.refs_2_.refs_0_.refs_1_.x_ref, bf16[32,256]{1,0:T(8,128)(2,1)} %copy-done.6, bf16[9,64,256]{2,1,0:T(8,128)(2,1)} %bitcast.15, ...), custom_call_target="tpu_custom_call", output_to_operand_aliasing={{0}: (9, {})} | custom-call | flops 1000000000 | bytes 1000000 | tf_op jit(solution)/shard_map/pallas_call | solution.py:117
  60.3 6.5 %all-to-all-done.1 = bf16[64,16,384]{2,1,0:T(8,128)(2,1)S(1)} async-done(((bf16[64,16,384]{2,1,0:T(8,128)(2,1)}), bf16[64,16,384]{2,1,0:T(8,128)(2,1)S(1)}, u32[]{:S(2)}, u32[]{:S(2)}) %all-to-all-start.1) | async-done | bytes 786464 | tf_op jit(solution)/shard_map/all_to_all | solution.py:682
  66.8 0.8 %shard_map.171 = (bf16[384,256]{1,0:T(8,128)(2,1)S(1)}, bf16[384,256]{1,0:T(8,128)(2,1)S(1)}, bf16[384,256]{1,0:T(8,128)(2,1)S(1)}) custom-call(bf16[3,1024,256]{2,1,0:T(8,128)(2,1)S(1)} %get-tuple-element.54.t_ref, bf16[1024,384]{1,0:T(8,128)(2,1)S(1)} %bitcast.11), custom_call_target="tpu_custom_call" | custom-call | flops 1000000 | bytes 1000 | tf_op jit(solution)/shard_map/pallas_call | solution.py:117
  68.1 1.9 %collective-permute-start.6 = (bf16[384,256]{1,0:T(8,128)(2,1)S(1)}, bf16[384,256]{1,0:T(8,128)(2,1)S(1)}, u32[]{:S(2)}, u32[]{:S(2)}) collective-permute-start(bf16[384,256]{1,0:T(8,128)(2,1)S(1)} %get-tuple-element.57), channel_id=1, source_target_pairs={{0,3},{1,2},{2,1},{3,0},{4,7},{5,6},{6,5},{7,4},{8,11},{9,10},{10,... | collective-permute-start | bytes 589832 | tf_op jit(solution)/shard_map/ppermute | solution.py:566
  70.0 3.3 %shard_map.172 = (bf16[16,256,256]{2,1,0:T(8,128)(2,1)S(1)}, f32[256,2]{1,0:T(8,128)S(1)}) custom-call(s32[1]{0:T(128)} %bitcast.me_ref.refs_0_.refs_11_, bf16[16,256,256]{2,1,0:T(8,128)(2,1)} %get-tuple-element.35.refs_2_.refs_0_.refs_1_.x_ref, bf16[16,256,256]{2,1,0:T(8,128)(2,1)} %get-tuple-element.52.refs_2_.pre_ref, bf16[192,96]{1,0:T(8,128)(2,1)} %w_ref.7, ...), custom_call_target="tpu_custom_call" | custom-call | flops 1000000 | bytes 1000 | tf_op jit(solution)/shard_map/pallas_call | solution.py:117
  73.2 1.1 %collective-permute-done.7.far_ref = bf16[384,256]{1,0:T(8,128)(2,1)S(1)} collective-permute-done((bf16[384,256]{1,0:T(8,128)(2,1)S(1)}, bf16[384,256]{1,0:T(8,128)(2,1)S(1)}, u32[]{:S(2)}, u32[]{:S(2)}) %collective-permute-start.7) | collective-permute-done | bytes 196640 | tf_op jit(solution)/shard_map/ppermute | solution.py:566
  74.3 1.7 %shard_map.173.given_ref = bf16[16,256,256]{2,1,0:T(8,128)(2,1)S(1)} custom-call(s32[1]{0:T(128)} %bitcast.me_ref.refs_0_.refs_11_, bf16[16,256,256]{2,1,0:T(8,128)(2,1)} %get-tuple-element.35.refs_2_.refs_0_.refs_1_.x_ref, bf16[16,256,256]{2,1,0:T(8,128)(2,1)} %get-tuple-element.52.refs_2_.pre_ref, ...), custom_call_target="tpu_custom_call", output_to_operand_aliasing={{}: (6, {})} | custom-call | flops 1000000 | bytes 1000 | tf_op jit(solution)/shard_map/pallas_call | solution.py:117
  76.0 2.9 %collective-permute-done.6.last_ref = bf16[384,256]{1,0:T(8,128)(2,1)S(1)} collective-permute-done((bf16[384,256]{1,0:T(8,128)(2,1)S(1)}, bf16[384,256]{1,0:T(8,128)(2,1)S(1)}, u32[]{:S(2)}, u32[]{:S(2)}) %collective-permute-start.6) | collective-permute-done | bytes 196640 | tf_op jit(solution)/shard_map/ppermute | solution.py:566
  78.9 1.9 %shard_map.174 = (bf16[16,256,256]{2,1,0:T(8,128)(2,1)S(1)}, bf16[256,16,256]{2,1,0:T(8,128)(2,1)}) custom-call(s32[1]{0:T(128)} %bitcast.me_ref.refs_0_.refs_11_, bf16[16,256,256]{2,1,0:T(8,128)(2,1)S(1)} %copy-done, bf16[16,256,256]{2,1,0:T(8,128)(2,1)S(1)} %copy-done.1, bf16[192,96]{1,0:T(8,128)(2,1)S(1)} %copy-done.3, ...), custom_call_target="tpu_custom_call", output_to_operand_aliasing={{0}: (6, {})} | custom-call | flops 1000000 | bytes 1000 | tf_op jit(solution)/shard_map/pallas_call | solution.py:117
  (22 shorter events, 1.2 us)
Async XLA Ops:
  0.0 2.0 %copy-start.4 = (bf16[96,192]{1,0:T(8,128)(2,1)S(1)}, bf16[96,192]{1,0:T(8,128)(2,1)}, u32[]{:S(2)}) copy-start(bf16[96,192]{1,0:T(8,128)(2,1)} %refs_5_.3) | copy-start | bytes 110596
  2.0 3.9 %copy-start.5 = (f32[96,2]{1,0:T(8,128)}, f32[96,2]{1,0:T(8,128)S(1)}, u32[]{:S(2)}) copy-start(f32[96,2]{1,0:T(8,128)S(1)} %get-tuple-element.34.refs_5_.affine_ref.refs_6_) | copy-start | bytes 2308
  2.9 9.3 %copy-start.2 = (bf16[4,1024,256]{2,1,0:T(8,128)(2,1)S(1)}, bf16[4,1024,256]{2,1,0:T(8,128)(2,1)}, u32[]{:S(2)}) copy-start(bf16[4,1024,256]{2,1,0:T(8,128)(2,1)} %constant.21.clone.t_ref) | copy-start | bytes 6291460
  2.9 9.3 %collective-permute-start = (bf16[416,256]{1,0:T(8,128)(2,1)S(1)}, bf16[416,256]{1,0:T(8,128)(2,1)S(1)}, u32[]{:S(2)}, u32[]{:S(2)}) collective-permute-start(bf16[416,256]{1,0:T(8,128)(2,1)S(1)} %get-tuple-element.37), channel_id=1, source_target_pairs={{0,1},{1,0},{2,3},{3,2},{4,5},{5,4},{6,7},{7,6},{8,9},{9,8},{10,11... | collective-permute-start | bytes 638984 | tf_op jit(solution)/shard_map/ppermute | solution.py:566
  4.4 10.9 %collective-permute-start.2 = (bf16[416,256]{1,0:T(8,128)(2,1)S(1)}, bf16[416,256]{1,0:T(8,128)(2,1)S(1)}, u32[]{:S(2)}, u32[]{:S(2)}) collective-permute-start(bf16[416,256]{1,0:T(8,128)(2,1)S(1)} %get-tuple-element.41), channel_id=1, source_target_pairs={{0,3},{1,2},{2,1},{3,0},{4,7},{5,6},{6,5},{7,4},{8,11},{9,10},{10,... | collective-permute-start | bytes 638984 | tf_op jit(solution)/shard_map/ppermute | solution.py:566
  5.7 9.5 %collective-permute-start.1 = (bf16[384,256]{1,0:T(8,128)(2,1)S(1)}, bf16[384,256]{1,0:T(8,128)(2,1)S(1)}, u32[]{:S(2)}, u32[]{:S(2)}) collective-permute-start(bf16[384,256]{1,0:T(8,128)(2,1)S(1)} %get-tuple-element.40), channel_id=1, source_target_pairs={{0,2},{1,3},{2,0},{3,1},{4,6},{5,7},{6,4},{7,5},{8,10},{9,11},{10,... | collective-permute-start | bytes 589832 | tf_op jit(solution)/shard_map/ppermute | solution.py:566
  16.7 25.9 %all-to-all-start = ((bf16[64,16,384]{2,1,0:T(8,128)(2,1)}), bf16[64,16,384]{2,1,0:T(8,128)(2,1)S(1)}, u32[]{:S(2)}, u32[]{:S(2)}) async-start(bf16[64,16,384]{2,1,0:T(8,128)(2,1)} %bitcast.13), calls=%async_computation | async-start | bytes 1572864 | tf_op jit(solution)/shard_map/all_to_all | solution.py:647
  29.3 0.6 copy-start.6
  29.9 17.4 %collective-permute-start.3 = (bf16[288,256]{1,0:T(8,128)(2,1)S(1)}, bf16[288,256]{1,0:T(8,128)(2,1)S(1)}, u32[]{:S(2)}, u32[]{:S(2)}) collective-permute-start(bf16[288,256]{1,0:T(8,128)(2,1)S(1)} %get-tuple-element.47), channel_id=1, source_target_pairs={{0,4},{4,8},{8,12},{12,16},{16,20},{20,24},{24,28},{28,32},{32,36}... | collective-permute-start | bytes 442376 | tf_op jit(solution)/shard_map/ppermute | solution.py:562
  33.1 14.1 %collective-permute-start.4 = (bf16[288,256]{1,0:T(8,128)(2,1)S(1)}, bf16[288,256]{1,0:T(8,128)(2,1)S(1)}, u32[]{:S(2)}, u32[]{:S(2)}) collective-permute-start(bf16[288,256]{1,0:T(8,128)(2,1)S(1)} %get-tuple-element.48), channel_id=1, source_target_pairs={{4,0},{8,4},{12,8},{16,12},{20,16},{24,20},{28,24},{32,28},{36,32}... | collective-permute-start | bytes 442376 | tf_op jit(solution)/shard_map/ppermute | solution.py:562
  47.2 19.5 %all-to-all-start.1 = ((bf16[64,16,384]{2,1,0:T(8,128)(2,1)}), bf16[64,16,384]{2,1,0:T(8,128)(2,1)S(1)}, u32[]{:S(2)}, u32[]{:S(2)}) async-start(bf16[64,16,384]{2,1,0:T(8,128)(2,1)} %shard_map.169), calls=%async_computation.1 | async-start | bytes 1572864 | tf_op jit(solution)/shard_map/all_to_all | solution.py:682
  67.6 2.4 %collective-permute-start.5 = (bf16[384,256]{1,0:T(8,128)(2,1)S(1)}, bf16[384,256]{1,0:T(8,128)(2,1)S(1)}, u32[]{:S(2)}, u32[]{:S(2)}) collective-permute-start(bf16[384,256]{1,0:T(8,128)(2,1)S(1)} %get-tuple-element.55), channel_id=1, source_target_pairs={{0,1},{1,0},{2,3},{3,2},{4,5},{5,4},{6,7},{7,6},{8,9},{9,8},{10,11... | collective-permute-start | bytes 589832 | tf_op jit(solution)/shard_map/ppermute | solution.py:566
  68.1 6.2 %collective-permute-start.7 = (bf16[384,256]{1,0:T(8,128)(2,1)S(1)}, bf16[384,256]{1,0:T(8,128)(2,1)S(1)}, u32[]{:S(2)}, u32[]{:S(2)}) collective-permute-start(bf16[384,256]{1,0:T(8,128)(2,1)S(1)} %get-tuple-element.58), channel_id=1, source_target_pairs={{0,2},{1,3},{2,0},{3,1},{4,6},{5,7},{6,4},{7,5},{8,10},{9,11},{10,... | collective-permute-start | bytes 589832 | tf_op jit(solution)/shard_map/ppermute | solution.py:566
  68.1 10.8 %collective-permute-start.6 = (bf16[384,256]{1,0:T(8,128)(2,1)S(1)}, bf16[384,256]{1,0:T(8,128)(2,1)S(1)}, u32[]{:S(2)}, u32[]{:S(2)}) collective-permute-start(bf16[384,256]{1,0:T(8,128)(2,1)S(1)} %get-tuple-element.57), channel_id=1, source_target_pairs={{0,3},{1,2},{2,1},{3,0},{4,7},{5,6},{6,5},{7,4},{8,11},{9,10},{10,... | collective-permute-start | bytes 589832 | tf_op jit(solution)/shard_map/ppermute | solution.py:566
  70.0 4.3 %copy-start.3 = (bf16[192,96]{1,0:T(8,128)(2,1)S(1)}, bf16[192,96]{1,0:T(8,128)(2,1)}, u32[]{:S(2)}) copy-start(bf16[192,96]{1,0:T(8,128)(2,1)} %w_ref.7) | copy-start | bytes 110596
  74.3 4.6 %copy-start = (bf16[16,256,256]{2,1,0:T(8,128)(2,1)S(1)}, bf16[16,256,256]{2,1,0:T(8,128)(2,1)}, u32[]{:S(2)}) copy-start(bf16[16,256,256]{2,1,0:T(8,128)(2,1)} %get-tuple-element.35.refs_2_.refs_0_.refs_1_.x_ref) | copy-start | bytes 6291460
  74.3 4.6 %copy-start.1 = (bf16[16,256,256]{2,1,0:T(8,128)(2,1)S(1)}, bf16[16,256,256]{2,1,0:T(8,128)(2,1)}, u32[]{:S(2)}) copy-start(bf16[16,256,256]{2,1,0:T(8,128)(2,1)} %get-tuple-element.52.refs_2_.pre_ref) | copy-start | bytes 6291460

commit v4 on v3

--- a/solution.py
+++ b/solution.py
@@ -24,7 +24,6 @@
 WIDE = HS * LANE
 MID = H // HS
 PARTS = 8
-SPLIT = 9
 
 
 def bf(table):
@@ -227,9 +226,12 @@
         load.wait()
 
 
-def width_near_body(me_ref, t_ref, near_ref, next_ref, o_ref):
+def width_near_body(me_ref, t_ref, near_ref, next_ref, x_ref, o_ref, copy_ref, sem):
     me = me_ref[0]
+    copy = pltpu.make_async_copy(x_ref, copy_ref, sem.at[0])
+    copy.start()
     o_ref[...] = dot_nt(t_ref[me], near_ref[...]) + dot_nt(t_ref[lax.bitwise_xor(me, 1)], next_ref[:LANES])
+    copy.wait()
 
 
 def width_far_body(me_ref, t_ref, part_ref, far_ref, last_ref, o_ref, held, sem):
@@ -391,11 +393,12 @@
     cl = wl_ref.shape[1] // 3
     local = jnp.concatenate([row[:cl] for row in three], 0)
     other = jnp.concatenate([row[cl:] for row in three], 0)
+    yl = dot(wl_ref[...], local)
+    yg = dot(wg_ref[...], other)
     parts = []
     for dx in range(3):
-        yl = dot(wl_ref[dx * channels : (dx + 1) * channels], local)
-        yg = dot(wg_ref[dx * cl : (dx + 1) * cl], other)
-        parts.append(jnp.concatenate([yl[:cl] + yg, yl[cl:]], 0))
+        own = yl[dx * channels : (dx + 1) * channels]
+        parts.append(jnp.concatenate([own[:cl] + yg[dx * cl : (dx + 1) * cl], own[cl:]], 0))
     before = pltpu.roll(parts[0], 1, 1)
     behind = pltpu.roll(parts[2], width - 1, 1)
     before, behind = edge_lanes(h, edge, before, behind)
@@ -406,26 +409,7 @@
     pltpu.make_async_copy(o_ref.at[h], out_ref.at[h], sem.at[0]).start()
 
 
-def conv_inner_body(
-    x_ref, fl_ref, fg_ref, wm_ref, ws_ref, affine_ref, out_ref, kept_ref, o_ref, edge, wl_ref, wg_ref, sem
-):
-    keep = pltpu.make_async_copy(x_ref, kept_ref, sem.at[1])
-    keep.start()
-    conv_setup(fl_ref, fg_ref, wl_ref, wg_ref)
-    edge[...] = jnp.zeros_like(edge)
-
-    def step(h, carry):
-        three = [x_ref[h - 1], x_ref[h], x_ref[h + 1]]
-        conv_row(h, three, wl_ref, wg_ref, wm_ref, ws_ref, affine_ref, edge, o_ref, out_ref, sem)
-        return carry
-
-    lax.fori_loop(1, SPLIT, step, 0)
-    done = pl.ds(1, SPLIT - 1)
-    pltpu.make_async_copy(o_ref.at[done], out_ref.at[done], sem.at[0]).wait()
-    keep.wait()
-
-
-def conv_outer_body(
+def conv_body(
     x_ref,
     side_ref,
     fl_ref,
@@ -435,7 +419,6 @@
     affine_ref,
     above_ref,
     below_ref,
-    given_ref,
     table_ref,
     me_ref,
     out_ref,
@@ -448,41 +431,26 @@
     sem,
 ):
     rows, channels, width = x_ref.shape
-    inner = pl.ds(1, SPLIT - 1)
-    load = pltpu.make_async_copy(given_ref.at[inner], o_ref.at[inner], sem.at[1])
-    load.start()
-    keeps = []
+    others = []
     for i, s in enumerate((2, 3, 1)):
         source = table_ref.at[lax.bitwise_xor(me_ref[0], s)]
-        keeps.append(pltpu.make_async_copy(source, kept_ref.at[i], sem.at[2 + i]))
-        keeps[-1].start()
+        others.append(pltpu.make_async_copy(source, kept_ref.at[i], sem.at[2 + i]))
+    for other in others:
+        other.start()
     conv_setup(fl_ref, fg_ref, wl_ref, wg_ref)
     conv_edges(side_ref, (above_ref, below_ref), wl_ref, wg_ref, cols, edge)
     rest = (wl_ref, wg_ref, wm_ref, ws_ref, affine_ref, edge, o_ref, out_ref, sem)
+    conv_row(0, [above_ref[:channels], x_ref[0], x_ref[1]], *rest)
 
     def step(h, carry):
         conv_row(h, [x_ref[h - 1], x_ref[h], x_ref[h + 1]], *rest)
         return carry
 
-    lax.fori_loop(SPLIT, rows - 1, step, 0)
-    conv_row(0, [above_ref[:channels], x_ref[0], x_ref[1]], *rest)
+    lax.fori_loop(1, rows - 1, step, 0, unroll=7)
     conv_row(rows - 1, [x_ref[rows - 2], x_ref[rows - 1], below_ref[:channels]], *rest)
-    load.wait()
-
-    def fix(h, carry):
-        none = jnp.zeros((channels, width), F32)
-        before, behind = edge_lanes(h, edge, none, none)
-        o_ref[h] = (o_ref[h].astype(F32) + before + behind).astype(BF16)
-        return carry
-
-    lax.fori_loop(1, SPLIT, fix, 0)
-    store = pltpu.make_async_copy(o_ref.at[inner], out_ref.at[inner], sem.at[1])
-    store.start()
-    for done in (pl.ds(SPLIT, rows - SPLIT), pl.ds(0, 1)):
-        pltpu.make_async_copy(o_ref.at[done], out_ref.at[done], sem.at[0]).wait()
-    store.wait()
-    for keep in keeps:
-        keep.wait()
+    pltpu.make_async_copy(o_ref, out_ref, sem.at[0]).wait()
+    for other in others:
+        other.wait()
 
 
 def final_rows(pieces, me_ref, x_ref, pre_ref, w_ref, affine_ref, o_ref, finish=None):
@@ -623,18 +591,17 @@
         pltpu.VMEM((3 * cl, 3 * cg), BF16),
         dma((5,)),
     ]
-    pre, x = call(
-        conv_inner_body,
-        (whole, whole),
-        (x,) + weights,
-        hbm_out=(0, 1),
-        stage=tuple(range(1, 6)),
+    fwd_w, inv_w = (jnp.asarray(t) for t in width_tables())
+    near, far = after(near, far)
+    part, x = call(
+        width_near_body,
+        (shape((W, LANES), F32), whole),
+        (me, fwd_w, near, other, x),
+        smem=(0,),
         flops=10**9,
-        scratch=scratch[:1] + scratch[2:],
-    )
-    fwd_w, inv_w = (jnp.asarray(t) for t in width_tables())
-    part = call(width_near_body, shape((W, LANES), F32), (me, fwd_w, near, other), smem=(0,))
-    part, pre = after(part, pre)
+        hbm_out=(1,),
+        scratch=[dma((1,))],
+    )
     spectra = call(
         width_far_body,
         shape((W, LANES), BF16),
@@ -681,15 +648,14 @@
     returned, above, below = after(returned, above, below)
     returned = lax.all_to_all(returned, ("row", "col"), split_axis=0, concat_axis=0, tiled=True).reshape(W, LANES)
     pre, table = call(
-        conv_outer_body,
+        conv_body,
         (whole, shape((3, W, width), BF16)),
-        (x, sides) + weights + (above, below, pre, inv_w, me),
-        smem=(11,),
-        hbm=(9, 10),
+        (x, sides) + weights + (above, below, inv_w, me),
+        smem=(10,),
+        hbm=(9,),
         hbm_out=(0,),
         stage=tuple(range(7)),
         flops=10**9,
-        input_output_aliases={9: 0},
         scratch=scratch,
     )
 

time: 81.6 us -> 81.2 us (level)
  waiting for transfers between devices: 21 us -> 27 us
  Pallas kernels: 34.5 us -> 28.7 us
    pallas_call x12 -> x11, Pallas kernels: 34.5 us -> 28.7 us  [call(): pl.pallas_call(body, out_shape=shapes[0] if single else tuple(shapes), in...]
    ppermute x6, waiting for transfers between devices: 6.3 us -> 11.7 us  [swap(): return lax.ppermute(block, 'col', [(i, i ^ s) for i in range(COLS)])]
  transfers between devices with their start and end apart: 10 -> 10, of which waited for: 5 -> 6; matrix products, arithmetic and copies ran while one was open for 0% -> 0% of each run, Pallas kernels for 34% -> 27%
where the time goes in v4:
time: 81.2 us; the launch traced here: 80.7 us
  Pallas kernels  28.7 us (35%)
  waiting for transfers between devices  27 us (33%)
  starting transfers between devices  24 us (30%)
    pallas_call x11, Pallas kernels, call(): pl.pallas_call(body, out_shape=shapes[0] if single else tuple(shapes), in...  28.7 us
    ppermute x6, waiting for transfers between devices, swap(): return lax.ppermute(block, 'col', [(i, i ^ s) for i in range(COLS)])  11.7 us
    all_to_all x1, starting transfers between devices, per_device(): lax.all_to_all(spectra.reshape(PEERS, 2 * NF, LANES), ('row', 'col'), spl...  9.66 us
    all_to_all x1, waiting for transfers between devices, per_device(): lax.all_to_all(spectra.reshape(PEERS, 2 * NF, LANES), ('row', 'col'), spl...  8.21 us
    all_to_all x1, waiting for transfers between devices, per_device(): lax.all_to_all(returned, ('row', 'col'), split_axis=0, concat_axis=0, til...  7.05 us
    ppermute x6, starting transfers between devices, swap(): return lax.ppermute(block, 'col', [(i, i ^ s) for i in range(COLS)])  5.38 us
    ppermute x2, starting transfers between devices, shift_along(): return lax.ppermute(block, axis, pairs)  4.58 us
    all_to_all x1, starting transfers between devices, per_device(): lax.all_to_all(returned, ('row', 'col'), split_axis=0, concat_axis=0, til...  4.4 us
  transfers between devices with their start and end apart: 10, of which 6 were waited for; matrix products, arithmetic and copies ran while one was open for 0% of the time, Pallas kernels for 27%

profile of v4, /device:TPU:1, one launch (start us, length us, event | category | flops | bytes accessed | tf_op | source)
XLA Modules:
  0.0 80.7 jit_solution(8124739985085201592)
XLA Ops:
  0.0 2.1 %shard_map.163 = (bf16[16,256,256]{2,1,0:T(8,128)(2,1)S(1)}, bf16[384,256]{1,0:T(8,128)(2,1)S(1)}, f32[96,2]{1,0:T(8,128)S(1)}) custom-call(s32[1]{0:T(128)} %bitcast.me_ref.refs_0_.refs_10_, bf16[256,16,256]{2,1,0:T(8,128)(2,1)} %image_ref.1, bf16[96,192]{1,0:T(8,128)(2,1)} %refs_5_.3, f32[1,96]{1,0:T(1,128)} %bitcast.19, f32[1,96]{1,0:T(1,128)} %bitcast.20), custom_call_target="tpu_custom_call" | custom-call | flops 1000000 | bytes 1000 | tf_op jit(solution)/shard_map/pallas_call | solution.py:116
  2.1 0.9 %shard_map.164 = (bf16[384,256]{1,0:T(8,128)(2,1)S(1)}, bf16[416,256]{1,0:T(8,128)(2,1)S(1)}, bf16[416,256]{1,0:T(8,128)(2,1)S(1)}) custom-call(s32[1]{0:T(128)} %bitcast.me_ref.refs_0_.refs_10_, bf16[16,256,256]{2,1,0:T(8,128)(2,1)S(1)} %get-tuple-element.33.x_ref, bf16[96,192]{1,0:T(8,128)(2,1)S(1)} %copy-done.4, ...), custom_call_target="tpu_custom_call" | custom-call | flops 1000000 | bytes 1000 | tf_op jit(solution)/shard_map/pallas_call | solution.py:116
  3.0 1.4 %collective-permute-start.1 = (bf16[416,256]{1,0:T(8,128)(2,1)S(1)}, bf16[416,256]{1,0:T(8,128)(2,1)S(1)}, u32[]{:S(2)}, u32[]{:S(2)}) collective-permute-start(bf16[416,256]{1,0:T(8,128)(2,1)S(1)} %get-tuple-element.38), channel_id=1, source_target_pairs={{0,1},{1,0},{2,3},{3,2},{4,5},{5,4},{6,7},{7,6},{8,9},{9,8},{10,11... | collective-permute-start | bytes 638984 | tf_op jit(solution)/shard_map/ppermute | solution.py:534
  4.5 1.4 %collective-permute-start = (bf16[384,256]{1,0:T(8,128)(2,1)S(1)}, bf16[384,256]{1,0:T(8,128)(2,1)S(1)}, u32[]{:S(2)}, u32[]{:S(2)}) collective-permute-start(bf16[384,256]{1,0:T(8,128)(2,1)S(1)} %get-tuple-element.36), channel_id=1, source_target_pairs={{0,2},{1,3},{2,0},{3,1},{4,6},{5,7},{6,4},{7,5},{8,10},{9,11},{10,... | collective-permute-start | bytes 589832 | tf_op jit(solution)/shard_map/ppermute | solution.py:534
  6.2 4.8 %collective-permute-done.far_ref = bf16[384,256]{1,0:T(8,128)(2,1)S(1)} collective-permute-done((bf16[384,256]{1,0:T(8,128)(2,1)S(1)}, bf16[384,256]{1,0:T(8,128)(2,1)S(1)}, u32[]{:S(2)}, u32[]{:S(2)}) %collective-permute-start) | collective-permute-done | bytes 196640 | tf_op jit(solution)/shard_map/ppermute | solution.py:534
  10.9 1.9 %shard_map.165 = (f32[1024,384]{1,0:T(8,128)S(1)}, bf16[16,256,256]{2,1,0:T(8,128)(2,1)}) custom-call(s32[1]{0:T(128)} %bitcast.me_ref.refs_0_.refs_10_, bf16[4,1024,256]{2,1,0:T(8,128)(2,1)S(1)} %copy-done.2, bf16[384,256]{1,0:T(8,128)(2,1)S(1)} %get-tuple-element.37.near_ref, bf16[416,256]{1,0:T(8,128)(2,1)S(1)} %collective-permute-done.1.next_ref.refs_3_, ...), custom_call_target="tpu_custom_call" | custom-call | flops 1000000000 | bytes 1000000 | tf_op jit(solution)/shard_map/pallas_call | solution.py:116
  12.8 2.8 %collective-permute-done.2.last_ref.refs_4_ = bf16[416,256]{1,0:T(8,128)(2,1)S(1)} collective-permute-done((bf16[416,256]{1,0:T(8,128)(2,1)S(1)}, bf16[416,256]{1,0:T(8,128)(2,1)S(1)}, u32[]{:S(2)}, u32[]{:S(2)}) %collective-permute-start.2) | collective-permute-done | bytes 213024 | tf_op jit(solution)/shard_map/ppermute | solution.py:534
  15.7 1.4 %shard_map.166 = bf16[1024,384]{1,0:T(8,128)(2,1)} custom-call(s32[1]{0:T(128)} %bitcast.me_ref.refs_0_.refs_10_, bf16[4,1024,256]{2,1,0:T(8,128)(2,1)S(1)} %copy-done.2, f32[1024,384]{1,0:T(8,128)S(1)} %get-tuple-element.40.part_ref, bf16[384,256]{1,0:T(8,128)(2,1)S(1)} %collective-permute-done.far_ref, ...), custom_call_target="tpu_custom_call" | custom-call | flops 1000000 | bytes 1000 | tf_op jit(solution)/shard_map/pallas_call | solution.py:116
  17.1 9.7 %all-to-all-start = ((bf16[64,16,384]{2,1,0:T(8,128)(2,1)}), bf16[64,16,384]{2,1,0:T(8,128)(2,1)S(1)}, u32[]{:S(2)}, u32[]{:S(2)}) async-start(bf16[64,16,384]{2,1,0:T(8,128)(2,1)} %bitcast.13), calls=%async_computation | async-start | bytes 1572864 | tf_op jit(solution)/shard_map/all_to_all | solution.py:614
  26.8 2.1 %shard_map.167 = (bf16[288,256]{1,0:T(8,128)(2,1)S(1)}, bf16[288,256]{1,0:T(8,128)(2,1)S(1)}, bf16[32,256]{1,0:T(8,128)(2,1)S(1)}, bf16[6,256,256]{2,1,0:T(8,128)(2,1)S(1)}) custom-call(s32[1]{0:T(128)} %bitcast.me_ref.refs_0_.refs_10_, s32[1]{0:T(128)} %bitcast.3.refs_1_, bf16[16,256,256]{2,1,0:T(8,128)(2,1)} %get-tuple-element.39.refs_2_.refs_0_.refs_1_.x_ref, ...), custom_call_target="tpu_custom_call" | custom-call | flops 1000000 | bytes 1000 | tf_op jit(solution)/shard_map/pallas_call | solution.py:116
  29.5 3.3 %collective-permute-start.3 = (bf16[288,256]{1,0:T(8,128)(2,1)S(1)}, bf16[288,256]{1,0:T(8,128)(2,1)S(1)}, u32[]{:S(2)}, u32[]{:S(2)}) collective-permute-start(bf16[288,256]{1,0:T(8,128)(2,1)S(1)} %get-tuple-element.48), channel_id=1, source_target_pairs={{0,4},{4,8},{8,12},{12,16},{16,20},{20,24},{24,28},{28,32},{32,36}... | collective-permute-start | bytes 442376 | tf_op jit(solution)/shard_map/ppermute | solution.py:530
  32.8 1.3 %collective-permute-start.4 = (bf16[288,256]{1,0:T(8,128)(2,1)S(1)}, bf16[288,256]{1,0:T(8,128)(2,1)S(1)}, u32[]{:S(2)}, u32[]{:S(2)}) collective-permute-start(bf16[288,256]{1,0:T(8,128)(2,1)S(1)} %get-tuple-element.49), channel_id=1, source_target_pairs={{4,0},{8,4},{12,8},{16,12},{20,16},{24,20},{28,24},{32,28},{36,32}... | collective-permute-start | bytes 442376 | tf_op jit(solution)/shard_map/ppermute | solution.py:530
  34.1 8.2 %all-to-all-done.d_ref = bf16[64,16,384]{2,1,0:T(8,128)(2,1)S(1)} async-done(((bf16[64,16,384]{2,1,0:T(8,128)(2,1)}), bf16[64,16,384]{2,1,0:T(8,128)(2,1)S(1)}, u32[]{:S(2)}, u32[]{:S(2)}) %all-to-all-start) | async-done | bytes 786464 | tf_op jit(solution)/shard_map/all_to_all | solution.py:614
  42.3 4.6 %shard_map.168 = bf16[64,16,384]{2,1,0:T(8,128)(2,1)} custom-call(bf16[64,16,384]{2,1,0:T(8,128)(2,1)S(1)} %all-to-all-done.d_ref, bf16[6,256,256]{2,1,0:T(8,128)(2,1)S(1)} %get-tuple-element.47.x_ref, f32[1,192]{1,0:T(1,128)} %bitcast.15, f32[1,192]{1,0:T(1,128)} %bitcast.16), custom_call_target="tpu_custom_call" | custom-call | flops 1000000 | bytes 1000 | tf_op jit(solution)/shard_map/pallas_call | solution.py:116
  46.9 4.4 %all-to-all-start.1 = ((bf16[64,16,384]{2,1,0:T(8,128)(2,1)}), bf16[64,16,384]{2,1,0:T(8,128)(2,1)S(1)}, u32[]{:S(2)}, u32[]{:S(2)}) async-start(bf16[64,16,384]{2,1,0:T(8,128)(2,1)} %shard_map.168), calls=%async_computation.1 | async-start | bytes 1572864 | tf_op jit(solution)/shard_map/all_to_all | solution.py:649
  51.3 8.1 %shard_map.169 = (bf16[16,256,256]{2,1,0:T(8,128)(2,1)}, bf16[3,1024,256]{2,1,0:T(8,128)(2,1)S(1)}) custom-call(bf16[16,256,256]{2,1,0:T(8,128)(2,1)} %get-tuple-element.39.refs_2_.refs_0_.refs_1_.x_ref, bf16[32,256]{1,0:T(8,128)(2,1)} %copy-done.6, bf16[9,64,256]{2,1,0:T(8,128)(2,1)} %bitcast.14, bf16[9,64,192]{2,1,0:T(8,128)(2,1)} %refs_3_.2, ...), custom_call_target="tpu_custom_call" | custom-call | flops 1000000000 | bytes 1000000 | tf_op jit(solution)/shard_map/pallas_call | solution.py:116
  59.3 7.1 %all-to-all-done.1 = bf16[64,16,384]{2,1,0:T(8,128)(2,1)S(1)} async-done(((bf16[64,16,384]{2,1,0:T(8,128)(2,1)}), bf16[64,16,384]{2,1,0:T(8,128)(2,1)S(1)}, u32[]{:S(2)}, u32[]{:S(2)}) %all-to-all-start.1) | async-done | bytes 786464 | tf_op jit(solution)/shard_map/all_to_all | solution.py:649
  66.4 0.8 %shard_map.170 = (bf16[384,256]{1,0:T(8,128)(2,1)S(1)}, bf16[384,256]{1,0:T(8,128)(2,1)S(1)}, bf16[384,256]{1,0:T(8,128)(2,1)S(1)}) custom-call(bf16[3,1024,256]{2,1,0:T(8,128)(2,1)S(1)} %get-tuple-element.54.t_ref, bf16[1024,384]{1,0:T(8,128)(2,1)S(1)} %bitcast.11), custom_call_target="tpu_custom_call" | custom-call | flops 1000000 | bytes 1000 | tf_op jit(solution)/shard_map/pallas_call | solution.py:116
  67.7 1.7 %collective-permute-start.6 = (bf16[384,256]{1,0:T(8,128)(2,1)S(1)}, bf16[384,256]{1,0:T(8,128)(2,1)S(1)}, u32[]{:S(2)}, u32[]{:S(2)}) collective-permute-start(bf16[384,256]{1,0:T(8,128)(2,1)S(1)} %get-tuple-element.57), channel_id=1, source_target_pairs={{0,3},{1,2},{2,1},{3,0},{4,7},{5,6},{6,5},{7,4},{8,11},{9,10},{10,... | collective-permute-start | bytes 589832 | tf_op jit(solution)/shard_map/ppermute | solution.py:534
  69.5 3.3 %shard_map.171 = (bf16[16,256,256]{2,1,0:T(8,128)(2,1)S(1)}, f32[256,2]{1,0:T(8,128)S(1)}) custom-call(s32[1]{0:T(128)} %bitcast.me_ref.refs_0_.refs_10_, bf16[16,256,256]{2,1,0:T(8,128)(2,1)} %get-tuple-element.39.refs_2_.refs_0_.refs_1_.x_ref, bf16[16,256,256]{2,1,0:T(8,128)(2,1)} %get-tuple-element.52.refs_2_.pre_ref, bf16[192,96]{1,0:T(8,128)(2,1)} %w_ref.7, ...), custom_call_target="tpu_custom_call" | custom-call | flops 1000000 | bytes 1000 | tf_op jit(solution)/shard_map/pallas_call | solution.py:116
  72.7 1.5 %collective-permute-done.7.far_ref = bf16[384,256]{1,0:T(8,128)(2,1)S(1)} collective-permute-done((bf16[384,256]{1,0:T(8,128)(2,1)S(1)}, bf16[384,256]{1,0:T(8,128)(2,1)S(1)}, u32[]{:S(2)}, u32[]{:S(2)}) %collective-permute-start.7) | collective-permute-done | bytes 196640 | tf_op jit(solution)/shard_map/ppermute | solution.py:534
  74.2 1.7 %shard_map.172.given_ref = bf16[16,256,256]{2,1,0:T(8,128)(2,1)S(1)} custom-call(s32[1]{0:T(128)} %bitcast.me_ref.refs_0_.refs_10_, bf16[16,256,256]{2,1,0:T(8,128)(2,1)} %get-tuple-element.39.refs_2_.refs_0_.refs_1_.x_ref, bf16[16,256,256]{2,1,0:T(8,128)(2,1)} %get-tuple-element.52.refs_2_.pre_ref, ...), custom_call_target="tpu_custom_call", output_to_operand_aliasing={{}: (6, {})} | custom-call | flops 1000000 | bytes 1000 | tf_op jit(solution)/shard_map/pallas_call | solution.py:116
  75.9 2.7 %collective-permute-done.6.last_ref = bf16[384,256]{1,0:T(8,128)(2,1)S(1)} collective-permute-done((bf16[384,256]{1,0:T(8,128)(2,1)S(1)}, bf16[384,256]{1,0:T(8,128)(2,1)S(1)}, u32[]{:S(2)}, u32[]{:S(2)}) %collective-permute-start.6) | collective-permute-done | bytes 196640 | tf_op jit(solution)/shard_map/ppermute | solution.py:534
  78.6 1.9 %shard_map.173 = (bf16[16,256,256]{2,1,0:T(8,128)(2,1)S(1)}, bf16[256,16,256]{2,1,0:T(8,128)(2,1)}) custom-call(s32[1]{0:T(128)} %bitcast.me_ref.refs_0_.refs_10_, bf16[16,256,256]{2,1,0:T(8,128)(2,1)S(1)} %copy-done, bf16[16,256,256]{2,1,0:T(8,128)(2,1)S(1)} %copy-done.1, bf16[192,96]{1,0:T(8,128)(2,1)S(1)} %copy-done.3, ...), custom_call_target="tpu_custom_call", output_to_operand_aliasing={{0}: (6, {})} | custom-call | flops 1000000 | bytes 1000 | tf_op jit(solution)/shard_map/pallas_call | solution.py:116
  (21 shorter events, 1.4 us)
Async XLA Ops:
  0.0 2.1 %copy-start.4 = (bf16[96,192]{1,0:T(8,128)(2,1)S(1)}, bf16[96,192]{1,0:T(8,128)(2,1)}, u32[]{:S(2)}) copy-start(bf16[96,192]{1,0:T(8,128)(2,1)} %refs_5_.3) | copy-start | bytes 110596
  0.0 10.9 %copy-start.2 = (bf16[4,1024,256]{2,1,0:T(8,128)(2,1)S(1)}, bf16[4,1024,256]{2,1,0:T(8,128)(2,1)}, u32[]{:S(2)}) copy-start(bf16[4,1024,256]{2,1,0:T(8,128)(2,1)} %constant.21.clone.t_ref) | copy-start | bytes 6291460
  2.1 10.7 %copy-start.5 = (f32[96,2]{1,0:T(8,128)}, f32[96,2]{1,0:T(8,128)S(1)}, u32[]{:S(2)}) copy-start(f32[96,2]{1,0:T(8,128)S(1)} %get-tuple-element.34.affine_ref.refs_6_) | copy-start | bytes 2308
  3.0 7.9 %collective-permute-start.1 = (bf16[416,256]{1,0:T(8,128)(2,1)S(1)}, bf16[416,256]{1,0:T(8,128)(2,1)S(1)}, u32[]{:S(2)}, u32[]{:S(2)}) collective-permute-start(bf16[416,256]{1,0:T(8,128)(2,1)S(1)} %get-tuple-element.38), channel_id=1, source_target_pairs={{0,1},{1,0},{2,3},{3,2},{4,5},{5,4},{6,7},{7,6},{8,9},{9,8},{10,11... | collective-permute-start | bytes 638984 | tf_op jit(solution)/shard_map/ppermute | solution.py:534
  4.5 6.5 %collective-permute-start = (bf16[384,256]{1,0:T(8,128)(2,1)S(1)}, bf16[384,256]{1,0:T(8,128)(2,1)S(1)}, u32[]{:S(2)}, u32[]{:S(2)}) collective-permute-start(bf16[384,256]{1,0:T(8,128)(2,1)S(1)} %get-tuple-element.36), channel_id=1, source_target_pairs={{0,2},{1,3},{2,0},{3,1},{4,6},{5,7},{6,4},{7,5},{8,10},{9,11},{10,... | collective-permute-start | bytes 589832 | tf_op jit(solution)/shard_map/ppermute | solution.py:534
  5.8 9.8 %collective-permute-start.2 = (bf16[416,256]{1,0:T(8,128)(2,1)S(1)}, bf16[416,256]{1,0:T(8,128)(2,1)S(1)}, u32[]{:S(2)}, u32[]{:S(2)}) collective-permute-start(bf16[416,256]{1,0:T(8,128)(2,1)S(1)} %get-tuple-element.42), channel_id=1, source_target_pairs={{0,3},{1,2},{2,1},{3,0},{4,7},{5,6},{6,5},{7,4},{8,11},{9,10},{10,... | collective-permute-start | bytes 638984 | tf_op jit(solution)/shard_map/ppermute | solution.py:534
  17.1 25.2 %all-to-all-start = ((bf16[64,16,384]{2,1,0:T(8,128)(2,1)}), bf16[64,16,384]{2,1,0:T(8,128)(2,1)S(1)}, u32[]{:S(2)}, u32[]{:S(2)}) async-start(bf16[64,16,384]{2,1,0:T(8,128)(2,1)} %bitcast.13), calls=%async_computation | async-start | bytes 1572864 | tf_op jit(solution)/shard_map/all_to_all | solution.py:614
  28.9 0.6 copy-start.6
  29.5 17.4 %collective-permute-start.3 = (bf16[288,256]{1,0:T(8,128)(2,1)S(1)}, bf16[288,256]{1,0:T(8,128)(2,1)S(1)}, u32[]{:S(2)}, u32[]{:S(2)}) collective-permute-start(bf16[288,256]{1,0:T(8,128)(2,1)S(1)} %get-tuple-element.48), channel_id=1, source_target_pairs={{0,4},{4,8},{8,12},{12,16},{16,20},{20,24},{24,28},{28,32},{32,36}... | collective-permute-start | bytes 442376 | tf_op jit(solution)/shard_map/ppermute | solution.py:530
  32.8 14.1 %collective-permute-start.4 = (bf16[288,256]{1,0:T(8,128)(2,1)S(1)}, bf16[288,256]{1,0:T(8,128)(2,1)S(1)}, u32[]{:S(2)}, u32[]{:S(2)}) collective-permute-start(bf16[288,256]{1,0:T(8,128)(2,1)S(1)} %get-tuple-element.49), channel_id=1, source_target_pairs={{4,0},{8,4},{12,8},{16,12},{20,16},{24,20},{28,24},{32,28},{36,32}... | collective-permute-start | bytes 442376 | tf_op jit(solution)/shard_map/ppermute | solution.py:530
  46.9 19.5 %all-to-all-start.1 = ((bf16[64,16,384]{2,1,0:T(8,128)(2,1)}), bf16[64,16,384]{2,1,0:T(8,128)(2,1)S(1)}, u32[]{:S(2)}, u32[]{:S(2)}) async-start(bf16[64,16,384]{2,1,0:T(8,128)(2,1)} %shard_map.168), calls=%async_computation.1 | async-start | bytes 1572864 | tf_op jit(solution)/shard_map/all_to_all | solution.py:649
  67.2 2.2 %collective-permute-start.5 = (bf16[384,256]{1,0:T(8,128)(2,1)S(1)}, bf16[384,256]{1,0:T(8,128)(2,1)S(1)}, u32[]{:S(2)}, u32[]{:S(2)}) collective-permute-start(bf16[384,256]{1,0:T(8,128)(2,1)S(1)} %get-tuple-element.55), channel_id=1, source_target_pairs={{0,1},{1,0},{2,3},{3,2},{4,5},{5,4},{6,7},{7,6},{8,9},{9,8},{10,11... | collective-permute-start | bytes 589832 | tf_op jit(solution)/shard_map/ppermute | solution.py:534
  67.7 6.5 %collective-permute-start.7 = (bf16[384,256]{1,0:T(8,128)(2,1)S(1)}, bf16[384,256]{1,0:T(8,128)(2,1)S(1)}, u32[]{:S(2)}, u32[]{:S(2)}) collective-permute-start(bf16[384,256]{1,0:T(8,128)(2,1)S(1)} %get-tuple-element.58), channel_id=1, source_target_pairs={{0,2},{1,3},{2,0},{3,1},{4,6},{5,7},{6,4},{7,5},{8,10},{9,11},{10,... | collective-permute-start | bytes 589832 | tf_op jit(solution)/shard_map/ppermute | solution.py:534
  67.7 10.9 %collective-permute-start.6 = (bf16[384,256]{1,0:T(8,128)(2,1)S(1)}, bf16[384,256]{1,0:T(8,128)(2,1)S(1)}, u32[]{:S(2)}, u32[]{:S(2)}) collective-permute-start(bf16[384,256]{1,0:T(8,128)(2,1)S(1)} %get-tuple-element.57), channel_id=1, source_target_pairs={{0,3},{1,2},{2,1},{3,0},{4,7},{5,6},{6,5},{7,4},{8,11},{9,10},{10,... | collective-permute-start | bytes 589832 | tf_op jit(solution)/shard_map/ppermute | solution.py:534
  69.4 4.7 %copy-start.3 = (bf16[192,96]{1,0:T(8,128)(2,1)S(1)}, bf16[192,96]{1,0:T(8,128)(2,1)}, u32[]{:S(2)}) copy-start(bf16[192,96]{1,0:T(8,128)(2,1)} %w_ref.7) | copy-start | bytes 110596
  74.2 4.4 %copy-start = (bf16[16,256,256]{2,1,0:T(8,128)(2,1)S(1)}, bf16[16,256,256]{2,1,0:T(8,128)(2,1)}, u32[]{:S(2)}) copy-start(bf16[16,256,256]{2,1,0:T(8,128)(2,1)} %get-tuple-element.39.refs_2_.refs_0_.refs_1_.x_ref) | copy-start | bytes 6291460
  74.2 4.4 %copy-start.1 = (bf16[16,256,256]{2,1,0:T(8,128)(2,1)S(1)}, bf16[16,256,256]{2,1,0:T(8,128)(2,1)}, u32[]{:S(2)}) copy-start(bf16[16,256,256]{2,1,0:T(8,128)(2,1)} %get-tuple-element.52.refs_2_.pre_ref) | copy-start | bytes 6291460

commit v5 on v4

--- a/solution.py
+++ b/solution.py
@@ -226,21 +226,21 @@
         load.wait()
 
 
-def width_near_body(me_ref, t_ref, near_ref, next_ref, x_ref, o_ref, copy_ref, sem):
+def width_near_body(me_ref, t_ref, near_ref, far_ref, x_ref, o_ref, copy_ref, sem):
     me = me_ref[0]
     copy = pltpu.make_async_copy(x_ref, copy_ref, sem.at[0])
     copy.start()
-    o_ref[...] = dot_nt(t_ref[me], near_ref[...]) + dot_nt(t_ref[lax.bitwise_xor(me, 1)], next_ref[:LANES])
+    o_ref[...] = dot_nt(t_ref[me], near_ref[...]) + dot_nt(t_ref[lax.bitwise_xor(me, 2)], far_ref[...])
     copy.wait()
 
 
-def width_far_body(me_ref, t_ref, part_ref, far_ref, last_ref, o_ref, held, sem):
+def width_last_body(me_ref, t_ref, part_ref, next_ref, last_ref, o_ref, held, sem):
     me = me_ref[0]
     size = o_ref.shape[0] // 4
     copies = []
     for i in range(4):
         span = pl.ds(i * size, size)
-        total = part_ref[span] + dot_nt(t_ref[lax.bitwise_xor(me, 2), span], far_ref[...])
+        total = part_ref[span] + dot_nt(t_ref[lax.bitwise_xor(me, 1), span], next_ref[:LANES])
         held[span] = (total + dot_nt(t_ref[lax.bitwise_xor(me, 3), span], last_ref[:LANES])).astype(BF16)
         copies.append(pltpu.make_async_copy(held.at[span], o_ref.at[span], sem.at[i]))
         copies[-1].start()
@@ -592,20 +592,19 @@
         dma((5,)),
     ]
     fwd_w, inv_w = (jnp.asarray(t) for t in width_tables())
-    near, far = after(near, far)
     part, x = call(
         width_near_body,
         (shape((W, LANES), F32), whole),
-        (me, fwd_w, near, other, x),
+        (me, fwd_w, near, far, x),
         smem=(0,),
         flops=10**9,
         hbm_out=(1,),
         scratch=[dma((1,))],
     )
     spectra = call(
-        width_far_body,
+        width_last_body,
         shape((W, LANES), BF16),
-        (me, fwd_w, part, far, last),
+        (me, fwd_w, part, other, last),
         smem=(0,),
         hbm_out=(0,),
         scratch=[pltpu.VMEM((W, LANES), BF16), dma((4,))],

time: 81.2 us -> 79.5 us (0.979)
  waiting for transfers between devices: 27 us -> 25.3 us
    ppermute x6, waiting for transfers between devices: 11.7 us -> 10 us  [swap(): return lax.ppermute(block, 'col', [(i, i ^ s) for i in range(COLS)])]
  transfers between devices with their start and end apart: 10 -> 10, of which waited for: 6 -> 6; matrix products, arithmetic and copies ran while one was open for 0% -> 0% of each run, Pallas kernels for 27% -> 28%
where the time goes in v5:
time: 79.5 us; the launch traced here: 79 us
  Pallas kernels  28.7 us (36%)
  waiting for transfers between devices  25.3 us (32%)
  starting transfers between devices  24.1 us (30%)
    pallas_call x11, Pallas kernels, call(): pl.pallas_call(body, out_shape=shapes[0] if single else tuple(shapes), in...  28.7 us
    ppermute x6, waiting for transfers between devices, swap(): return lax.ppermute(block, 'col', [(i, i ^ s) for i in range(COLS)])  10 us
    all_to_all x1, starting transfers between devices, per_device(): lax.all_to_all(spectra.reshape(PEERS, 2 * NF, LANES), ('row', 'col'), spl...  9.63 us
    all_to_all x1, waiting for transfers between devices, per_device(): lax.all_to_all(spectra.reshape(PEERS, 2 * NF, LANES), ('row', 'col'), spl...  8.21 us
    all_to_all x1, waiting for transfers between devices, per_device(): lax.all_to_all(returned, ('row', 'col'), split_axis=0, concat_axis=0, til...  7.05 us
    ppermute x6, starting transfers between devices, swap(): return lax.ppermute(block, 'col', [(i, i ^ s) for i in range(COLS)])  5.47 us
    ppermute x2, starting transfers between devices, shift_along(): return lax.ppermute(block, axis, pairs)  4.58 us
    all_to_all x1, starting transfers between devices, per_device(): lax.all_to_all(returned, ('row', 'col'), split_axis=0, concat_axis=0, til...  4.4 us
  transfers between devices with their start and end apart: 10, of which 6 were waited for; matrix products, arithmetic and copies ran while one was open for 0% of the time, Pallas kernels for 28%

profile of v5, /device:TPU:1, one launch (start us, length us, event | category | flops | bytes accessed | tf_op | source)
XLA Modules:
  0.0 79.0 jit_solution(5845683504347272267)
XLA Ops:
  0.0 2.1 %shard_map.163 = (bf16[16,256,256]{2,1,0:T(8,128)(2,1)S(1)}, bf16[384,256]{1,0:T(8,128)(2,1)S(1)}, f32[96,2]{1,0:T(8,128)S(1)}) custom-call(s32[1]{0:T(128)} %bitcast.me_ref.refs_0_.refs_10_, bf16[256,16,256]{2,1,0:T(8,128)(2,1)} %image_ref.1, bf16[96,192]{1,0:T(8,128)(2,1)} %refs_5_.3, f32[1,96]{1,0:T(1,128)} %bitcast.19, f32[1,96]{1,0:T(1,128)} %bitcast.20), custom_call_target="tpu_custom_call" | custom-call | flops 1000000 | bytes 1000 | tf_op jit(solution)/shard_map/pallas_call | solution.py:116
  2.1 2.2 %collective-permute-start = (bf16[384,256]{1,0:T(8,128)(2,1)S(1)}, bf16[384,256]{1,0:T(8,128)(2,1)S(1)}, u32[]{:S(2)}, u32[]{:S(2)}) collective-permute-start(bf16[384,256]{1,0:T(8,128)(2,1)S(1)} %get-tuple-element.34), channel_id=1, source_target_pairs={{0,2},{1,3},{2,0},{3,1},{4,6},{5,7},{6,4},{7,5},{8,10},{9,11},{10,... | collective-permute-start | bytes 589832 | tf_op jit(solution)/shard_map/ppermute | solution.py:534
  4.3 0.9 %shard_map.164 = (bf16[384,256]{1,0:T(8,128)(2,1)S(1)}, bf16[416,256]{1,0:T(8,128)(2,1)S(1)}, bf16[416,256]{1,0:T(8,128)(2,1)S(1)}) custom-call(s32[1]{0:T(128)} %bitcast.me_ref.refs_0_.refs_10_, bf16[16,256,256]{2,1,0:T(8,128)(2,1)S(1)} %get-tuple-element.31.x_ref, bf16[96,192]{1,0:T(8,128)(2,1)S(1)} %copy-done.4, ...), custom_call_target="tpu_custom_call" | custom-call | flops 1000000 | bytes 1000 | tf_op jit(solution)/shard_map/pallas_call | solution.py:116
  5.2 1.0 %collective-permute-start.1 = (bf16[416,256]{1,0:T(8,128)(2,1)S(1)}, bf16[416,256]{1,0:T(8,128)(2,1)S(1)}, u32[]{:S(2)}, u32[]{:S(2)}) collective-permute-start(bf16[416,256]{1,0:T(8,128)(2,1)S(1)} %get-tuple-element.37), channel_id=1, source_target_pairs={{0,1},{1,0},{2,3},{3,2},{4,5},{5,4},{6,7},{7,6},{8,9},{9,8},{10,11... | collective-permute-start | bytes 638984 | tf_op jit(solution)/shard_map/ppermute | solution.py:534
  6.2 2.3 %collective-permute-done.far_ref = bf16[384,256]{1,0:T(8,128)(2,1)S(1)} collective-permute-done((bf16[384,256]{1,0:T(8,128)(2,1)S(1)}, bf16[384,256]{1,0:T(8,128)(2,1)S(1)}, u32[]{:S(2)}, u32[]{:S(2)}) %collective-permute-start) | collective-permute-done | bytes 196640 | tf_op jit(solution)/shard_map/ppermute | solution.py:534
  8.5 1.9 %shard_map.165 = (f32[1024,384]{1,0:T(8,128)S(1)}, bf16[16,256,256]{2,1,0:T(8,128)(2,1)}) custom-call(s32[1]{0:T(128)} %bitcast.me_ref.refs_0_.refs_10_, bf16[4,1024,256]{2,1,0:T(8,128)(2,1)S(1)} %copy-done.2, bf16[384,256]{1,0:T(8,128)(2,1)S(1)} %get-tuple-element.33.near_ref, bf16[384,256]{1,0:T(8,128)(2,1)S(1)} %collective-permute-done.far_ref, ...), custom_call_target="tpu_custom_call" | custom-call | flops 1000000000 | bytes 1000000 | tf_op jit(solution)/shard_map/pallas_call | solution.py:116
  10.4 3.6 %collective-permute-done.2.last_ref.refs_4_ = bf16[416,256]{1,0:T(8,128)(2,1)S(1)} collective-permute-done((bf16[416,256]{1,0:T(8,128)(2,1)S(1)}, bf16[416,256]{1,0:T(8,128)(2,1)S(1)}, u32[]{:S(2)}, u32[]{:S(2)}) %collective-permute-start.2) | collective-permute-done | bytes 213024 | tf_op jit(solution)/shard_map/ppermute | solution.py:534
  14.0 1.4 %shard_map.166 = bf16[1024,384]{1,0:T(8,128)(2,1)} custom-call(s32[1]{0:T(128)} %bitcast.me_ref.refs_0_.refs_10_, bf16[4,1024,256]{2,1,0:T(8,128)(2,1)S(1)} %copy-done.2, f32[1024,384]{1,0:T(8,128)S(1)} %get-tuple-element.36.part_ref, bf16[416,256]{1,0:T(8,128)(2,1)S(1)} %collective-permute-done.1.next_ref.refs_3_, ...), custom_call_target="tpu_custom_call" | custom-call | flops 1000000 | bytes 1000 | tf_op jit(solution)/shard_map/pallas_call | solution.py:116
  15.5 9.6 %all-to-all-start = ((bf16[64,16,384]{2,1,0:T(8,128)(2,1)}), bf16[64,16,384]{2,1,0:T(8,128)(2,1)S(1)}, u32[]{:S(2)}, u32[]{:S(2)}) async-start(bf16[64,16,384]{2,1,0:T(8,128)(2,1)} %bitcast.13), calls=%async_computation | async-start | bytes 1572864 | tf_op jit(solution)/shard_map/all_to_all | solution.py:613
  25.1 2.1 %shard_map.167 = (bf16[288,256]{1,0:T(8,128)(2,1)S(1)}, bf16[288,256]{1,0:T(8,128)(2,1)S(1)}, bf16[32,256]{1,0:T(8,128)(2,1)S(1)}, bf16[6,256,256]{2,1,0:T(8,128)(2,1)S(1)}) custom-call(s32[1]{0:T(128)} %bitcast.me_ref.refs_0_.refs_10_, s32[1]{0:T(128)} %bitcast.3.refs_1_, bf16[16,256,256]{2,1,0:T(8,128)(2,1)} %get-tuple-element.35.refs_2_.refs_0_.refs_1_.x_ref, ...), custom_call_target="tpu_custom_call" | custom-call | flops 1000000 | bytes 1000 | tf_op jit(solution)/shard_map/pallas_call | solution.py:116
  27.8 3.3 %collective-permute-start.3 = (bf16[288,256]{1,0:T(8,128)(2,1)S(1)}, bf16[288,256]{1,0:T(8,128)(2,1)S(1)}, u32[]{:S(2)}, u32[]{:S(2)}) collective-permute-start(bf16[288,256]{1,0:T(8,128)(2,1)S(1)} %get-tuple-element.44), channel_id=1, source_target_pairs={{0,4},{4,8},{8,12},{12,16},{16,20},{20,24},{24,28},{28,32},{32,36}... | collective-permute-start | bytes 442376 | tf_op jit(solution)/shard_map/ppermute | solution.py:530
  31.1 1.3 %collective-permute-start.4 = (bf16[288,256]{1,0:T(8,128)(2,1)S(1)}, bf16[288,256]{1,0:T(8,128)(2,1)S(1)}, u32[]{:S(2)}, u32[]{:S(2)}) collective-permute-start(bf16[288,256]{1,0:T(8,128)(2,1)S(1)} %get-tuple-element.45), channel_id=1, source_target_pairs={{4,0},{8,4},{12,8},{16,12},{20,16},{24,20},{28,24},{32,28},{36,32}... | collective-permute-start | bytes 442376 | tf_op jit(solution)/shard_map/ppermute | solution.py:530
  32.4 8.2 %all-to-all-done.d_ref = bf16[64,16,384]{2,1,0:T(8,128)(2,1)S(1)} async-done(((bf16[64,16,384]{2,1,0:T(8,128)(2,1)}), bf16[64,16,384]{2,1,0:T(8,128)(2,1)S(1)}, u32[]{:S(2)}, u32[]{:S(2)}) %all-to-all-start) | async-done | bytes 786464 | tf_op jit(solution)/shard_map/all_to_all | solution.py:613
  40.6 4.6 %shard_map.168 = bf16[64,16,384]{2,1,0:T(8,128)(2,1)} custom-call(bf16[64,16,384]{2,1,0:T(8,128)(2,1)S(1)} %all-to-all-done.d_ref, bf16[6,256,256]{2,1,0:T(8,128)(2,1)S(1)} %get-tuple-element.43.x_ref, f32[1,192]{1,0:T(1,128)} %bitcast.15, f32[1,192]{1,0:T(1,128)} %bitcast.16), custom_call_target="tpu_custom_call" | custom-call | flops 1000000 | bytes 1000 | tf_op jit(solution)/shard_map/pallas_call | solution.py:116
  45.2 4.4 %all-to-all-start.1 = ((bf16[64,16,384]{2,1,0:T(8,128)(2,1)}), bf16[64,16,384]{2,1,0:T(8,128)(2,1)S(1)}, u32[]{:S(2)}, u32[]{:S(2)}) async-start(bf16[64,16,384]{2,1,0:T(8,128)(2,1)} %shard_map.168), calls=%async_computation.1 | async-start | bytes 1572864 | tf_op jit(solution)/shard_map/all_to_all | solution.py:648
  49.6 8.1 %shard_map.169 = (bf16[16,256,256]{2,1,0:T(8,128)(2,1)}, bf16[3,1024,256]{2,1,0:T(8,128)(2,1)S(1)}) custom-call(bf16[16,256,256]{2,1,0:T(8,128)(2,1)} %get-tuple-element.35.refs_2_.refs_0_.refs_1_.x_ref, bf16[32,256]{1,0:T(8,128)(2,1)} %copy-done.6, bf16[9,64,256]{2,1,0:T(8,128)(2,1)} %bitcast.14, bf16[9,64,192]{2,1,0:T(8,128)(2,1)} %refs_3_.2, ...), custom_call_target="tpu_custom_call" | custom-call | flops 1000000000 | bytes 1000000 | tf_op jit(solution)/shard_map/pallas_call | solution.py:116
  57.7 7.1 %all-to-all-done.1 = bf16[64,16,384]{2,1,0:T(8,128)(2,1)S(1)} async-done(((bf16[64,16,384]{2,1,0:T(8,128)(2,1)}), bf16[64,16,384]{2,1,0:T(8,128)(2,1)S(1)}, u32[]{:S(2)}, u32[]{:S(2)}) %all-to-all-start.1) | async-done | bytes 786464 | tf_op jit(solution)/shard_map/all_to_all | solution.py:648
  64.8 0.8 %shard_map.170 = (bf16[384,256]{1,0:T(8,128)(2,1)S(1)}, bf16[384,256]{1,0:T(8,128)(2,1)S(1)}, bf16[384,256]{1,0:T(8,128)(2,1)S(1)}) custom-call(bf16[3,1024,256]{2,1,0:T(8,128)(2,1)S(1)} %get-tuple-element.50.t_ref, bf16[1024,384]{1,0:T(8,128)(2,1)S(1)} %bitcast.11), custom_call_target="tpu_custom_call" | custom-call | flops 1000000 | bytes 1000 | tf_op jit(solution)/shard_map/pallas_call | solution.py:116
  66.1 1.7 %collective-permute-start.6 = (bf16[384,256]{1,0:T(8,128)(2,1)S(1)}, bf16[384,256]{1,0:T(8,128)(2,1)S(1)}, u32[]{:S(2)}, u32[]{:S(2)}) collective-permute-start(bf16[384,256]{1,0:T(8,128)(2,1)S(1)} %get-tuple-element.53), channel_id=1, source_target_pairs={{0,3},{1,2},{2,1},{3,0},{4,7},{5,6},{6,5},{7,4},{8,11},{9,10},{10,... | collective-permute-start | bytes 589832 | tf_op jit(solution)/shard_map/ppermute | solution.py:534
  67.8 3.3 %shard_map.171 = (bf16[16,256,256]{2,1,0:T(8,128)(2,1)S(1)}, f32[256,2]{1,0:T(8,128)S(1)}) custom-call(s32[1]{0:T(128)} %bitcast.me_ref.refs_0_.refs_10_, bf16[16,256,256]{2,1,0:T(8,128)(2,1)} %get-tuple-element.35.refs_2_.refs_0_.refs_1_.x_ref, bf16[16,256,256]{2,1,0:T(8,128)(2,1)} %get-tuple-element.48.refs_2_.pre_ref, bf16[192,96]{1,0:T(8,128)(2,1)} %w_ref.7, ...), custom_call_target="tpu_custom_call" | custom-call | flops 1000000 | bytes 1000 | tf_op jit(solution)/shard_map/pallas_call | solution.py:116
  71.1 1.5 %collective-permute-done.7.far_ref = bf16[384,256]{1,0:T(8,128)(2,1)S(1)} collective-permute-done((bf16[384,256]{1,0:T(8,128)(2,1)S(1)}, bf16[384,256]{1,0:T(8,128)(2,1)S(1)}, u32[]{:S(2)}, u32[]{:S(2)}) %collective-permute-start.7) | collective-permute-done | bytes 196640 | tf_op jit(solution)/shard_map/ppermute | solution.py:534
  72.5 1.7 %shard_map.172.given_ref = bf16[16,256,256]{2,1,0:T(8,128)(2,1)S(1)} custom-call(s32[1]{0:T(128)} %bitcast.me_ref.refs_0_.refs_10_, bf16[16,256,256]{2,1,0:T(8,128)(2,1)} %get-tuple-element.35.refs_2_.refs_0_.refs_1_.x_ref, bf16[16,256,256]{2,1,0:T(8,128)(2,1)} %get-tuple-element.48.refs_2_.pre_ref, ...), custom_call_target="tpu_custom_call", output_to_operand_aliasing={{}: (6, {})} | custom-call | flops 1000000 | bytes 1000 | tf_op jit(solution)/shard_map/pallas_call | solution.py:116
  74.3 2.7 %collective-permute-done.6.last_ref = bf16[384,256]{1,0:T(8,128)(2,1)S(1)} collective-permute-done((bf16[384,256]{1,0:T(8,128)(2,1)S(1)}, bf16[384,256]{1,0:T(8,128)(2,1)S(1)}, u32[]{:S(2)}, u32[]{:S(2)}) %collective-permute-start.6) | collective-permute-done | bytes 196640 | tf_op jit(solution)/shard_map/ppermute | solution.py:534
  76.9 1.9 %shard_map.173 = (bf16[16,256,256]{2,1,0:T(8,128)(2,1)S(1)}, bf16[256,16,256]{2,1,0:T(8,128)(2,1)}) custom-call(s32[1]{0:T(128)} %bitcast.me_ref.refs_0_.refs_10_, bf16[16,256,256]{2,1,0:T(8,128)(2,1)S(1)} %copy-done, bf16[16,256,256]{2,1,0:T(8,128)(2,1)S(1)} %copy-done.1, bf16[192,96]{1,0:T(8,128)(2,1)S(1)} %copy-done.3, ...), custom_call_target="tpu_custom_call", output_to_operand_aliasing={{0}: (6, {})} | custom-call | flops 1000000 | bytes 1000 | tf_op jit(solution)/shard_map/pallas_call | solution.py:116
  (21 shorter events, 1.2 us)
Async XLA Ops:
  0.0 4.3 %copy-start.4 = (bf16[96,192]{1,0:T(8,128)(2,1)S(1)}, bf16[96,192]{1,0:T(8,128)(2,1)}, u32[]{:S(2)}) copy-start(bf16[96,192]{1,0:T(8,128)(2,1)} %refs_5_.3) | copy-start | bytes 110596
  0.0 8.5 %copy-start.2 = (bf16[4,1024,256]{2,1,0:T(8,128)(2,1)S(1)}, bf16[4,1024,256]{2,1,0:T(8,128)(2,1)}, u32[]{:S(2)}) copy-start(bf16[4,1024,256]{2,1,0:T(8,128)(2,1)} %constant.21.clone.t_ref) | copy-start | bytes 6291460
  2.1 8.3 %copy-start.5 = (f32[96,2]{1,0:T(8,128)}, f32[96,2]{1,0:T(8,128)S(1)}, u32[]{:S(2)}) copy-start(f32[96,2]{1,0:T(8,128)S(1)} %get-tuple-element.32.affine_ref.refs_6_) | copy-start | bytes 2308
  2.1 6.4 %collective-permute-start = (bf16[384,256]{1,0:T(8,128)(2,1)S(1)}, bf16[384,256]{1,0:T(8,128)(2,1)S(1)}, u32[]{:S(2)}, u32[]{:S(2)}) collective-permute-start(bf16[384,256]{1,0:T(8,128)(2,1)S(1)} %get-tuple-element.34), channel_id=1, source_target_pairs={{0,2},{1,3},{2,0},{3,1},{4,6},{5,7},{6,4},{7,5},{8,10},{9,11},{10,... | collective-permute-start | bytes 589832 | tf_op jit(solution)/shard_map/ppermute | solution.py:534
  5.2 5.2 %collective-permute-start.1 = (bf16[416,256]{1,0:T(8,128)(2,1)S(1)}, bf16[416,256]{1,0:T(8,128)(2,1)S(1)}, u32[]{:S(2)}, u32[]{:S(2)}) collective-permute-start(bf16[416,256]{1,0:T(8,128)(2,1)S(1)} %get-tuple-element.37), channel_id=1, source_target_pairs={{0,1},{1,0},{2,3},{3,2},{4,5},{5,4},{6,7},{7,6},{8,9},{9,8},{10,11... | collective-permute-start | bytes 638984 | tf_op jit(solution)/shard_map/ppermute | solution.py:534
  6.2 7.9 %collective-permute-start.2 = (bf16[416,256]{1,0:T(8,128)(2,1)S(1)}, bf16[416,256]{1,0:T(8,128)(2,1)S(1)}, u32[]{:S(2)}, u32[]{:S(2)}) collective-permute-start(bf16[416,256]{1,0:T(8,128)(2,1)S(1)} %get-tuple-element.38), channel_id=1, source_target_pairs={{0,3},{1,2},{2,1},{3,0},{4,7},{5,6},{6,5},{7,4},{8,11},{9,10},{10,... | collective-permute-start | bytes 638984 | tf_op jit(solution)/shard_map/ppermute | solution.py:534
  15.5 25.2 %all-to-all-start = ((bf16[64,16,384]{2,1,0:T(8,128)(2,1)}), bf16[64,16,384]{2,1,0:T(8,128)(2,1)S(1)}, u32[]{:S(2)}, u32[]{:S(2)}) async-start(bf16[64,16,384]{2,1,0:T(8,128)(2,1)} %bitcast.13), calls=%async_computation | async-start | bytes 1572864 | tf_op jit(solution)/shard_map/all_to_all | solution.py:613
  27.2 0.6 copy-start.6
  27.8 17.4 %collective-permute-start.3 = (bf16[288,256]{1,0:T(8,128)(2,1)S(1)}, bf16[288,256]{1,0:T(8,128)(2,1)S(1)}, u32[]{:S(2)}, u32[]{:S(2)}) collective-permute-start(bf16[288,256]{1,0:T(8,128)(2,1)S(1)} %get-tuple-element.44), channel_id=1, source_target_pairs={{0,4},{4,8},{8,12},{12,16},{16,20},{20,24},{24,28},{28,32},{32,36}... | collective-permute-start | bytes 442376 | tf_op jit(solution)/shard_map/ppermute | solution.py:530
  31.1 14.1 %collective-permute-start.4 = (bf16[288,256]{1,0:T(8,128)(2,1)S(1)}, bf16[288,256]{1,0:T(8,128)(2,1)S(1)}, u32[]{:S(2)}, u32[]{:S(2)}) collective-permute-start(bf16[288,256]{1,0:T(8,128)(2,1)S(1)} %get-tuple-element.45), channel_id=1, source_target_pairs={{4,0},{8,4},{12,8},{16,12},{20,16},{24,20},{28,24},{32,28},{36,32}... | collective-permute-start | bytes 442376 | tf_op jit(solution)/shard_map/ppermute | solution.py:530
  45.2 19.5 %all-to-all-start.1 = ((bf16[64,16,384]{2,1,0:T(8,128)(2,1)}), bf16[64,16,384]{2,1,0:T(8,128)(2,1)S(1)}, u32[]{:S(2)}, u32[]{:S(2)}) async-start(bf16[64,16,384]{2,1,0:T(8,128)(2,1)} %shard_map.168), calls=%async_computation.1 | async-start | bytes 1572864 | tf_op jit(solution)/shard_map/all_to_all | solution.py:648
  65.6 2.2 %collective-permute-start.5 = (bf16[384,256]{1,0:T(8,128)(2,1)S(1)}, bf16[384,256]{1,0:T(8,128)(2,1)S(1)}, u32[]{:S(2)}, u32[]{:S(2)}) collective-permute-start(bf16[384,256]{1,0:T(8,128)(2,1)S(1)} %get-tuple-element.51), channel_id=1, source_target_pairs={{0,1},{1,0},{2,3},{3,2},{4,5},{5,4},{6,7},{7,6},{8,9},{9,8},{10,11... | collective-permute-start | bytes 589832 | tf_op jit(solution)/shard_map/ppermute | solution.py:534
  66.1 6.5 %collective-permute-start.7 = (bf16[384,256]{1,0:T(8,128)(2,1)S(1)}, bf16[384,256]{1,0:T(8,128)(2,1)S(1)}, u32[]{:S(2)}, u32[]{:S(2)}) collective-permute-start(bf16[384,256]{1,0:T(8,128)(2,1)S(1)} %get-tuple-element.54), channel_id=1, source_target_pairs={{0,2},{1,3},{2,0},{3,1},{4,6},{5,7},{6,4},{7,5},{8,10},{9,11},{10,... | collective-permute-start | bytes 589832 | tf_op jit(solution)/shard_map/ppermute | solution.py:534
  66.1 10.9 %collective-permute-start.6 = (bf16[384,256]{1,0:T(8,128)(2,1)S(1)}, bf16[384,256]{1,0:T(8,128)(2,1)S(1)}, u32[]{:S(2)}, u32[]{:S(2)}) collective-permute-start(bf16[384,256]{1,0:T(8,128)(2,1)S(1)} %get-tuple-element.53), channel_id=1, source_target_pairs={{0,3},{1,2},{2,1},{3,0},{4,7},{5,6},{6,5},{7,4},{8,11},{9,10},{10,... | collective-permute-start | bytes 589832 | tf_op jit(solution)/shard_map/ppermute | solution.py:534
  67.8 4.7 %copy-start.3 = (bf16[192,96]{1,0:T(8,128)(2,1)S(1)}, bf16[192,96]{1,0:T(8,128)(2,1)}, u32[]{:S(2)}) copy-start(bf16[192,96]{1,0:T(8,128)(2,1)} %w_ref.7) | copy-start | bytes 110596
  72.5 4.4 %copy-start = (bf16[16,256,256]{2,1,0:T(8,128)(2,1)S(1)}, bf16[16,256,256]{2,1,0:T(8,128)(2,1)}, u32[]{:S(2)}) copy-start(bf16[16,256,256]{2,1,0:T(8,128)(2,1)} %get-tuple-element.35.refs_2_.refs_0_.refs_1_.x_ref) | copy-start | bytes 6291460
  72.5 4.4 %copy-start.1 = (bf16[16,256,256]{2,1,0:T(8,128)(2,1)S(1)}, bf16[16,256,256]{2,1,0:T(8,128)(2,1)}, u32[]{:S(2)}) copy-start(bf16[16,256,256]{2,1,0:T(8,128)(2,1)} %get-tuple-element.48.refs_2_.pre_ref) | copy-start | bytes 6291460

commit v6 on v5

--- a/solution.py
+++ b/solution.py
@@ -23,7 +23,7 @@
 LANE = 128
 WIDE = HS * LANE
 MID = H // HS
-PARTS = 8
+PARTS = 4
 
 
 def bf(table):

time: 79.5 us -> 79.6 us (level)
  no operation moved by 1% of the time
where the time goes in v6:
time: 79.6 us; the launch traced here: 79.1 us
  Pallas kernels  28.8 us (36%)
  waiting for transfers between devices  25.3 us (32%)
  starting transfers between devices  24.1 us (30%)
    pallas_call x11, Pallas kernels, call(): pl.pallas_call(body, out_shape=shapes[0] if single else tuple(shapes), in...  28.8 us
    ppermute x6, waiting for transfers between devices, swap(): return lax.ppermute(block, 'col', [(i, i ^ s) for i in range(COLS)])  10 us
    all_to_all x1, starting transfers between devices, per_device(): lax.all_to_all(spectra.reshape(PEERS, 2 * NF, LANES), ('row', 'col'), spl...  9.63 us
    all_to_all x1, waiting for transfers between devices, per_device(): lax.all_to_all(spectra.reshape(PEERS, 2 * NF, LANES), ('row', 'col'), spl...  8.21 us
    all_to_all x1, waiting for transfers between devices, per_device(): lax.all_to_all(returned, ('row', 'col'), split_axis=0, concat_axis=0, til...  7.05 us
    ppermute x6, starting transfers between devices, swap(): return lax.ppermute(block, 'col', [(i, i ^ s) for i in range(COLS)])  5.47 us
    ppermute x2, starting transfers between devices, shift_along(): return lax.ppermute(block, axis, pairs)  4.58 us
    all_to_all x1, starting transfers between devices, per_device(): lax.all_to_all(returned, ('row', 'col'), split_axis=0, concat_axis=0, til...  4.4 us
  transfers between devices with their start and end apart: 10, of which 6 were waited for; matrix products, arithmetic and copies ran while one was open for 0% of the time, Pallas kernels for 28%

profile of v6, /device:TPU:1, one launch (start us, length us, event | category | flops | bytes accessed | tf_op | source)
XLA Modules:
  0.0 79.1 jit_solution(7619372523118868420)
XLA Ops:
  0.0 2.1 %shard_map.163 = (bf16[16,256,256]{2,1,0:T(8,128)(2,1)S(1)}, bf16[384,256]{1,0:T(8,128)(2,1)S(1)}, f32[96,2]{1,0:T(8,128)S(1)}) custom-call(s32[1]{0:T(128)} %bitcast.me_ref.refs_0_.refs_10_, bf16[256,16,256]{2,1,0:T(8,128)(2,1)} %image_ref.1, bf16[96,192]{1,0:T(8,128)(2,1)} %refs_5_.3, f32[1,96]{1,0:T(1,128)} %bitcast.19, f32[1,96]{1,0:T(1,128)} %bitcast.20), custom_call_target="tpu_custom_call" | custom-call | flops 1000000 | bytes 1000 | tf_op jit(solution)/shard_map/pallas_call | solution.py:116
  2.2 2.2 %collective-permute-start = (bf16[384,256]{1,0:T(8,128)(2,1)S(1)}, bf16[384,256]{1,0:T(8,128)(2,1)S(1)}, u32[]{:S(2)}, u32[]{:S(2)}) collective-permute-start(bf16[384,256]{1,0:T(8,128)(2,1)S(1)} %get-tuple-element.34), channel_id=1, source_target_pairs={{0,2},{1,3},{2,0},{3,1},{4,6},{5,7},{6,4},{7,5},{8,10},{9,11},{10,... | collective-permute-start | bytes 589832 | tf_op jit(solution)/shard_map/ppermute | solution.py:534
  4.4 0.9 %shard_map.164 = (bf16[384,256]{1,0:T(8,128)(2,1)S(1)}, bf16[416,256]{1,0:T(8,128)(2,1)S(1)}, bf16[416,256]{1,0:T(8,128)(2,1)S(1)}) custom-call(s32[1]{0:T(128)} %bitcast.me_ref.refs_0_.refs_10_, bf16[16,256,256]{2,1,0:T(8,128)(2,1)S(1)} %get-tuple-element.31.x_ref, bf16[96,192]{1,0:T(8,128)(2,1)S(1)} %copy-done.4, ...), custom_call_target="tpu_custom_call" | custom-call | flops 1000000 | bytes 1000 | tf_op jit(solution)/shard_map/pallas_call | solution.py:116
  5.2 1.0 %collective-permute-start.1 = (bf16[416,256]{1,0:T(8,128)(2,1)S(1)}, bf16[416,256]{1,0:T(8,128)(2,1)S(1)}, u32[]{:S(2)}, u32[]{:S(2)}) collective-permute-start(bf16[416,256]{1,0:T(8,128)(2,1)S(1)} %get-tuple-element.37), channel_id=1, source_target_pairs={{0,1},{1,0},{2,3},{3,2},{4,5},{5,4},{6,7},{7,6},{8,9},{9,8},{10,11... | collective-permute-start | bytes 638984 | tf_op jit(solution)/shard_map/ppermute | solution.py:534
  6.3 2.3 %collective-permute-done.far_ref = bf16[384,256]{1,0:T(8,128)(2,1)S(1)} collective-permute-done((bf16[384,256]{1,0:T(8,128)(2,1)S(1)}, bf16[384,256]{1,0:T(8,128)(2,1)S(1)}, u32[]{:S(2)}, u32[]{:S(2)}) %collective-permute-start) | collective-permute-done | bytes 196640 | tf_op jit(solution)/shard_map/ppermute | solution.py:534
  8.6 1.9 %shard_map.165 = (f32[1024,384]{1,0:T(8,128)S(1)}, bf16[16,256,256]{2,1,0:T(8,128)(2,1)}) custom-call(s32[1]{0:T(128)} %bitcast.me_ref.refs_0_.refs_10_, bf16[4,1024,256]{2,1,0:T(8,128)(2,1)S(1)} %copy-done.2, bf16[384,256]{1,0:T(8,128)(2,1)S(1)} %get-tuple-element.33.near_ref, bf16[384,256]{1,0:T(8,128)(2,1)S(1)} %collective-permute-done.far_ref, ...), custom_call_target="tpu_custom_call" | custom-call | flops 1000000000 | bytes 1000000 | tf_op jit(solution)/shard_map/pallas_call | solution.py:116
  10.5 3.6 %collective-permute-done.2.last_ref.refs_4_ = bf16[416,256]{1,0:T(8,128)(2,1)S(1)} collective-permute-done((bf16[416,256]{1,0:T(8,128)(2,1)S(1)}, bf16[416,256]{1,0:T(8,128)(2,1)S(1)}, u32[]{:S(2)}, u32[]{:S(2)}) %collective-permute-start.2) | collective-permute-done | bytes 213024 | tf_op jit(solution)/shard_map/ppermute | solution.py:534
  14.1 1.4 %shard_map.166 = bf16[1024,384]{1,0:T(8,128)(2,1)} custom-call(s32[1]{0:T(128)} %bitcast.me_ref.refs_0_.refs_10_, bf16[4,1024,256]{2,1,0:T(8,128)(2,1)S(1)} %copy-done.2, f32[1024,384]{1,0:T(8,128)S(1)} %get-tuple-element.36.part_ref, bf16[416,256]{1,0:T(8,128)(2,1)S(1)} %collective-permute-done.1.next_ref.refs_3_, ...), custom_call_target="tpu_custom_call" | custom-call | flops 1000000 | bytes 1000 | tf_op jit(solution)/shard_map/pallas_call | solution.py:116
  15.5 9.6 %all-to-all-start = ((bf16[64,16,384]{2,1,0:T(8,128)(2,1)}), bf16[64,16,384]{2,1,0:T(8,128)(2,1)S(1)}, u32[]{:S(2)}, u32[]{:S(2)}) async-start(bf16[64,16,384]{2,1,0:T(8,128)(2,1)} %bitcast.13), calls=%async_computation | async-start | bytes 1572864 | tf_op jit(solution)/shard_map/all_to_all | solution.py:613
  25.2 2.1 %shard_map.167 = (bf16[288,256]{1,0:T(8,128)(2,1)S(1)}, bf16[288,256]{1,0:T(8,128)(2,1)S(1)}, bf16[32,256]{1,0:T(8,128)(2,1)S(1)}, bf16[6,256,256]{2,1,0:T(8,128)(2,1)S(1)}) custom-call(s32[1]{0:T(128)} %bitcast.me_ref.refs_0_.refs_10_, s32[1]{0:T(128)} %bitcast.3.refs_1_, bf16[16,256,256]{2,1,0:T(8,128)(2,1)} %get-tuple-element.35.refs_2_.refs_0_.refs_1_.x_ref, ...), custom_call_target="tpu_custom_call" | custom-call | flops 1000000 | bytes 1000 | tf_op jit(solution)/shard_map/pallas_call | solution.py:116
  27.9 3.3 %collective-permute-start.3 = (bf16[288,256]{1,0:T(8,128)(2,1)S(1)}, bf16[288,256]{1,0:T(8,128)(2,1)S(1)}, u32[]{:S(2)}, u32[]{:S(2)}) collective-permute-start(bf16[288,256]{1,0:T(8,128)(2,1)S(1)} %get-tuple-element.44), channel_id=1, source_target_pairs={{0,4},{4,8},{8,12},{12,16},{16,20},{20,24},{24,28},{28,32},{32,36}... | collective-permute-start | bytes 442376 | tf_op jit(solution)/shard_map/ppermute | solution.py:530
  31.2 1.3 %collective-permute-start.4 = (bf16[288,256]{1,0:T(8,128)(2,1)S(1)}, bf16[288,256]{1,0:T(8,128)(2,1)S(1)}, u32[]{:S(2)}, u32[]{:S(2)}) collective-permute-start(bf16[288,256]{1,0:T(8,128)(2,1)S(1)} %get-tuple-element.45), channel_id=1, source_target_pairs={{4,0},{8,4},{12,8},{16,12},{20,16},{24,20},{28,24},{32,28},{36,32}... | collective-permute-start | bytes 442376 | tf_op jit(solution)/shard_map/ppermute | solution.py:530
  32.5 8.2 %all-to-all-done.d_ref = bf16[64,16,384]{2,1,0:T(8,128)(2,1)S(1)} async-done(((bf16[64,16,384]{2,1,0:T(8,128)(2,1)}), bf16[64,16,384]{2,1,0:T(8,128)(2,1)S(1)}, u32[]{:S(2)}, u32[]{:S(2)}) %all-to-all-start) | async-done | bytes 786464 | tf_op jit(solution)/shard_map/all_to_all | solution.py:613
  40.7 4.6 %shard_map.168 = bf16[64,16,384]{2,1,0:T(8,128)(2,1)} custom-call(bf16[64,16,384]{2,1,0:T(8,128)(2,1)S(1)} %all-to-all-done.d_ref, bf16[6,256,256]{2,1,0:T(8,128)(2,1)S(1)} %get-tuple-element.43.x_ref, f32[1,192]{1,0:T(1,128)} %bitcast.15, f32[1,192]{1,0:T(1,128)} %bitcast.16), custom_call_target="tpu_custom_call" | custom-call | flops 1000000 | bytes 1000 | tf_op jit(solution)/shard_map/pallas_call | solution.py:116
  45.3 4.4 %all-to-all-start.1 = ((bf16[64,16,384]{2,1,0:T(8,128)(2,1)}), bf16[64,16,384]{2,1,0:T(8,128)(2,1)S(1)}, u32[]{:S(2)}, u32[]{:S(2)}) async-start(bf16[64,16,384]{2,1,0:T(8,128)(2,1)} %shard_map.168), calls=%async_computation.1 | async-start | bytes 1572864 | tf_op jit(solution)/shard_map/all_to_all | solution.py:648
  49.7 8.1 %shard_map.169 = (bf16[16,256,256]{2,1,0:T(8,128)(2,1)}, bf16[3,1024,256]{2,1,0:T(8,128)(2,1)S(1)}) custom-call(bf16[16,256,256]{2,1,0:T(8,128)(2,1)} %get-tuple-element.35.refs_2_.refs_0_.refs_1_.x_ref, bf16[32,256]{1,0:T(8,128)(2,1)} %copy-done.6, bf16[9,64,256]{2,1,0:T(8,128)(2,1)} %bitcast.14, bf16[9,64,192]{2,1,0:T(8,128)(2,1)} %refs_3_.2, ...), custom_call_target="tpu_custom_call" | custom-call | flops 1000000000 | bytes 1000000 | tf_op jit(solution)/shard_map/pallas_call | solution.py:116
  57.8 7.1 %all-to-all-done.1 = bf16[64,16,384]{2,1,0:T(8,128)(2,1)S(1)} async-done(((bf16[64,16,384]{2,1,0:T(8,128)(2,1)}), bf16[64,16,384]{2,1,0:T(8,128)(2,1)S(1)}, u32[]{:S(2)}, u32[]{:S(2)}) %all-to-all-start.1) | async-done | bytes 786464 | tf_op jit(solution)/shard_map/all_to_all | solution.py:648
  64.8 0.8 %shard_map.170 = (bf16[384,256]{1,0:T(8,128)(2,1)S(1)}, bf16[384,256]{1,0:T(8,128)(2,1)S(1)}, bf16[384,256]{1,0:T(8,128)(2,1)S(1)}) custom-call(bf16[3,1024,256]{2,1,0:T(8,128)(2,1)S(1)} %get-tuple-element.50.t_ref, bf16[1024,384]{1,0:T(8,128)(2,1)S(1)} %bitcast.11), custom_call_target="tpu_custom_call" | custom-call | flops 1000000 | bytes 1000 | tf_op jit(solution)/shard_map/pallas_call | solution.py:116
  66.1 1.7 %collective-permute-start.6 = (bf16[384,256]{1,0:T(8,128)(2,1)S(1)}, bf16[384,256]{1,0:T(8,128)(2,1)S(1)}, u32[]{:S(2)}, u32[]{:S(2)}) collective-permute-start(bf16[384,256]{1,0:T(8,128)(2,1)S(1)} %get-tuple-element.53), channel_id=1, source_target_pairs={{0,3},{1,2},{2,1},{3,0},{4,7},{5,6},{6,5},{7,4},{8,11},{9,10},{10,... | collective-permute-start | bytes 589832 | tf_op jit(solution)/shard_map/ppermute | solution.py:534
  67.9 3.3 %shard_map.171 = (bf16[16,256,256]{2,1,0:T(8,128)(2,1)S(1)}, f32[256,2]{1,0:T(8,128)S(1)}) custom-call(s32[1]{0:T(128)} %bitcast.me_ref.refs_0_.refs_10_, bf16[16,256,256]{2,1,0:T(8,128)(2,1)} %get-tuple-element.35.refs_2_.refs_0_.refs_1_.x_ref, bf16[16,256,256]{2,1,0:T(8,128)(2,1)} %get-tuple-element.48.refs_2_.pre_ref, bf16[192,96]{1,0:T(8,128)(2,1)} %w_ref.7, ...), custom_call_target="tpu_custom_call" | custom-call | flops 1000000 | bytes 1000 | tf_op jit(solution)/shard_map/pallas_call | solution.py:116
  71.1 1.5 %collective-permute-done.7.far_ref = bf16[384,256]{1,0:T(8,128)(2,1)S(1)} collective-permute-done((bf16[384,256]{1,0:T(8,128)(2,1)S(1)}, bf16[384,256]{1,0:T(8,128)(2,1)S(1)}, u32[]{:S(2)}, u32[]{:S(2)}) %collective-permute-start.7) | collective-permute-done | bytes 196640 | tf_op jit(solution)/shard_map/ppermute | solution.py:534
  72.6 1.7 %shard_map.172.given_ref = bf16[16,256,256]{2,1,0:T(8,128)(2,1)S(1)} custom-call(s32[1]{0:T(128)} %bitcast.me_ref.refs_0_.refs_10_, bf16[16,256,256]{2,1,0:T(8,128)(2,1)} %get-tuple-element.35.refs_2_.refs_0_.refs_1_.x_ref, bf16[16,256,256]{2,1,0:T(8,128)(2,1)} %get-tuple-element.48.refs_2_.pre_ref, ...), custom_call_target="tpu_custom_call", output_to_operand_aliasing={{}: (6, {})} | custom-call | flops 1000000 | bytes 1000 | tf_op jit(solution)/shard_map/pallas_call | solution.py:116
  74.3 2.7 %collective-permute-done.6.last_ref = bf16[384,256]{1,0:T(8,128)(2,1)S(1)} collective-permute-done((bf16[384,256]{1,0:T(8,128)(2,1)S(1)}, bf16[384,256]{1,0:T(8,128)(2,1)S(1)}, u32[]{:S(2)}, u32[]{:S(2)}) %collective-permute-start.6) | collective-permute-done | bytes 196640 | tf_op jit(solution)/shard_map/ppermute | solution.py:534
  77.0 1.9 %shard_map.173 = (bf16[16,256,256]{2,1,0:T(8,128)(2,1)S(1)}, bf16[256,16,256]{2,1,0:T(8,128)(2,1)}) custom-call(s32[1]{0:T(128)} %bitcast.me_ref.refs_0_.refs_10_, bf16[16,256,256]{2,1,0:T(8,128)(2,1)S(1)} %copy-done, bf16[16,256,256]{2,1,0:T(8,128)(2,1)S(1)} %copy-done.1, bf16[192,96]{1,0:T(8,128)(2,1)S(1)} %copy-done.3, ...), custom_call_target="tpu_custom_call", output_to_operand_aliasing={{0}: (6, {})} | custom-call | flops 1000000 | bytes 1000 | tf_op jit(solution)/shard_map/pallas_call | solution.py:116
  (21 shorter events, 1.2 us)
Async XLA Ops:
  0.0 4.4 %copy-start.4 = (bf16[96,192]{1,0:T(8,128)(2,1)S(1)}, bf16[96,192]{1,0:T(8,128)(2,1)}, u32[]{:S(2)}) copy-start(bf16[96,192]{1,0:T(8,128)(2,1)} %refs_5_.3) | copy-start | bytes 110596
  0.0 8.6 %copy-start.2 = (bf16[4,1024,256]{2,1,0:T(8,128)(2,1)S(1)}, bf16[4,1024,256]{2,1,0:T(8,128)(2,1)}, u32[]{:S(2)}) copy-start(bf16[4,1024,256]{2,1,0:T(8,128)(2,1)} %constant.21.clone.t_ref) | copy-start | bytes 6291460
  2.1 8.3 %copy-start.5 = (f32[96,2]{1,0:T(8,128)}, f32[96,2]{1,0:T(8,128)S(1)}, u32[]{:S(2)}) copy-start(f32[96,2]{1,0:T(8,128)S(1)} %get-tuple-element.32.affine_ref.refs_6_) | copy-start | bytes 2308
  2.2 6.4 %collective-permute-start = (bf16[384,256]{1,0:T(8,128)(2,1)S(1)}, bf16[384,256]{1,0:T(8,128)(2,1)S(1)}, u32[]{:S(2)}, u32[]{:S(2)}) collective-permute-start(bf16[384,256]{1,0:T(8,128)(2,1)S(1)} %get-tuple-element.34), channel_id=1, source_target_pairs={{0,2},{1,3},{2,0},{3,1},{4,6},{5,7},{6,4},{7,5},{8,10},{9,11},{10,... | collective-permute-start | bytes 589832 | tf_op jit(solution)/shard_map/ppermute | solution.py:534
  5.2 5.2 %collective-permute-start.1 = (bf16[416,256]{1,0:T(8,128)(2,1)S(1)}, bf16[416,256]{1,0:T(8,128)(2,1)S(1)}, u32[]{:S(2)}, u32[]{:S(2)}) collective-permute-start(bf16[416,256]{1,0:T(8,128)(2,1)S(1)} %get-tuple-element.37), channel_id=1, source_target_pairs={{0,1},{1,0},{2,3},{3,2},{4,5},{5,4},{6,7},{7,6},{8,9},{9,8},{10,11... | collective-permute-start | bytes 638984 | tf_op jit(solution)/shard_map/ppermute | solution.py:534
  6.2 7.9 %collective-permute-start.2 = (bf16[416,256]{1,0:T(8,128)(2,1)S(1)}, bf16[416,256]{1,0:T(8,128)(2,1)S(1)}, u32[]{:S(2)}, u32[]{:S(2)}) collective-permute-start(bf16[416,256]{1,0:T(8,128)(2,1)S(1)} %get-tuple-element.38), channel_id=1, source_target_pairs={{0,3},{1,2},{2,1},{3,0},{4,7},{5,6},{6,5},{7,4},{8,11},{9,10},{10,... | collective-permute-start | bytes 638984 | tf_op jit(solution)/shard_map/ppermute | solution.py:534
  15.5 25.2 %all-to-all-start = ((bf16[64,16,384]{2,1,0:T(8,128)(2,1)}), bf16[64,16,384]{2,1,0:T(8,128)(2,1)S(1)}, u32[]{:S(2)}, u32[]{:S(2)}) async-start(bf16[64,16,384]{2,1,0:T(8,128)(2,1)} %bitcast.13), calls=%async_computation | async-start | bytes 1572864 | tf_op jit(solution)/shard_map/all_to_all | solution.py:613
  27.3 0.6 copy-start.6
  27.9 17.4 %collective-permute-start.3 = (bf16[288,256]{1,0:T(8,128)(2,1)S(1)}, bf16[288,256]{1,0:T(8,128)(2,1)S(1)}, u32[]{:S(2)}, u32[]{:S(2)}) collective-permute-start(bf16[288,256]{1,0:T(8,128)(2,1)S(1)} %get-tuple-element.44), channel_id=1, source_target_pairs={{0,4},{4,8},{8,12},{12,16},{16,20},{20,24},{24,28},{28,32},{32,36}... | collective-permute-start | bytes 442376 | tf_op jit(solution)/shard_map/ppermute | solution.py:530
  31.2 14.1 %collective-permute-start.4 = (bf16[288,256]{1,0:T(8,128)(2,1)S(1)}, bf16[288,256]{1,0:T(8,128)(2,1)S(1)}, u32[]{:S(2)}, u32[]{:S(2)}) collective-permute-start(bf16[288,256]{1,0:T(8,128)(2,1)S(1)} %get-tuple-element.45), channel_id=1, source_target_pairs={{4,0},{8,4},{12,8},{16,12},{20,16},{24,20},{28,24},{32,28},{36,32}... | collective-permute-start | bytes 442376 | tf_op jit(solution)/shard_map/ppermute | solution.py:530
  45.3 19.5 %all-to-all-start.1 = ((bf16[64,16,384]{2,1,0:T(8,128)(2,1)}), bf16[64,16,384]{2,1,0:T(8,128)(2,1)S(1)}, u32[]{:S(2)}, u32[]{:S(2)}) async-start(bf16[64,16,384]{2,1,0:T(8,128)(2,1)} %shard_map.168), calls=%async_computation.1 | async-start | bytes 1572864 | tf_op jit(solution)/shard_map/all_to_all | solution.py:648
  65.6 2.2 %collective-permute-start.5 = (bf16[384,256]{1,0:T(8,128)(2,1)S(1)}, bf16[384,256]{1,0:T(8,128)(2,1)S(1)}, u32[]{:S(2)}, u32[]{:S(2)}) collective-permute-start(bf16[384,256]{1,0:T(8,128)(2,1)S(1)} %get-tuple-element.51), channel_id=1, source_target_pairs={{0,1},{1,0},{2,3},{3,2},{4,5},{5,4},{6,7},{7,6},{8,9},{9,8},{10,11... | collective-permute-start | bytes 589832 | tf_op jit(solution)/shard_map/ppermute | solution.py:534
  66.1 6.5 %collective-permute-start.7 = (bf16[384,256]{1,0:T(8,128)(2,1)S(1)}, bf16[384,256]{1,0:T(8,128)(2,1)S(1)}, u32[]{:S(2)}, u32[]{:S(2)}) collective-permute-start(bf16[384,256]{1,0:T(8,128)(2,1)S(1)} %get-tuple-element.54), channel_id=1, source_target_pairs={{0,2},{1,3},{2,0},{3,1},{4,6},{5,7},{6,4},{7,5},{8,10},{9,11},{10,... | collective-permute-start | bytes 589832 | tf_op jit(solution)/shard_map/ppermute | solution.py:534
  66.1 10.9 %collective-permute-start.6 = (bf16[384,256]{1,0:T(8,128)(2,1)S(1)}, bf16[384,256]{1,0:T(8,128)(2,1)S(1)}, u32[]{:S(2)}, u32[]{:S(2)}) collective-permute-start(bf16[384,256]{1,0:T(8,128)(2,1)S(1)} %get-tuple-element.53), channel_id=1, source_target_pairs={{0,3},{1,2},{2,1},{3,0},{4,7},{5,6},{6,5},{7,4},{8,11},{9,10},{10,... | collective-permute-start | bytes 589832 | tf_op jit(solution)/shard_map/ppermute | solution.py:534
  67.9 4.7 %copy-start.3 = (bf16[192,96]{1,0:T(8,128)(2,1)S(1)}, bf16[192,96]{1,0:T(8,128)(2,1)}, u32[]{:S(2)}) copy-start(bf16[192,96]{1,0:T(8,128)(2,1)} %w_ref.7) | copy-start | bytes 110596
  72.6 4.4 %copy-start = (bf16[16,256,256]{2,1,0:T(8,128)(2,1)S(1)}, bf16[16,256,256]{2,1,0:T(8,128)(2,1)}, u32[]{:S(2)}) copy-start(bf16[16,256,256]{2,1,0:T(8,128)(2,1)} %get-tuple-element.35.refs_2_.refs_0_.refs_1_.x_ref) | copy-start | bytes 6291460
  72.6 4.4 %copy-start.1 = (bf16[16,256,256]{2,1,0:T(8,128)(2,1)S(1)}, bf16[16,256,256]{2,1,0:T(8,128)(2,1)}, u32[]{:S(2)}) copy-start(bf16[16,256,256]{2,1,0:T(8,128)(2,1)} %get-tuple-element.48.refs_2_.pre_ref) | copy-start | bytes 6291460
